TPU v7x, 128 devices: a whole 4x4x4 slice. The times are simulated.
128 devices in a mesh: seq: 8 (over y, core), enc: 16 (over z, x).
Axes of the slice: x: 4, y: 4, z: 4, core: 2. Of those that a mesh axis runs over, the one named last changes fastest.
Arguments:
- hidden: bfloat16 [2048, 8192], P('seq', 'enc'), may hold values from -56 to 56
- query_weight: bfloat16 [8192, 8192], P(None, 'enc'), may hold values from -0.0625 to 0.0625
- key_weight: bfloat16 [2048, 8192], P(None, 'enc'), may hold values from -0.125 to 0.125
- value_weight: bfloat16 [2048, 8192], P(None, 'enc'), may hold values from -0.125 to 0.125
- output_weight: bfloat16 [8192, 8192], P('enc'), may hold values from -0.0625 to 0.0625
- neighbour_states: bfloat16 [128, 128, 2048], P('enc', None, 'seq'), may hold values from -6 to 6
- neighbour_slot: int32 [32, 2], P('seq'), may hold values from 0 to 127, as said below
- d_output: bfloat16 [2048, 8192], P('seq', 'enc'), may hold values from -6 to 6
Outputs:
- output: bfloat16 [2048, 8192], P('seq', 'enc')
- d_hidden: bfloat16 [2048, 8192], P('seq', 'enc')
- d_states: bfloat16 [128, 128, 2048], P('enc', None, 'seq')
Inputs may be any that keep to these rules, and one draw needn't show every extreme that they name: `neighbour_slot`: each entry is e * 8 + s + b, where e is the encoder shard that holds the neighbour, s the seq index holding the span that reads it, and b below 1; no two entries are equal; in every draw some bucket of 1 slots is full.
All inputs are finite; a program needn't handle non-finite values.
Results may differ from a plain program's by a relative error of at most 0.02.
Values may be sent and summed in bfloat16 or wider, within the bound.
No kernel may reach another device: no remote copies, remote signals or barrier semaphores. Data moves between devices by JAX's collectives and lax.ppermute only.
A program may use at most 128 MiB of HBM per device.

v0:
```python
import jax
import jax.numpy as jnp
from jax import lax
from jax.sharding import PartitionSpec as P

HEAD = 128
SPAN = 64


def on_device(
    hidden,
    query_weight,
    key_weight,
    value_weight,
    output_weight,
    neighbour_states,
    neighbour_slot,
    d_output,
):
    seq_count = lax.axis_size("seq")
    enc_count = lax.axis_size("enc")
    token_rows = hidden.shape[0]
    head_cols = query_weight.shape[1]
    local_heads = head_cols // HEAD
    span_count = token_rows // SPAN
    bucket_size = neighbour_states.shape[0] // seq_count
    neigh_rows = neighbour_states.shape[1]
    score_scale = HEAD ** (-0.5)
    both_weight = jnp.concatenate([key_weight, value_weight], axis=1)
    queries = jnp.dot(
        lax.all_gather(hidden, "enc", axis=1, tiled=True),
        query_weight,
        preferred_element_type=jnp.float32,
    ).astype(jnp.bfloat16)
    pooled = lax.all_gather(neighbour_states, "enc", axis=0, tiled=True)
    pooled = pooled.reshape(enc_count, seq_count, bucket_size, neigh_rows, -1)
    pooled = pooled.transpose(1, 0, 2, 3, 4).reshape(
        seq_count * enc_count * bucket_size, neigh_rows, -1
    )
    arrived = lax.all_to_all(pooled, "seq", split_axis=0, concat_axis=2, tiled=True)
    flattened = arrived.reshape(-1, arrived.shape[2])
    product = jnp.dot(flattened, both_weight, preferred_element_type=jnp.float32)
    projected = product.astype(jnp.bfloat16).reshape(
        arrived.shape[0], arrived.shape[1], 2 * head_cols
    )
    shard_index = neighbour_slot // (seq_count * bucket_size)
    flat_slot = (shard_index * bucket_size + neighbour_slot % bucket_size).reshape(-1)
    picked = jnp.take(projected, flat_slot, axis=0).reshape(span_count, -1, 2 * head_cols)
    key_four = picked[:, :, :head_cols].reshape(span_count, -1, local_heads, HEAD)
    value_four = picked[:, :, head_cols:].reshape(span_count, -1, local_heads, HEAD)
    query_four = queries.reshape(span_count, SPAN, local_heads, HEAD)
    scores = (
        jnp.einsum("cqhd,ckhd->chqk", query_four, key_four, preferred_element_type=jnp.float32)
        * score_scale
    )
    exponent = jnp.exp(scores - jnp.max(scores, axis=-1, keepdims=True))
    attention = exponent / jnp.sum(exponent, axis=-1, keepdims=True)
    attention_low = attention.astype(jnp.bfloat16)
    context = jnp.einsum(
        "chqk,ckhd->cqhd", attention_low, value_four, preferred_element_type=jnp.float32
    )
    context = context.astype(jnp.bfloat16).reshape(token_rows, head_cols)
    head_terms = jnp.dot(context, output_weight, preferred_element_type=jnp.float32)
    output = lax.psum_scatter(
        head_terms.astype(jnp.bfloat16), "enc", scatter_dimension=1, tiled=True
    )
    d_context = lax.dot_general(
        lax.all_gather(d_output, "enc", axis=1, tiled=True),
        output_weight,
        (((1,), (1,)), ((), ())),
        preferred_element_type=jnp.float32,
    ).astype(jnp.bfloat16)
    d_four = d_context.reshape(span_count, SPAN, local_heads, HEAD)
    d_attention = jnp.einsum(
        "cqhd,ckhd->chqk", d_four, value_four, preferred_element_type=jnp.float32
    )
    inner_sum = jnp.sum(attention * d_attention, axis=-1, keepdims=True)
    d_scores = (attention * (d_attention - inner_sum) * score_scale).astype(jnp.bfloat16)
    d_queries = jnp.einsum(
        "chqk,ckhd->cqhd", d_scores, key_four, preferred_element_type=jnp.float32
    )
    d_queries = d_queries.astype(jnp.bfloat16).reshape(token_rows, head_cols)
    d_keys = jnp.einsum(
        "chqk,cqhd->ckhd", d_scores, query_four, preferred_element_type=jnp.float32
    ).astype(jnp.bfloat16)
    d_values = jnp.einsum(
        "chqk,cqhd->ckhd", attention_low, d_four, preferred_element_type=jnp.float32
    ).astype(jnp.bfloat16)
    input_terms = lax.dot_general(
        d_queries, query_weight, (((1,), (1,)), ((), ())), preferred_element_type=jnp.float32
    )
    d_hidden = lax.psum_scatter(
        input_terms.astype(jnp.bfloat16), "enc", scatter_dimension=1, tiled=True
    )
    used_count = flat_slot.shape[0]
    pair_grads = jnp.concatenate(
        [
            d_keys.reshape(used_count, neigh_rows, head_cols),
            d_values.reshape(used_count, neigh_rows, head_cols),
        ],
        axis=2,
    )
    slot_count = enc_count * bucket_size
    placing = (
        lax.broadcasted_iota(jnp.int32, (slot_count, used_count), 0) == flat_slot[None, :]
    ).astype(jnp.bfloat16)
    slot_grads = jnp.dot(
        placing, pair_grads.reshape(used_count, -1), preferred_element_type=jnp.float32
    )
    slot_grads = slot_grads.astype(jnp.bfloat16).reshape(slot_count, neigh_rows, 2 * head_cols)
    product = lax.dot_general(
        slot_grads.reshape(-1, 2 * head_cols),
        both_weight,
        (((1,), (1,)), ((), ())),
        preferred_element_type=jnp.float32,
    )
    summed = lax.psum_scatter(
        product.reshape(lax.axis_size("enc") * bucket_size, neigh_rows, -1).astype(jnp.bfloat16),
        "enc",
        scatter_dimension=0,
        tiled=True,
    )
    d_states = lax.all_to_all(summed, "seq", split_axis=2, concat_axis=0, tiled=True)
    return (output, d_hidden, d_states)


def solution(mesh):
    in_specs = (
        P("seq", "enc"),
        P(None, "enc"),
        P(None, "enc"),
        P(None, "enc"),
        P("enc", None),
        P("enc", None, "seq"),
        P("seq", None),
        P("seq", "enc"),
    )
    out_specs = (P("seq", "enc"), P("seq", "enc"), P("enc", None, "seq"))
    return jax.shard_map(
        on_device, mesh=mesh, in_specs=in_specs, out_specs=out_specs, check_vma=False
    )
```

profile of v0, /device:TPU:1, one launch (start us, length us, event | category | flops | bytes accessed | tf_op | source)
XLA Modules:
  0.0 555.5 jit_solution(3698630960442013874)
XLA Ops:
  7.2 0.0 all-gather.4.cloned.1.call-start
  7.2 0.7 all-gather.4.cloned.1.call-update
  7.9 0.0 all-gather.6.cloned.1.call-start
  7.9 0.7 all-gather.6.cloned.1.call-update
  8.6 0.0 all-gather.8.cloned.1.call-start
  8.7 0.7 all-gather.8.cloned.1.call-update
  9.4 74.9 %all-gather.4.cloned.1.call-done = bf16[128,128,256]{2,1,0:T(8,128)(2,1)} async-done(((bf16[8,128,256]{2,1,0:T(8,128)(2,1)}), bf16[128,128,256]{2,1,0:T(8,128)(2,1)}) %all-gather.4.cloned.1.call-update) | async-done | bytes 8388624 | tf_op jit(solution)/shard_map/all_gather | solution.py:35
  84.2 7.7 %copy.76 = bf16[8,16,1,128,256]{4,3,1,0,2:T(8,128)(2,1)} copy(bf16[8,16,1,128,256]{4,3,0,1,2:T(8,128)(2,1)} %bitcast.75) | data formatting | bytes 16777216 | tf_op jit(solution)/shard_map/transpose | solution.py:37
  92.0 5.7 %all-to-all-start = ((bf16[128,128,256]{2,1,0:T(8,128)(2,1)}), bf16[128,128,256]{2,1,0:T(8,128)(2,1)}, u32[]{:S(2)}, u32[]{:S(2)}) async-start(bf16[128,128,256]{2,1,0:T(8,128)(2,1)} %bitcast.70), calls=%async_computation | async-start | bytes 16777216 | tf_op jit(solution)/shard_map/all_to_all | solution.py:40
  97.6 0.1 copy.78
  97.7 0.1 reshape.108
  97.8 0.1 reshape.101
  97.9 0.1 broadcast_bitcast_fusion
  98.0 1.5 constant_dynamic-update-slice_fusion.1
  99.5 0.7 copy-done.3
  100.3 1.5 constant_dynamic-update-slice_fusion
  101.7 41.0 %all-gather.6.cloned.1.call-done = bf16[256,8192]{1,0:T(8,128)(2,1)} async-done(((bf16[256,512]{1,0:T(8,128)(2,1)}), bf16[256,8192]{1,0:T(8,128)(2,1)}) %all-gather.6.cloned.1.call-update) | async-done | bytes 4194320 | tf_op jit(solution)/shard_map/all_gather | solution.py:31
  142.8 7.0 %convolution_convert_fusion.9 = bf16[256,512]{1,0:T(8,128)(2,1)S(1)} fusion(bf16[256,8192]{1,0:T(8,128)(2,1)} %all-gather.6.cloned.1.call-done, bf16[8192,512]{1,0:T(8,128)(2,1)} %param.9), kind=kOutput, calls=%fused_computation.25 | convolution fusion | flops 2147614720 | bytes 12845056 | tf_op jit(solution)/shard_map/dot_general | solution.py:30
  149.8 0.1 reshape.103
  149.8 52.1 %all-gather.8.cloned.1.call-done = bf16[256,8192]{1,0:T(8,128)(2,1)} async-done(((bf16[256,512]{1,0:T(8,128)(2,1)}), bf16[256,8192]{1,0:T(8,128)(2,1)}) %all-gather.8.cloned.1.call-update) | async-done | bytes 4194320 | tf_op jit(solution)/shard_map/all_gather | solution.py:68
  201.9 7.0 %convolution_convert_fusion.8 = bf16[256,512]{1,0:T(8,128)(2,1)S(1)} fusion(bf16[256,8192]{1,0:T(8,128)(2,1)} %all-gather.8.cloned.1.call-done, bf16[512,8192]{1,0:T(8,128)(2,1)} %param.12), kind=kOutput, calls=%fused_computation.24 | convolution fusion | flops 2147614720 | bytes 12845056 | tf_op jit(solution)/shard_map/dot_general | solution.py:67
  208.9 0.8 reshape.106
  209.7 12.3 %copy.77 = bf16[8,16,128,256]{3,0,2,1:T(8,128)(2,1)} copy(bf16[8,16,128,256]{3,2,1,0:T(8,128)(2,1)} %bitcast.4) | data formatting | bytes 16777216 | tf_op jit(solution)/shard_map/all_to_all | solution.py:40
  222.0 10.6 %copy.102 = bf16[256,8,8,256]{3,1,2,0:T(8,128)(2,1)} copy(bf16[256,8,8,256]{3,2,1,0:T(8,128)(2,1)} %bitcast.71) | data formatting | bytes 16777216
  232.6 13.9 %convert_bitcast_fusion = bf16[2048,1024]{0,1:T(8,128)(2,1)} fusion(bf16[2048,1024]{1,0:T(8,128)(2,1)} %constant_dynamic-update-slice_fusion, bf16[2048,2048]{1,0:T(8,128)(2,1)} %bitcast.76), kind=kOutput, calls=%fused_computation.8 | convolution fusion | flops 8592031744 | bytes 16777216 | tf_op jit(solution)/shard_map/dot_general | solution.py:42
  246.6 6.4 %copy.100 = bf16[2048,1024]{1,0:T(8,128)(2,1)} copy(bf16[2048,1024]{0,1:T(8,128)(2,1)} %convert_bitcast_fusion) | data formatting | bytes 8388608 | tf_op jit(solution)/shard_map/reshape | solution.py:43
  253.0 4.2 gather_fusion
  257.2 2.8 copy.80
  260.0 0.2 broadcast_select_fusion
  260.2 0.1 fusion.36
  260.4 0.3 convolution_multiply_fusion
  260.7 1.3 fusion.37
  262.0 1.3 fusion.26
  263.2 4.0 fusion.5
  267.2 9.0 %fusion.4 = bf16[4,256,4,128]{1,3,2,0:T(8,128)(2,1)} fusion(f32[4,4,64,256]{3,2,1,0:T(8,128)} %fusion.26, bf16[4,64,4,128]{3,2,1,0:T(4,128)(2,1)S(1)} %reshape.103, f32[4,4,64,256]{3,2,1,0:T(8,128)} %get-tuple-element.11, f32[4,4,64]{2,1,0:T(4,128)S(1)} %get-tuple-element.10), kind=kOutput, calls=%fused_computation.14 | convolution fusion | flops 69469440 | bytes 3411968 | tf_op jit(solution)/shard_map/chqk,cqhd->ckhd/dot_general | solution.py:83
  276.2 1.6 copy.91
  277.9 1.2 reshape.109
  279.1 1.6 copy.93
  280.7 1.4 reshape.110
  282.1 1.8 maximum_bitcast_fusion
  283.9 1.2 copy.105
  285.0 1.2 convolution_convert_fusion
  286.3 2.3 copy.106
  288.6 13.3 %convolution_convert_fusion.3 = bf16[16,128,2048]{2,1,0:T(8,128)(2,1)} fusion(bf16[16,128,1024]{2,1,0:T(8,128)(2,1)S(1)} %bitcast.79, bf16[2048,1024]{1,0:T(8,128)(2,1)} %constant_dynamic-update-slice_fusion), kind=kOutput, calls=%fused_computation.6 | convolution fusion | flops 8594128896 | bytes 16777216 | tf_op jit(solution)/shard_map/dot_general | solution.py:111
  301.9 0.0 reduce-scatter.6.cloned.1.call-start
  301.9 1.1 copy-done.1
  303.1 1.8 fusion.11
  304.9 0.2 copy.84
  305.2 7.7 %convolution_convert_fusion.2 = bf16[256,8192]{1,0:T(8,128)(2,1)} fusion(bf16[512,8192]{1,0:T(8,128)(2,1)} %param.12, bf16[32,8,4,128]{3,2,1,0:T(4,128)(2,1)S(1)} %bitcast.87), kind=kOutput, calls=%fused_computation.5 | convolution fusion | flops 2149580800 | bytes 12845056 | tf_op jit(solution)/shard_map/dot_general | solution.py:63
  312.9 0.3 reduce-scatter.8.cloned.1.call-start
  313.2 7.7 %fusion.12 = bf16[4,64,4,128]{3,1,2,0:T(8,128)(2,1)S(1)} fusion(bf16[4,256,4,128]{1,3,2,0:T(8,128)(2,1)S(1)} %bitcast.82, f32[4,4,64,256]{3,2,1,0:T(8,128)} %fusion.26, f32[4,4,64,256]{3,2,1,0:T(8,128)} %get-tuple-element.11, f32[4,4,64]{2,1,0:T(4,128)S(1)} %get-tuple-element.10), kind=kOutput, calls=%fused_computation.27 | convolution fusion | flops 69076224 | bytes 3411968 | tf_op jit(solution)/shard_map/chqk,ckhd->cqhd/dot_general | solution.py:79
  320.9 0.2 copy.88
  321.1 8.0 %convolution_convert_fusion.1 = bf16[256,8192]{1,0:T(8,128)(2,1)} fusion(bf16[8192,512]{1,0:T(8,128)(2,1)} %param.9, bf16[32,8,4,128]{3,2,1,0:T(4,128)(2,1)S(1)} %bitcast.86), kind=kOutput, calls=%fused_computation.4 | convolution fusion | flops 2149580800 | bytes 12845056 | tf_op jit(solution)/shard_map/dot_general | solution.py:89
  329.1 57.5 %reduce-scatter.10.cloned.1.call-done = bf16[1,128,2048]{2,1,0:T(8,128)(2,1)} async-done(((bf16[16,128,2048]{2,1,0:T(8,128)(2,1)}), bf16[1,128,2048]{2,1,0:T(8,128)(2,1)}) %reduce-scatter.10.cloned.1.call-update) | async-done | bytes 524304
  386.5 2.3 copy.94
  388.9 0.5 broadcast.82
  389.4 11.5 %reduce = bf16[2048,128]{1,0:T(8,128)(2,1)S(1)} reduce(bf16[2048,1,128]{2,1,0:T(2,128)(2,1)S(1)} %bitcast.80, bf16[]{:T(256)} %broadcast.82), dimensions={1}, to_apply=%bitcast.51.reduce_sub_computation | reduce | bytes 1048578
  400.9 0.1 reshape.122
  401.1 15.4 %all_to_all.33 = bf16[8,2,16384]{2,1,0:T(2,128)(2,1)S(1)} all-to-all(bf16[8,2,16384]{2,1,0:T(2,128)(2,1)S(1)} %reshape.122), channel_id=1, replica_groups=mesh['seq'=8,'enc'=16] {'seq'}, dimensions={0} | all-to-all | bytes 1048576 | tf_op jit(solution)/shard_map/all_to_all | solution.py:123
  416.5 0.5 reshape.123
  417.0 0.1 copy.101
  417.1 1.0 copy.95
  418.1 49.1 %reduce-scatter.6.cloned.1.call-done = bf16[256,512]{1,0:T(8,128)(2,1)} async-done(((bf16[256,8192]{1,0:T(8,128)(2,1)}), bf16[256,512]{1,0:T(8,128)(2,1)}) %reduce-scatter.6.cloned.1.call-update) | async-done | bytes 262160 | tf_op jit(solution)/shard_map/reduce_scatter | solution.py:64
  467.2 81.2 %reduce-scatter.8.cloned.1.call-done = bf16[256,512]{1,0:T(8,128)(2,1)} async-done(((bf16[256,8192]{1,0:T(8,128)(2,1)}), bf16[256,512]{1,0:T(8,128)(2,1)}) %reduce-scatter.8.cloned.1.call-update) | async-done | bytes 262160 | tf_op jit(solution)/shard_map/reduce_scatter | solution.py:92
  (18 shorter events, 0.1 us)
Async XLA Ops:
  7.2 77.1 %all-gather.4.cloned.1.call-start = ((), (), s32[]{:S(2)}) async-start(), calls=%async_computation.5 | async-start | bytes 8912896 | tf_op jit(solution)/shard_map/all_gather | solution.py:35
  7.9 134.9 %all-gather.6.cloned.1.call-start = ((), (), s32[]{:S(2)}) async-start(), calls=%async_computation.6 | async-start | bytes 4456448 | tf_op jit(solution)/shard_map/all_gather | solution.py:31
  8.6 193.3 %all-gather.8.cloned.1.call-start = ((), (), s32[]{:S(2)}) async-start(), calls=%async_computation.8 | async-start | bytes 4456448 | tf_op jit(solution)/shard_map/all_gather | solution.py:68
  91.9 5.7 %copy-start.5 = (s32[4,2]{0,1:T(2,128)S(1)}, s32[4,2]{0,1:T(2,128)}, u32[]{:S(2)}) copy-start(s32[4,2]{0,1:T(2,128)} %param.14) | copy-start | bytes 100
  91.9 6.0 %copy-start.2 = (bf16[2048,512]{1,0:T(8,128)(2,1)S(1)}, bf16[2048,512]{1,0:T(8,128)(2,1)}, u32[]{:S(2)}) copy-start(bf16[2048,512]{1,0:T(8,128)(2,1)} %param.10) | copy-start | bytes 6291460
  92.0 117.8 %all-to-all-start = ((bf16[128,128,256]{2,1,0:T(8,128)(2,1)}), bf16[128,128,256]{2,1,0:T(8,128)(2,1)}, u32[]{:S(2)}, u32[]{:S(2)}) async-start(bf16[128,128,256]{2,1,0:T(8,128)(2,1)} %bitcast.70), calls=%async_computation | async-start | bytes 16777216 | tf_op jit(solution)/shard_map/all_to_all | solution.py:40
  97.6 288.9 %reduce-scatter.10.cloned.1.call-start = ((), (), s32[]{:S(2)}) async-start(), calls=%async_computation.10 | async-start | bytes 8912896
  97.9 2.4 copy-start.3
  260.2 1.8 copy-start.4
  260.4 6.9 %copy-start = (bf16[4,256,512]{1,2,0:T(8,128)(2,1)}, bf16[4,256,512]{1,2,0:T(8,128)(2,1)S(1)}, u32[]{:S(2)}) copy-start(bf16[4,256,512]{1,2,0:T(8,128)(2,1)S(1)} %get-tuple-element.9) | copy-start | bytes 3145732
  301.9 1.2 copy-start.1
  301.9 165.3 %reduce-scatter.6.cloned.1.call-start = ((), (), s32[]{:S(2)}) async-start(), calls=%async_computation.7 | async-start | bytes 4456448 | tf_op jit(solution)/shard_map/reduce_scatter | solution.py:64
  312.9 235.5 %reduce-scatter.8.cloned.1.call-start = ((), (), s32[]{:S(2)}) async-start(), calls=%async_computation.9 | async-start | bytes 4456448 | tf_op jit(solution)/shard_map/reduce_scatter | solution.py:92
Sparse Core Ops, SparseCore 0:
  10.1 74.0 all-gather.3
  86.4 56.3 all-gather.5
  144.9 56.9 all-gather.7
  302.0 84.4 reduce-scatter.9
  390.3 76.8 reduce-scatter.5
  471.4 77.0 reduce-scatter.7
where the time goes:
time: 566 us; the launch traced here: 556 us
  waiting for transfers between devices  358 us (63%)
  matrix products  82.1 us (15%)
  local copies, waits for them, and re-layouts  64.7 us (11%)
  blocking collectives  15.4 us (3%)
  other arithmetic  14.8 us (3%)
  between operations  14.5 us (3%)
  starting transfers between devices  6.07 us (1%)
    reduce_scatter x1, waiting for transfers between devices, on_device(): lax.psum_scatter(input_terms.astype(jnp.bfloat16), 'enc', scatter_dimensi...  81.2 us
    all_gather x1, waiting for transfers between devices, on_device(): pooled = lax.all_gather(neighbour_states, 'enc', axis=0, tiled=True)  74.9 us
    unnamed x7, waiting for transfers between devices  59.6 us
    all_gather x1, waiting for transfers between devices, on_device(): lax.all_gather(d_output, 'enc', axis=1, tiled=True)  52.1 us
    reduce_scatter x1, waiting for transfers between devices, on_device(): lax.psum_scatter(head_terms.astype(jnp.bfloat16), 'enc', scatter_dimensio...  49.1 us
    all_gather x1, waiting for transfers between devices, on_device(): lax.all_gather(hidden, 'enc', axis=1, tiled=True)  41 us
    unnamed x21, local copies, waits for them, and re-layouts  19.8 us
    all_to_all x1, blocking collectives, on_device(): lax.all_to_all(summed, 'seq', split_axis=2, concat_axis=0, tiled=True)  15.4 us
  transfers between devices with their start and end apart: 7, of which 6 were waited for; matrix products, arithmetic and copies ran while one was open for 12% of the time, Pallas kernels for 0%

commit v1 on v0

v1 whole, which is shorter than its diff:
```python
import functools

import jax
import jax.numpy as jnp
from jax import lax
from jax.experimental import pallas as pl
from jax.experimental.pallas import tpu as pltpu
from jax.sharding import PartitionSpec as P

HEAD = 128
SPAN = 64
SEQ = 8
SIDE = 4
ENC = SIDE * SIDE
BF = jnp.bfloat16
F32 = jnp.float32
AXES = ("seq", "enc")
NT = (((1,), (1,)), ((), ()))
NN = (((1,), (0,)), ((), ()))
TN = (((0,), (0,)), ((), ()))


def dot(a, b, dims):
    return lax.dot_general(a, b, dims, preferred_element_type=F32)


def shift_table(long_phase, shift):
    pairs = []
    for seq in range(SEQ):
        for z in range(SIDE):
            for x in range(SIDE):
                if (seq % 2 == 0) == long_phase:
                    to_z, to_x = (z + shift) % SIDE, x
                else:
                    to_z, to_x = z, (x + shift) % SIDE
                pairs.append((seq * ENC + z * SIDE + x, seq * ENC + to_z * SIDE + to_x))
    return pairs


def move_u(value, shift):
    return lax.ppermute(value, AXES, shift_table(False, shift))


def move_v(value, shift):
    return lax.ppermute(value, AXES, shift_table(True, shift))


def relative_index():
    seq, enc = lax.axis_index("seq"), lax.axis_index("enc")
    z, x = enc // SIDE, enc % SIDE
    even = seq % 2 == 0
    u, v = jnp.where(even, x, z), jnp.where(even, z, x)
    k = lax.broadcasted_iota(jnp.int32, (SIDE, SIDE), 0)
    j = lax.broadcasted_iota(jnp.int32, (SIDE, SIDE), 1)
    uu, vv = (u - j) % SIDE, (v - k) % SIDE
    return jnp.where(even, vv * SIDE + uu, uu * SIDE + vv).astype(jnp.int32)


def gather_short(own):
    one, two, three = move_u(own, 1), move_u(own, 2), move_u(own, -1)
    return jnp.stack([own, one, two, three])


def gather_long(group):
    one, three = move_v(group, 1), move_v(group, -1)
    return one, three


def gather_last(one, three):
    return move_v(one[:2], 1), move_v(three[2:], -1)


def params():
    return pltpu.CompilerParams(vmem_limit_bytes=24 * 1024 * 1024)


def accumulate_kernel(count, has_start, dims, index_ref, *refs):
    x_refs, w_refs = refs[:count], refs[count : 2 * count]
    start_ref = refs[2 * count] if has_start else None
    out_ref, total = refs[-2], refs[-1]
    step = pl.program_id(0)

    @pl.when(step == 0)
    def _():
        total[...] = start_ref[...] if has_start else jnp.zeros_like(total)

    for x_ref, w_ref in zip(x_refs, w_refs):
        total[...] += dot(x_ref[0], w_ref[...], dims)

    @pl.when(step == pl.num_programs(0) - 1)
    def _():
        out_ref[...] = total[...].astype(out_ref.dtype)


def gathered_dot(index, buffers, weight, by_rows, start, out_type):
    count, steps = len(buffers), buffers[0].shape[0]
    rows, width = buffers[0].shape[1:]
    dims = NN if by_rows else NT

    def weight_spec(b):
        if by_rows:
            return pl.BlockSpec((width, weight.shape[1]), lambda i, ix: (ix[b * steps + i], 0))
        return pl.BlockSpec((weight.shape[0], width), lambda i, ix: (0, ix[b * steps + i]))

    cols = weight.shape[1] if by_rows else weight.shape[0]
    in_specs = [pl.BlockSpec((1, rows, width), lambda i, ix: (i, 0, 0))] * count
    in_specs += [weight_spec(b) for b in range(count)]
    operands = list(buffers) + [weight] * count
    if start is not None:
        in_specs.append(pl.BlockSpec((rows, cols), lambda i, ix: (0, 0)))
        operands.append(start)
    return pl.pallas_call(
        functools.partial(accumulate_kernel, count, start is not None, dims),
        out_shape=jax.ShapeDtypeStruct((rows, cols), out_type),
        grid_spec=pltpu.PrefetchScalarGridSpec(
            num_scalar_prefetch=1,
            grid=(steps,),
            in_specs=in_specs,
            out_specs=pl.BlockSpec((rows, cols), lambda i, ix: (0, 0)),
            scratch_shapes=[pltpu.VMEM((rows, cols), F32)],
        ),
        compiler_params=params(),
        cost_estimate=pl.CostEstimate(
            flops=2 * count * steps * rows * width * cols,
            bytes_accessed=2 * count * steps * (rows + cols) * width,
            transcendentals=0,
        ),
    )(index.reshape(-1), *operands)


def far_kernel(dims, index_ref, x_ref, wa_ref, wb_ref, a_ref, b_ref):
    a_ref[0] = dot(x_ref[...], wa_ref[...], dims).astype(BF)
    b_ref[0] = dot(x_ref[...], wb_ref[...], dims).astype(BF)


def side_kernel(dims, index_ref, x_ref, w3_ref, w1_ref, a_ref, b_ref, g3_ref, g1_ref):
    first = pl.program_id(0) < 2
    g3 = dot(x_ref[...], w3_ref[...], dims)
    g1 = dot(x_ref[...], w1_ref[...], dims)
    a, b = a_ref[0].astype(F32), b_ref[0].astype(F32)
    g3_ref[0] = (g3 + jnp.where(first, a, 0.0)).astype(BF)
    g1_ref[0] = (g1 + jnp.where(first, 0.0, b)).astype(BF)


def near_kernel(dims, index_ref, x_ref, w_ref, r3_ref, r1_ref, *t_refs):
    step = pl.program_id(0)
    value = dot(x_ref[...], w_ref[...], dims) + r3_ref[0].astype(F32) + r1_ref[0].astype(F32)
    for j, t_ref in enumerate(t_refs):

        @pl.when(step == j)
        def _():
            t_ref[...] = value.astype(BF)


def scatter_sum(index, x, weight, by_rows):
    rows, inner = x.shape
    width = weight.shape[0] // ENC if by_rows else weight.shape[1] // ENC
    dims = NT if by_rows else NN

    def weight_spec(pick):
        if by_rows:
            return pl.BlockSpec((width, inner), lambda i, ix: (ix[pick(i)], 0))
        return pl.BlockSpec((inner, width), lambda i, ix: (0, ix[pick(i)]))

    x_spec = pl.BlockSpec((rows, inner), lambda i, ix: (0, 0))
    block = pl.BlockSpec((1, rows, width), lambda i, ix: (i, 0, 0))
    half = jax.ShapeDtypeStruct((2, rows, width), BF)
    whole = jax.ShapeDtypeStruct((4, rows, width), BF)
    one = jax.ShapeDtypeStruct((rows, width), BF)
    flat = index.reshape(-1)

    def call(kernel, steps, picks, extra_specs, extra, out_shape, out_specs):
        terms = steps * len(picks)
        return pl.pallas_call(
            functools.partial(kernel, dims),
            out_shape=out_shape,
            grid_spec=pltpu.PrefetchScalarGridSpec(
                num_scalar_prefetch=1,
                grid=(steps,),
                in_specs=[x_spec] + [weight_spec(pick) for pick in picks] + extra_specs,
                out_specs=out_specs,
            ),
            compiler_params=params(),
            cost_estimate=pl.CostEstimate(
                flops=2 * terms * rows * inner * width,
                bytes_accessed=2 * terms * (inner + 2 * rows) * width,
                transcendentals=0,
            ),
        )(flat, x, *([weight] * len(picks)), *extra)

    far_a, far_b = call(
        far_kernel, 2, [lambda i: 8 + i, lambda i: 10 + i], [], [], [half, half], [block, block]
    )
    from_a, from_b = move_v(far_a, 1), move_v(far_b, -1)
    low = pl.BlockSpec((1, rows, width), lambda i, ix: (jnp.minimum(i, 1), 0, 0))
    high = pl.BlockSpec((1, rows, width), lambda i, ix: (jnp.maximum(i - 2, 0), 0, 0))
    g3, g1 = call(
        side_kernel, 4, [lambda i: 12 + i, lambda i: 4 + i], [low, high], [from_a, from_b],
        [whole, whole], [block, block],
    )
    r3, r1 = move_v(g3, 1), move_v(g1, -1)
    pieces = call(
        near_kernel, 4, [lambda i: i], [block, block], [r3, r1], [one] * 4,
        [pl.BlockSpec((rows, width), lambda i, ix: (0, 0))] * 4,
    )
    return scatter_short(pieces)


def scatter_short(pieces):
    t0, t1, t2, t3 = pieces
    q1, q2, q3 = move_u(t1, -1), move_u(t2, 2), move_u(t3, 1)
    total = t0.astype(F32) + q1.astype(F32) + q2.astype(F32) + q3.astype(F32)
    return total.astype(BF)


def pair_kernel(extra, dk_ref, dv_ref, wk_ref, wv_ref, *refs):
    out_refs = refs[len(extra) :]
    total = dot(dk_ref[...], wk_ref[...], NT) + dot(dv_ref[...], wv_ref[...], NT)
    rows = total.shape[0]
    for place, ref in zip(extra, refs):
        part = ref[...].astype(F32)
        if place == "low":
            total = total + jnp.concatenate([part, jnp.zeros_like(part)], axis=0)
        elif place == "high":
            total = total + jnp.concatenate([jnp.zeros_like(part), part], axis=0)
        else:
            total = total + part
    each = rows // len(out_refs)
    for n, out_ref in enumerate(out_refs):
        out_ref[...] = total[n * each : (n + 1) * each].astype(BF)


def pair_dot(dk, dv, key_weight, value_weight, extra, places, outs):
    rows, inner = dk.shape
    features = key_weight.shape[0]
    tile = 512
    d_spec = pl.BlockSpec((rows, inner), lambda i: (0, 0))
    w_spec = pl.BlockSpec((tile, inner), lambda i: (i, 0))

    def cols(height):
        return pl.BlockSpec((height, tile), lambda i: (0, i))

    return pl.pallas_call(
        functools.partial(pair_kernel, places),
        out_shape=[jax.ShapeDtypeStruct((rows // outs, features), BF)] * outs,
        grid=(features // tile,),
        in_specs=[d_spec, d_spec, w_spec, w_spec] + [cols(value.shape[0]) for value in extra],
        out_specs=[cols(rows // outs)] * outs,
        compiler_params=params(),
        cost_estimate=pl.CostEstimate(
            flops=4 * rows * inner * features,
            bytes_accessed=4 * (rows + inner) * features,
            transcendentals=0,
        ),
    )(dk, dv, key_weight, value_weight, *extra)


def read_rows(refs):
    return jnp.concatenate([ref[...].reshape(-1, ref.shape[-1]) for ref in refs], axis=0)


def softmax(q, k):
    scores = dot(q, k, NT) * HEAD ** (-0.5)
    exponent = jnp.exp(scores - jnp.max(scores, axis=-1, keepdims=True))
    return exponent / jnp.sum(exponent, axis=-1, keepdims=True)


def forward_kernel(count, q_ref, *refs):
    keys, values = read_rows(refs[:count]), read_rows(refs[count : 2 * count])
    out_ref = refs[-1]
    for h in range(q_ref.shape[1] // HEAD):
        cols = slice(h * HEAD, (h + 1) * HEAD)
        low = softmax(q_ref[:, cols], keys[:, cols]).astype(BF)
        out_ref[:, cols] = dot(low, values[:, cols], NN).astype(BF)


def backward_kernel(count, q_ref, d_ref, *refs):
    keys, values = read_rows(refs[:count]), read_rows(refs[count : 2 * count])
    dq_ref, dk_refs, dv_refs = refs[2 * count], refs[2 * count + 1 : 2 * count + 5], refs[2 * count + 5 :]
    for h in range(q_ref.shape[1] // HEAD):
        cols = slice(h * HEAD, (h + 1) * HEAD)
        q, d, k, v = q_ref[:, cols], d_ref[:, cols], keys[:, cols], values[:, cols]
        attention = softmax(q, k)
        d_attention = dot(d, v, NT)
        inner = jnp.sum(attention * d_attention, axis=-1, keepdims=True)
        d_scores = (attention * (d_attention - inner) * HEAD ** (-0.5)).astype(BF)
        dq_ref[:, cols] = dot(d_scores, k, NN).astype(BF)
        dk = dot(d_scores, q, TN).astype(BF)
        dv = dot(attention.astype(BF), d, TN).astype(BF)
        for n in range(SIDE):
            shape = dk_refs[n].shape[:3] + (HEAD,)
            rows = slice(n * SPAN, (n + 1) * SPAN)
            dk_refs[n][:, :, :, cols] = dk[rows].reshape(shape)
            dv_refs[n][:, :, :, cols] = dv[rows].reshape(shape)


def attention_specs(keys, cols):
    return [pl.BlockSpec((k.shape[0], 1, 16, cols), lambda c: (0, c, 0, 0)) for k in keys]


def attend(queries, keys, values):
    rows, cols = queries.shape
    q_spec = pl.BlockSpec((SPAN, cols), lambda c: (c, 0))
    kv = attention_specs(keys, cols)
    return pl.pallas_call(
        functools.partial(forward_kernel, len(keys)),
        out_shape=jax.ShapeDtypeStruct((rows, cols), BF),
        grid=(rows // SPAN,),
        in_specs=[q_spec] + kv + kv,
        out_specs=q_spec,
        compiler_params=params(),
        cost_estimate=pl.CostEstimate(
            flops=4 * rows * 256 * cols, bytes_accessed=6 * 1024 * cols, transcendentals=rows * 1024
        ),
    )(queries, *keys, *values)


def attend_back(queries, d_context, keys, values):
    rows, cols = queries.shape
    q_spec = pl.BlockSpec((SPAN, cols), lambda c: (c, 0))
    kv = attention_specs(keys, cols)
    group = jax.ShapeDtypeStruct((SIDE, rows // SPAN, 16, cols), BF)
    group_spec = pl.BlockSpec((SIDE, 1, 16, cols), lambda c: (0, c, 0, 0))
    out = pl.pallas_call(
        functools.partial(backward_kernel, len(keys)),
        out_shape=[jax.ShapeDtypeStruct((rows, cols), BF)] + [group] * 8,
        grid=(rows // SPAN,),
        in_specs=[q_spec, q_spec] + kv + kv,
        out_specs=[q_spec] + [group_spec] * 8,
        compiler_params=params(),
        cost_estimate=pl.CostEstimate(
            flops=12 * rows * 256 * cols, bytes_accessed=12 * 1024 * cols, transcendentals=rows * 1024
        ),
    )(queries, d_context, *keys, *values)
    return out[0], [g.reshape(-1, cols) for g in out[1:5]], [g.reshape(-1, cols) for g in out[5:]]


def on_device(
    hidden,
    query_weight,
    key_weight,
    value_weight,
    output_weight,
    neighbour_states,
    neighbour_slot,
    d_output,
):
    index = relative_index()
    features = key_weight.shape[0]
    local = neighbour_states.shape[2]
    cols = query_weight.shape[1]
    chunk = neighbour_states.shape[1] // ENC
    used = neighbour_slot.size
    slot_shard = neighbour_slot.reshape(-1) // SEQ

    def index_of(*places):
        return jnp.concatenate([index[k, a:b] for k, a, b in places])

    arrived = lax.all_to_all(
        neighbour_states.reshape(SEQ * ENC, chunk, local), AXES, split_axis=0, concat_axis=0, tiled=True
    )
    h0 = gather_short(hidden)
    d0 = gather_short(d_output)
    arrived = arrived.reshape(SEQ, ENC, chunk, local)
    picked = jnp.take(arrived, slot_shard, axis=1)
    picked = picked.transpose(1, 2, 0, 3).reshape(used * chunk, features)

    s0 = gather_short(picked)
    h1, h3 = gather_long(h0)
    s1, s3 = gather_long(s0)
    h2a, h2b = gather_last(h1, h3)
    s2a, s2b = gather_last(s1, s3)
    d1, d3 = gather_long(d0)

    queries = gathered_dot(index_of((0, 0, 4)), [h0], query_weight, True, None, F32)
    queries = gathered_dot(index_of((1, 0, 4), (3, 0, 4)), [h1, h3], query_weight, True, queries, F32)
    queries = gathered_dot(index_of((2, 0, 2), (2, 2, 4)), [h2a, h2b], query_weight, True, queries, BF)

    def project(group, weight):
        flat = group.reshape(-1, features)
        return dot(flat, weight, NN).astype(BF).reshape(group.shape[0], -1, 16, cols)

    groups = [s0, s1, s2a, s2b, s3]
    keys = [project(group, key_weight) for group in groups]
    values = [project(group, value_weight) for group in groups]

    context = attend(queries, keys, values)
    output = scatter_sum(index, context, output_weight, False)

    d2a, d2b = gather_last(d1, d3)
    d_context = gathered_dot(index_of((0, 0, 4)), [d0], output_weight, False, None, F32)
    d_context = gathered_dot(index_of((1, 0, 4), (3, 0, 4)), [d1, d3], output_weight, False, d_context, F32)
    d_context = gathered_dot(index_of((2, 0, 2), (2, 2, 4)), [d2a, d2b], output_weight, False, d_context, BF)

    d_queries, d_keys, d_values = attend_back(queries, d_context, keys, values)

    def pair(k, extra, places, outs):
        return pair_dot(d_keys[k], d_values[k], key_weight, value_weight, extra, places, outs)

    far_a, far_b = pair(2, [], (), 2)
    from_a, from_b = move_v(far_a, 1), move_v(far_b, -1)
    (g3,) = pair(3, [from_a], ("low",), 1)
    (g1,) = pair(1, [from_b], ("high",), 1)
    r3, r1 = move_v(g3, 1), move_v(g1, -1)
    summed = scatter_short(pair(0, [r3, r1], ("all", "all"), 4))

    d_hidden = scatter_sum(index, d_queries, query_weight, True)

    placing = lax.broadcasted_iota(jnp.int32, (ENC, used), 0) == slot_shard[None, :]
    spread = summed.reshape(used, chunk, SEQ, local).transpose(2, 0, 1, 3)
    rank = jnp.argmax(placing, axis=1)
    spread = jnp.take(spread, rank, axis=1)
    spread = jnp.where(jnp.any(placing, axis=1)[None, :, None, None], spread, 0)
    back = lax.all_to_all(
        spread.reshape(SEQ * ENC, chunk, local), AXES, split_axis=0, concat_axis=0, tiled=True
    )
    d_states = back.reshape(neighbour_states.shape)
    return (output, d_hidden, d_states)


def solution(mesh):
    in_specs = (
        P("seq", "enc"),
        P(None, "enc"),
        P(None, "enc"),
        P(None, "enc"),
        P("enc", None),
        P("enc", None, "seq"),
        P("seq", None),
        P("seq", "enc"),
    )
    out_specs = (P("seq", "enc"), P("seq", "enc"), P("enc", None, "seq"))
    return jax.shard_map(
        on_device, mesh=mesh, in_specs=in_specs, out_specs=out_specs, check_vma=False
    )
```

time: 566 us -> 236 us (0.42); the launches traced: 556 us -> 234 us
  waiting for transfers between devices: 358 us -> 44.7 us
  starting transfers between devices: 6.07 us -> 79.1 us
  matrix products: 82.1 us -> 11.2 us
  Pallas kernels: 0 us -> 64.7 us
  local copies, waits for them, and re-layouts: 64.7 us -> 26 us
  blocking collectives: 15.4 us -> 0 us
  between operations: 14.5 us -> 1.31 us
  other arithmetic: 14.8 us -> 7.42 us
    all_gather x3 -> x0, waiting for transfers between devices: 168 us -> none  [the longest x1 74.9 us: on_device(): pooled = lax.all_gather(neighbour_states, 'enc', axis=0, tiled=True)]
    reduce_scatter x2 -> x0, waiting for transfers between devices: 130 us -> none  [the longest x1 81.2 us: on_device(): lax.psum_scatter(input_terms.astype(jnp.bfloat16), 'enc', scatter_dimensi...]
    dot_general x13 -> x10, matrix products: 82.1 us -> 11.2 us  [dot(): return lax.dot_general(a, b, dims, preferred_element_type=F32)]
    pallas_call x0 -> x18, Pallas kernels: none -> 64.7 us  [the longest x6 20 us: call(): pl.pallas_call(functools.partial(kernel, dims), out_shape=out_shape, grid...]
    unnamed x7 -> x0, waiting for transfers between devices: 59.6 us -> none
    ppermute x0 -> x42, starting transfers between devices: none -> 56.9 us  [the longest x24 30.3 us: move_v(): return lax.ppermute(value, AXES, shift_table(True, shift))]
    ppermute x0 -> x42, waiting for transfers between devices: none -> 37.2 us  [the longest x24 19.7 us: move_v(): return lax.ppermute(value, AXES, shift_table(True, shift))]
    all_to_all x1 -> x2, starting transfers between devices: 5.66 us -> 22.3 us  [the longest x1 11.7 us: on_device(): lax.all_to_all(spread.reshape(SEQ * ENC, chunk, local), AXES, split_axis=...]
  transfers between devices with their start and end apart: 7 -> 44, of which waited for: 6 -> 9; matrix products, arithmetic and copies ran while one was open for 12% -> 11% of each run, Pallas kernels for 0% -> 23%
where the time goes in v1:
time: 236 us; the launch traced here: 234 us
  starting transfers between devices  79.1 us (34%)
  Pallas kernels  64.7 us (27%)
  waiting for transfers between devices  44.7 us (19%)
  local copies, waits for them, and re-layouts  26 us (11%)
  matrix products  11.2 us (5%)
  other arithmetic  7.42 us (3%)
    ppermute x24, starting transfers between devices, move_v(): return lax.ppermute(value, AXES, shift_table(True, shift))  30.3 us
    ppermute x18, starting transfers between devices, move_u(): return lax.ppermute(value, AXES, shift_table(False, shift))  26.6 us
    pallas_call x6, Pallas kernels, call(): pl.pallas_call(functools.partial(kernel, dims), out_shape=out_shape, grid...  20 us
    ppermute x24, waiting for transfers between devices, move_v(): return lax.ppermute(value, AXES, shift_table(True, shift))  19.7 us
    unnamed x32, local copies, waits for them, and re-layouts  18.5 us
    pallas_call x6, Pallas kernels, gathered_dot(): pl.pallas_call(functools.partial(accumulate_kernel, count, start is not N...  17.9 us
    ppermute x18, waiting for transfers between devices, move_u(): return lax.ppermute(value, AXES, shift_table(False, shift))  17.6 us
    pallas_call x4, Pallas kernels, pair_dot(): pl.pallas_call(functools.partial(pair_kernel, places), out_shape=[jax.Sha...  12.3 us
  transfers between devices with their start and end apart: 44, of which 9 were waited for; matrix products, arithmetic and copies ran while one was open for 11% of the time, Pallas kernels for 23%

profile of v1, /device:TPU:1, one launch (start us, length us, event | category | flops | bytes accessed | tf_op | source)
XLA Modules:
  0.0 234.5 jit_solution(2327386520182207401)
XLA Ops:
  0.6 2.5 %collective-permute-start.21 = (bf16[256,512]{1,0:T(8,128)(2,1)}, bf16[256,512]{1,0:T(8,128)(2,1)S(1)}, u32[]{:S(2)}, u32[]{:S(2)}) collective-permute-start(bf16[256,512]{1,0:T(8,128)(2,1)} %param.15), channel_id=1, source_target_pairs={{0,1},{1,2},{2,3},{3,0},{4,5},{5,6},{6,7},{7,4},{8,9},{9,10},{10,1... | collective-permute-start | bytes 786440 | tf_op jit(solution)/shard_map/ppermute | solution.py:41
  3.2 3.3 %collective-permute-start.22 = (bf16[256,512]{1,0:T(8,128)(2,1)}, bf16[256,512]{1,0:T(8,128)(2,1)S(1)}, u32[]{:S(2)}, u32[]{:S(2)}) collective-permute-start(bf16[256,512]{1,0:T(8,128)(2,1)} %param.15), channel_id=1, source_target_pairs={{0,2},{1,3},{2,0},{3,1},{4,6},{5,7},{6,4},{7,5},{8,10},{9,11},{10,... | collective-permute-start | bytes 786440 | tf_op jit(solution)/shard_map/ppermute | solution.py:41
  8.4 10.6 %all-to-all-start = ((bf16[128,8,256]{2,1,0:T(8,128)(2,1)}), bf16[128,8,256]{2,1,0:T(8,128)(2,1)S(1)}, u32[]{:S(2)}, u32[]{:S(2)}) async-start(bf16[128,8,256]{2,1,0:T(8,128)(2,1)} %bitcast.128), calls=%async_computation | async-start | bytes 1048576 | tf_op jit(solution)/shard_map/all_to_all | solution.py:359
  20.1 3.3 %collective-permute-start.2 = (bf16[256,512]{1,0:T(8,128)(2,1)}, bf16[256,512]{1,0:T(8,128)(2,1)S(1)}, u32[]{:S(2)}, u32[]{:S(2)}) collective-permute-start(bf16[256,512]{1,0:T(8,128)(2,1)} %param.8), channel_id=1, source_target_pairs={{0,3},{1,0},{2,1},{3,2},{4,7},{5,4},{6,5},{7,6},{8,11},{9,8},{10,9... | collective-permute-start | bytes 786440 | tf_op jit(solution)/shard_map/ppermute | solution.py:41
  23.5 1.1 pad_maximum_fusion.2.refs_0_
  24.6 1.3 collective-permute-start.24
  25.8 7.4 %all-to-all-done = bf16[128,8,256]{2,1,0:T(8,128)(2,1)S(1)} async-done(((bf16[128,8,256]{2,1,0:T(8,128)(2,1)}), bf16[128,8,256]{2,1,0:T(8,128)(2,1)S(1)}, u32[]{:S(2)}, u32[]{:S(2)}) %all-to-all-start) | async-done | bytes 524320 | tf_op jit(solution)/shard_map/all_to_all | solution.py:359
  34.1 1.5 collective-permute-start.8
  35.6 1.8 collective-permute-start.9
  37.7 1.1 pad_maximum_fusion.refs_0_
  38.8 6.0 %collective-permute-done.7 = bf16[64,2048]{1,0:T(8,128)(2,1)S(1)} collective-permute-done((bf16[64,2048]{1,0:T(8,128)(2,1)S(1)}, bf16[64,2048]{1,0:T(8,128)(2,1)S(1)}, u32[]{:S(2)}, u32[]{:S(2)}) %collective-permute-start.7) | collective-permute-done | bytes 262176 | tf_op jit(solution)/shard_map/ppermute | solution.py:41
  45.1 2.7 %collective-permute-done.8 = bf16[64,2048]{1,0:T(8,128)(2,1)S(1)} collective-permute-done((bf16[64,2048]{1,0:T(8,128)(2,1)S(1)}, bf16[64,2048]{1,0:T(8,128)(2,1)S(1)}, u32[]{:S(2)}, u32[]{:S(2)}) %collective-permute-start.8) | collective-permute-done | bytes 262176 | tf_op jit(solution)/shard_map/ppermute | solution.py:41
  48.4 1.1 pad_maximum_fusion.1
  50.8 3.4 %copy-done.2 = bf16[512,8192]{1,0:T(8,128)(2,1)S(1)} copy-done((bf16[512,8192]{1,0:T(8,128)(2,1)S(1)}, bf16[512,8192]{1,0:T(8,128)(2,1)}, u32[]{:S(2)}) %copy-start.2) | copy-done | bytes 8388632
  54.2 2.2 shard_map.110.refs_4_
  56.4 3.4 %copy-done = bf16[8192,512]{1,0:T(8,128)(2,1)S(1)} copy-done((bf16[8192,512]{1,0:T(8,128)(2,1)S(1)}, bf16[8192,512]{1,0:T(8,128)(2,1)}, u32[]{:S(2)}) %copy-start) | copy-done | bytes 8388632
  59.8 3.7 %shard_map.103.refs_4_ = f32[256,512]{1,0:T(8,128)S(1)} custom-call(s32[4]{0:T(128)S(1)} %get-tuple-element.69.index_ref, bf16[4,256,512]{2,1,0:T(8,128)(2,1)} %pad_maximum_fusion.refs_0_, bf16[8192,512]{1,0:T(8,128)(2,1)S(1)} %copy-done), custom_call_target="tpu_custom_call" | custom-call | flops 536870912 | bytes 3145728 | tf_op jit(solution)/shard_map/pallas_call | solution.py:112
  63.6 2.1 convolution_convert_fusion.5
  65.7 1.9 collective-permute-start.12
  67.5 2.0 convolution_convert_fusion.2
  69.5 1.1 slice.57
  70.7 1.1 slice.58
  71.8 2.7 %collective-permute-start.27 = (bf16[2,256,512]{2,1,0:T(8,128)(2,1)S(1)}, bf16[2,256,512]{2,1,0:T(8,128)(2,1)S(1)}, u32[]{:S(2)}, u32[]{:S(2)}) collective-permute-start(bf16[2,256,512]{2,1,0:T(8,128)(2,1)S(1)} %slice.58), channel_id=1, source_target_pairs={{0,12},{1,13},{2,14},{3,15},{4,0},{5,1},{6,2},{7,3},{8,4},{9,5},{1... | collective-permute-start | bytes 1572872 | tf_op jit(solution)/shard_map/ppermute | solution.py:45
  75.7 1.2 slice.54
  76.9 4.7 %shard_map.111.refs_4_ = f32[256,512]{1,0:T(8,128)S(1)} custom-call(s32[8]{0:T(128)S(1)} %pad_add_fusion.1.index_ref, bf16[4,256,512]{2,1,0:T(8,128)(2,1)} %collective-permute-done.24.refs_0_, bf16[4,256,512]{2,1,0:T(8,128)(2,1)} %collective-permute-done.26.refs_1_, bf16[512,8192]{1,0:T(8,128)(2,1)S(1)} %bitcast.86, bf16[512,8192]{1,0:T(8,128)(2,1)S(1)} %bitcast.86, ...), custom_call_target="tpu_custom_call" | custom-call | flops 1073741824 | bytes 6291456 | tf_op jit(solution)/shard_map/pallas_call | solution.py:112
  81.7 4.1 %shard_map.104.refs_4_ = f32[256,512]{1,0:T(8,128)S(1)} custom-call(s32[8]{0:T(128)S(1)} %pad_add_fusion.1.index_ref, bf16[4,256,512]{2,1,0:T(8,128)(2,1)} %collective-permute-done.3.refs_0_, bf16[4,256,512]{2,1,0:T(8,128)(2,1)} %collective-permute-done.5.refs_1_, bf16[8192,512]{1,0:T(8,128)(2,1)S(1)} %bitcast.84, bf16[8192,512]{1,0:T(8,128)(2,1)S(1)} %bitcast.84, ...), custom_call_target="tpu_custom_call" | custom-call | flops 1073741824 | bytes 6291456 | tf_op jit(solution)/shard_map/pallas_call | solution.py:112
  85.7 2.7 %collective-permute-start.6 = (bf16[2,256,512]{2,1,0:T(8,128)(2,1)S(1)}, bf16[2,256,512]{2,1,0:T(8,128)(2,1)S(1)}, u32[]{:S(2)}, u32[]{:S(2)}) collective-permute-start(bf16[2,256,512]{2,1,0:T(8,128)(2,1)S(1)} %slice.54), channel_id=1, source_target_pairs={{0,12},{1,13},{2,14},{3,15},{4,0},{5,1},{6,2},{7,3},{8,4},{9,5},{1... | collective-permute-start | bytes 1572872 | tf_op jit(solution)/shard_map/ppermute | solution.py:45
  88.5 1.1 slice.55
  89.6 1.9 convolution_convert_fusion.4
  91.5 1.9 convolution_convert_fusion.1
  95.2 2.7 %collective-permute-start.13 = (bf16[2,64,2048]{2,1,0:T(8,128)(2,1)S(1)}, bf16[2,64,2048]{2,1,0:T(8,128)(2,1)S(1)}, u32[]{:S(2)}, u32[]{:S(2)}) collective-permute-start(bf16[2,64,2048]{2,1,0:T(8,128)(2,1)S(1)} %slice.56), channel_id=1, source_target_pairs={{0,12},{1,13},{2,14},{3,15},{4,0},{5,1},{6,2},{7,3},{8,4},{9,5},{1... | collective-permute-start | bytes 1572872 | tf_op jit(solution)/shard_map/ppermute | solution.py:45
  98.0 1.8 shard_map.112.d_ref
  99.8 1.5 shard_map.105.q_ref
  101.3 1.9 collective-permute-done.11
  105.2 8.6 %shard_map.113 = (bf16[256,512]{1,0:T(8,128)(2,1)S(1)}, bf16[4,4,16,512]{3,2,1,0:T(8,128)(2,1)S(1)}, bf16[4,4,16,512]{3,2,1,0:T(8,128)(2,1)S(1)}, bf16[4,4,16,51...) custom-call(bf16[256,512]{1,0:T(8,128)(2,1)S(1)} %shard_map.105.q_re, ...), custom_call_target="tpu_custom_call" | custom-call | flops 402653184 | bytes 6291456 | tf_op jit(solution)/shard_map/pallas_call | solution.py:324
  113.8 2.0 shard_map.117
  115.8 3.4 %collective-permute-start.37 = (bf16[128,2048]{1,0:T(8,128)(2,1)S(1)}, bf16[128,2048]{1,0:T(8,128)(2,1)S(1)}, u32[]{:S(2)}, u32[]{:S(2)}) collective-permute-start(bf16[128,2048]{1,0:T(8,128)(2,1)S(1)} %get-tuple-element.62), channel_id=1, source_target_pairs={{0,12},{1,13},{2,14},{3,15},{4,0},{5,1},{6,2},{7,3},{8,4},{9,5},{1... | collective-permute-start | bytes 1572872 | tf_op jit(solution)/shard_map/ppermute | solution.py:45
  119.2 1.5 shard_map.114
  120.8 2.7 %collective-permute-start.29 = (bf16[2,256,512]{2,1,0:T(8,128)(2,1)S(1)}, bf16[2,256,512]{2,1,0:T(8,128)(2,1)S(1)}, u32[]{:S(2)}, u32[]{:S(2)}) collective-permute-start(bf16[2,256,512]{2,1,0:T(8,128)(2,1)S(1)} %get-tuple-element.45), channel_id=1, source_target_pairs={{0,12},{1,13},{2,14},{3,15},{4,0},{5,1},{6,2},{7,3},{8,4},{9,5},{1... | collective-permute-start | bytes 1572872 | tf_op jit(solution)/shard_map/ppermute | solution.py:45
  123.5 5.9 %shard_map.106.x_ref = bf16[256,512]{1,0:T(8,128)(2,1)S(1)} custom-call(bf16[256,512]{1,0:T(8,128)(2,1)S(1)} %shard_map.105.q_ref, bf16[4,4,16,512]{3,2,1,0:T(8,128)(2,1)S(1)} %bitcast.96, bf16[4,4,16,512]{3,2,1,0:T(8,128)(2,1)S(1)} %bitcast.100, bf16[2,4,16,512]{3,2,1,0:T(8,128)(2,1)S(1)} %bitcast.88, bf16[2,4,16,512]{3,2,1,0:T(8,128)(2,1)S(1)} %bitcast.92, ...), custom_call_target="tpu_custom_call" | custom-call | flops 134217728 | bytes 3145728 | tf_op jit(solution)/shard_map/pallas_call | solution.py:305
  129.4 2.3 %shard_map.107 = (bf16[2,256,512]{2,1,0:T(8,128)(2,1)S(1)}, bf16[2,256,512]{2,1,0:T(8,128)(2,1)}) custom-call(s32[16]{0:T(128)S(1)} %broadcast_select_fusion.1.index_ref, bf16[256,512]{1,0:T(8,128)(2,1)S(1)} %shard_map.106.x_ref, bf16[512,8192]{1,0:T(8,128)(2,1)S(1)} %bitcast.86, bf16[512,8192]{1,0:T(8,128)(2,1)S(1)} %bitcast.86), custom_call_target="tpu_custom_call" | custom-call | flops 536870912 | bytes 4194304 | tf_op jit(solution)/shard_map/pallas_call | solution.py:174
  131.8 3.0 %shard_map.119 = bf16[256,2048]{1,0:T(8,128)(2,1)} custom-call(bf16[256,512]{1,0:T(8,128)(2,1)S(1)} %bitcast.109, bf16[256,512]{1,0:T(8,128)(2,1)S(1)} %bitcast.110, bf16[2048,512]{1,0:T(8,128)(2,1)S(1)} %copy-done.5, bf16[2048,512]{1,0:T(8,128)(2,1)S(1)} %copy-done.6, bf16[128,2048]{1,0:T(8,128)(2,1)S(1)} %collective-permute-done.37.refs_0_), custom_call_target="tpu_custom_call" | custom-call | flops 1073741824 | bytes 6291456 | tf_op jit(solution)/shard_map/pallas_call | solution.py:243
  134.8 2.7 %collective-permute-start.38 = (bf16[256,2048]{1,0:T(8,128)(2,1)}, bf16[256,2048]{1,0:T(8,128)(2,1)}, u32[]{:S(2)}, u32[]{:S(2)}) collective-permute-start(bf16[256,2048]{1,0:T(8,128)(2,1)} %shard_map.119), channel_id=1, source_target_pairs={{0,12},{1,13},{2,14},{3,15},{4,0},{5,1},{6,2},{7,3},{8,4},{9,5},{1... | collective-permute-start | bytes 3145736 | tf_op jit(solution)/shard_map/ppermute | solution.py:45
  137.4 2.9 %shard_map.118 = bf16[256,2048]{1,0:T(8,128)(2,1)} custom-call(bf16[256,512]{1,0:T(8,128)(2,1)S(1)} %bitcast.107, bf16[256,512]{1,0:T(8,128)(2,1)S(1)} %bitcast.108, bf16[2048,512]{1,0:T(8,128)(2,1)S(1)} %copy-done.5, bf16[2048,512]{1,0:T(8,128)(2,1)S(1)} %copy-done.6, bf16[128,2048]{1,0:T(8,128)(2,1)S(1)} %collective-permute-done.35.refs_0_), custom_call_target="tpu_custom_call" | custom-call | flops 1073741824 | bytes 6291456 | tf_op jit(solution)/shard_map/pallas_call | solution.py:243
  140.4 3.4 %shard_map.115 = (bf16[4,256,512]{2,1,0:T(8,128)(2,1)}, bf16[4,256,512]{2,1,0:T(8,128)(2,1)}) custom-call(s32[16]{0:T(128)S(1)} %broadcast_select_fusion.1.index_ref, bf16[256,512]{1,0:T(8,128)(2,1)S(1)} %get-tuple-element.43.x_ref, bf16[8192,512]{1,0:T(8,128)(2,1)S(1)} %bitcast.84, bf16[8192,512]{1,0:T(8,128)(2,1)S(1)} %bitcast.84, ...), custom_call_target="tpu_custom_call" | custom-call | flops 1073741824 | bytes 8388608 | tf_op jit(solution)/shard_map/pallas_call | solution.py:174
  143.8 2.7 %collective-permute-start.31 = (bf16[4,256,512]{2,1,0:T(8,128)(2,1)}, bf16[4,256,512]{2,1,0:T(8,128)(2,1)}, u32[]{:S(2)}, u32[]{:S(2)}) collective-permute-start(bf16[4,256,512]{2,1,0:T(8,128)(2,1)} %get-tuple-element.47), channel_id=1, source_target_pairs={{0,12},{1,13},{2,14},{3,15},{4,0},{5,1},{6,2},{7,3},{8,4},{9,5},{1... | collective-permute-start | bytes 3145736 | tf_op jit(solution)/shard_map/ppermute | solution.py:45
  146.5 1.5 collective-permute-start.15
  148.7 17.7 %collective-permute-done.15.b_ref = bf16[2,256,512]{2,1,0:T(8,128)(2,1)} collective-permute-done((bf16[2,256,512]{2,1,0:T(8,128)(2,1)}, bf16[2,256,512]{2,1,0:T(8,128)(2,1)}, u32[]{:S(2)}, u32[]{:S(2)}) %collective-permute-start.15) | collective-permute-done | bytes 524320 | tf_op jit(solution)/shard_map/ppermute | solution.py:45
  166.3 3.4 %copy-done.3 = bf16[512,8192]{1,0:T(8,128)(2,1)S(1)} copy-done((bf16[512,8192]{1,0:T(8,128)(2,1)S(1)}, bf16[512,8192]{1,0:T(8,128)(2,1)}, u32[]{:S(2)}) %copy-start.3) | copy-done | bytes 8388632
  169.7 5.0 %shard_map.108 = (bf16[4,256,512]{2,1,0:T(8,128)(2,1)}, bf16[4,256,512]{2,1,0:T(8,128)(2,1)}) custom-call(s32[16]{0:T(128)S(1)} %broadcast_select_fusion.1.index_ref, bf16[256,512]{1,0:T(8,128)(2,1)S(1)} %shard_map.106.x_ref, bf16[512,8192]{1,0:T(8,128)(2,1)S(1)} %copy-done.3, bf16[512,8192]{1,0:T(8,128)(2,1)S(1)} %copy-done.3, ...), custom_call_target="tpu_custom_call" | custom-call | flops 1073741824 | bytes 8388608 | tf_op jit(solution)/shard_map/pallas_call | solution.py:174
  175.1 3.2 %collective-permute-start.17 = (bf16[4,256,512]{2,1,0:T(8,128)(2,1)}, bf16[4,256,512]{2,1,0:T(8,128)(2,1)}, u32[]{:S(2)}, u32[]{:S(2)}) collective-permute-start(bf16[4,256,512]{2,1,0:T(8,128)(2,1)} %get-tuple-element.38), channel_id=1, source_target_pairs={{0,12},{1,13},{2,14},{3,15},{4,0},{5,1},{6,2},{7,3},{8,4},{9,5},{1... | collective-permute-start | bytes 3145736 | tf_op jit(solution)/shard_map/ppermute | solution.py:45
  178.2 4.4 %shard_map.120 = (bf16[64,2048]{1,0:T(8,128)(2,1)S(1)}, bf16[64,2048]{1,0:T(8,128)(2,1)}, bf16[64,2048]{1,0:T(8,128)(2,1)}, bf16[64,2048]{1,0:T(8,128)(2,1)}) custom-call(bf16[256,512]{1,0:T(8,128)(2,1)S(1)} %bitcast.113, bf16[256,512]{1,0:T(8,128)(2,1)S(1)} %bitcast.114, bf16[2048,512]{1,0:T(8,128)(2,1)S(1)} %copy-done.5, bf16[2048,512]{1,0:T(8,128)(2,1)S(1)} %copy-done.7, ...), custom_call_target="tpu_custom_call" | custom-call | flops 1073741824 | bytes 6291456 | tf_op jit(solution)/shard_map/pallas_call | solution.py:243
  184.4 3.4 %copy-done.1 = bf16[8192,512]{1,0:T(8,128)(2,1)S(1)} copy-done((bf16[8192,512]{1,0:T(8,128)(2,1)S(1)}, bf16[8192,512]{1,0:T(8,128)(2,1)}, u32[]{:S(2)}) %copy-start.1) | copy-done | bytes 8388632
  187.8 3.8 %shard_map.116 = (bf16[256,512]{1,0:T(8,128)(2,1)S(1)}, bf16[256,512]{1,0:T(8,128)(2,1)S(1)}, bf16[256,512]{1,0:T(8,128)(2,1)S(1)}, bf16[256,512]{1,0:T(8,128)(2,1)S(1)}) custom-call(s32[16]{0:T(128)S(1)} %broadcast_select_fusion.1.index_ref, bf16[256,512]{1,0:T(8,128)(2,1)S(1)} %get-tuple-element.43.x_ref, bf16[8192,512]{1,0:T(8,128)(2,1)S(1)} %copy-done.1, ...), custom_call_target="tpu_custom_call" | custom-call | flops 536870912 | bytes 4194304 | tf_op jit(solution)/shard_map/pallas_call | solution.py:174
  191.6 2.4 %collective-permute-start.32 = (bf16[256,512]{1,0:T(8,128)(2,1)S(1)}, bf16[256,512]{1,0:T(8,128)(2,1)S(1)}, u32[]{:S(2)}, u32[]{:S(2)}) collective-permute-start(bf16[256,512]{1,0:T(8,128)(2,1)S(1)} %get-tuple-element.49), channel_id=1, source_target_pairs={{0,3},{1,0},{2,1},{3,2},{4,7},{5,4},{6,5},{7,6},{8,11},{9,8},{10,9... | collective-permute-start | bytes 786440 | tf_op jit(solution)/shard_map/ppermute | solution.py:41
  194.0 1.5 collective-permute-start.33
  196.4 2.5 %collective-permute-start.34 = (bf16[256,512]{1,0:T(8,128)(2,1)S(1)}, bf16[256,512]{1,0:T(8,128)(2,1)S(1)}, u32[]{:S(2)}, u32[]{:S(2)}) collective-permute-start(bf16[256,512]{1,0:T(8,128)(2,1)S(1)} %get-tuple-element.51), channel_id=1, source_target_pairs={{0,1},{1,2},{2,3},{3,0},{4,5},{5,6},{6,7},{7,4},{8,9},{9,10},{10,1... | collective-permute-start | bytes 786440 | tf_op jit(solution)/shard_map/ppermute | solution.py:41
  199.8 1.1 fusion
  200.9 11.7 %all-to-all-start.1 = ((bf16[128,8,256]{2,1,0:T(8,128)(2,1)}), bf16[128,8,256]{2,1,0:T(8,128)(2,1)S(1)}, u32[]{:S(2)}, u32[]{:S(2)}) async-start(bf16[128,8,256]{2,1,0:T(8,128)(2,1)} %fusion), calls=%async_computation.1 | async-start | bytes 1048576 | tf_op jit(solution)/shard_map/all_to_all | solution.py:414
  212.7 3.4 %copy-done.4 = bf16[512,8192]{1,0:T(8,128)(2,1)S(1)} copy-done((bf16[512,8192]{1,0:T(8,128)(2,1)S(1)}, bf16[512,8192]{1,0:T(8,128)(2,1)}, u32[]{:S(2)}) %copy-start.4) | copy-done | bytes 8388632
  216.0 3.8 %shard_map.109 = (bf16[256,512]{1,0:T(8,128)(2,1)S(1)}, bf16[256,512]{1,0:T(8,128)(2,1)S(1)}, bf16[256,512]{1,0:T(8,128)(2,1)S(1)}, bf16[256,512]{1,0:T(8,128)(2,1)S(1)}) custom-call(s32[16]{0:T(128)S(1)} %broadcast_select_fusion.1.index_ref, bf16[256,512]{1,0:T(8,128)(2,1)S(1)} %shard_map.106.x_ref, bf16[512,8192]{1,0:T(8,128)(2,1)S(1)} %copy-done.4, ...), custom_call_target="tpu_custom_call" | custom-call | flops 536870912 | bytes 4194304 | tf_op jit(solution)/shard_map/pallas_call | solution.py:174
  219.9 3.3 %collective-permute-start.18 = (bf16[256,512]{1,0:T(8,128)(2,1)S(1)}, bf16[256,512]{1,0:T(8,128)(2,1)S(1)}, u32[]{:S(2)}, u32[]{:S(2)}) collective-permute-start(bf16[256,512]{1,0:T(8,128)(2,1)S(1)} %get-tuple-element.40), channel_id=1, source_target_pairs={{0,3},{1,0},{2,1},{3,2},{4,7},{5,4},{6,5},{7,6},{8,11},{9,8},{10,9... | collective-permute-start | bytes 786440 | tf_op jit(solution)/shard_map/ppermute | solution.py:41
  224.9 4.4 %collective-permute-done.18 = bf16[256,512]{1,0:T(8,128)(2,1)S(1)} collective-permute-done((bf16[256,512]{1,0:T(8,128)(2,1)S(1)}, bf16[256,512]{1,0:T(8,128)(2,1)S(1)}, u32[]{:S(2)}, u32[]{:S(2)}) %collective-permute-start.18) | collective-permute-done | bytes 262176 | tf_op jit(solution)/shard_map/ppermute | solution.py:41
  230.2 2.6 %collective-permute-done.20 = bf16[256,512]{1,0:T(8,128)(2,1)S(1)} collective-permute-done((bf16[256,512]{1,0:T(8,128)(2,1)S(1)}, bf16[256,512]{1,0:T(8,128)(2,1)S(1)}, u32[]{:S(2)}, u32[]{:S(2)}) %collective-permute-start.20) | collective-permute-done | bytes 262176 | tf_op jit(solution)/shard_map/ppermute | solution.py:41
  (132 shorter events, 20.2 us)
Async XLA Ops:
  0.6 19.5 %collective-permute-start.21 = (bf16[256,512]{1,0:T(8,128)(2,1)}, bf16[256,512]{1,0:T(8,128)(2,1)S(1)}, u32[]{:S(2)}, u32[]{:S(2)}) collective-permute-start(bf16[256,512]{1,0:T(8,128)(2,1)} %param.15), channel_id=1, source_target_pairs={{0,1},{1,2},{2,3},{3,0},{4,5},{5,6},{6,7},{7,4},{8,9},{9,10},{10,1... | collective-permute-start | bytes 786440 | tf_op jit(solution)/shard_map/ppermute | solution.py:41
  3.2 20.3 %collective-permute-start.22 = (bf16[256,512]{1,0:T(8,128)(2,1)}, bf16[256,512]{1,0:T(8,128)(2,1)S(1)}, u32[]{:S(2)}, u32[]{:S(2)}) collective-permute-start(bf16[256,512]{1,0:T(8,128)(2,1)} %param.15), channel_id=1, source_target_pairs={{0,2},{1,3},{2,0},{3,1},{4,6},{5,7},{6,4},{7,5},{8,10},{9,11},{10,... | collective-permute-start | bytes 786440 | tf_op jit(solution)/shard_map/ppermute | solution.py:41
  6.5 17.0 %collective-permute-start.23 = (bf16[256,512]{1,0:T(8,128)(2,1)}, bf16[256,512]{1,0:T(8,128)(2,1)S(1)}, u32[]{:S(2)}, u32[]{:S(2)}) collective-permute-start(bf16[256,512]{1,0:T(8,128)(2,1)} %param.15), channel_id=1, source_target_pairs={{0,3},{1,0},{2,1},{3,2},{4,7},{5,4},{6,5},{7,6},{8,11},{9,8},{10,9... | collective-permute-start | bytes 786440 | tf_op jit(solution)/shard_map/ppermute | solution.py:41
  7.2 26.9 %collective-permute-start = (bf16[256,512]{1,0:T(8,128)(2,1)}, bf16[256,512]{1,0:T(8,128)(2,1)S(1)}, u32[]{:S(2)}, u32[]{:S(2)}) collective-permute-start(bf16[256,512]{1,0:T(8,128)(2,1)} %param.8), channel_id=1, source_target_pairs={{0,1},{1,2},{2,3},{3,0},{4,5},{5,6},{6,7},{7,4},{8,9},{9,10},{10,1... | collective-permute-start | bytes 786440 | tf_op jit(solution)/shard_map/ppermute | solution.py:41
  7.9 27.6 %collective-permute-start.1 = (bf16[256,512]{1,0:T(8,128)(2,1)}, bf16[256,512]{1,0:T(8,128)(2,1)S(1)}, u32[]{:S(2)}, u32[]{:S(2)}) collective-permute-start(bf16[256,512]{1,0:T(8,128)(2,1)} %param.8), channel_id=1, source_target_pairs={{0,2},{1,3},{2,0},{3,1},{4,6},{5,7},{6,4},{7,5},{8,10},{9,11},{10,... | collective-permute-start | bytes 786440 | tf_op jit(solution)/shard_map/ppermute | solution.py:41
  8.4 29.3 %copy-start.10 = (bf16[256,512]{1,0:T(8,128)(2,1)S(1)}, bf16[256,512]{1,0:T(8,128)(2,1)}, u32[]{:S(2)}) copy-start(bf16[256,512]{1,0:T(8,128)(2,1)} %param.8) | copy-start | bytes 786436
  8.4 24.9 %all-to-all-start = ((bf16[128,8,256]{2,1,0:T(8,128)(2,1)}), bf16[128,8,256]{2,1,0:T(8,128)(2,1)S(1)}, u32[]{:S(2)}, u32[]{:S(2)}) async-start(bf16[128,8,256]{2,1,0:T(8,128)(2,1)} %bitcast.128), calls=%async_computation | async-start | bytes 1048576 | tf_op jit(solution)/shard_map/all_to_all | solution.py:359
  20.1 17.3 %collective-permute-start.2 = (bf16[256,512]{1,0:T(8,128)(2,1)}, bf16[256,512]{1,0:T(8,128)(2,1)S(1)}, u32[]{:S(2)}, u32[]{:S(2)}) collective-permute-start(bf16[256,512]{1,0:T(8,128)(2,1)} %param.8), channel_id=1, source_target_pairs={{0,3},{1,0},{2,1},{3,2},{4,7},{5,4},{6,5},{7,6},{8,11},{9,8},{10,9... | collective-permute-start | bytes 786440 | tf_op jit(solution)/shard_map/ppermute | solution.py:41
  24.6 41.1 %collective-permute-start.24 = (bf16[4,256,512]{2,1,0:T(8,128)(2,1)S(1)}, bf16[4,256,512]{2,1,0:T(8,128)(2,1)}, u32[]{:S(2)}, u32[]{:S(2)}) collective-permute-start(bf16[4,256,512]{2,1,0:T(8,128)(2,1)S(1)} %pad_maximum_fusion.2.refs_0_), channel_id=1, source_target_pairs={{0,4},{1,5},{2,6},{3,7},{4,8},{5,9},{6,10},{7,11},{8,12},{9,13},{1... | collective-permute-start | bytes 3145736 | tf_op jit(solution)/shard_map/ppermute | solution.py:45
  33.9 10.9 %collective-permute-start.7 = (bf16[64,2048]{1,0:T(8,128)(2,1)S(1)}, bf16[64,2048]{1,0:T(8,128)(2,1)S(1)}, u32[]{:S(2)}, u32[]{:S(2)}) collective-permute-start(bf16[64,2048]{1,0:T(8,128)(2,1)S(1)} %bitcast.124), channel_id=1, source_target_pairs={{0,1},{1,2},{2,3},{3,0},{4,5},{5,6},{6,7},{7,4},{8,9},{9,10},{10,1... | collective-permute-start | bytes 786440 | tf_op jit(solution)/shard_map/ppermute | solution.py:41
  34.1 13.7 %collective-permute-start.8 = (bf16[64,2048]{1,0:T(8,128)(2,1)S(1)}, bf16[64,2048]{1,0:T(8,128)(2,1)S(1)}, u32[]{:S(2)}, u32[]{:S(2)}) collective-permute-start(bf16[64,2048]{1,0:T(8,128)(2,1)S(1)} %bitcast.125), channel_id=1, source_target_pairs={{0,2},{1,3},{2,0},{3,1},{4,6},{5,7},{6,4},{7,5},{8,10},{9,11},{10,... | collective-permute-start | bytes 786440 | tf_op jit(solution)/shard_map/ppermute | solution.py:41
  35.6 12.8 %collective-permute-start.9 = (bf16[64,2048]{1,0:T(8,128)(2,1)S(1)}, bf16[64,2048]{1,0:T(8,128)(2,1)S(1)}, u32[]{:S(2)}, u32[]{:S(2)}) collective-permute-start(bf16[64,2048]{1,0:T(8,128)(2,1)S(1)} %bitcast.126), channel_id=1, source_target_pairs={{0,3},{1,0},{2,1},{3,2},{4,7},{5,4},{6,5},{7,6},{8,11},{9,8},{10,9... | collective-permute-start | bytes 786440 | tf_op jit(solution)/shard_map/ppermute | solution.py:41
  37.4 33.1 %collective-permute-start.26 = (bf16[4,256,512]{2,1,0:T(8,128)(2,1)S(1)}, bf16[4,256,512]{2,1,0:T(8,128)(2,1)}, u32[]{:S(2)}, u32[]{:S(2)}) collective-permute-start(bf16[4,256,512]{2,1,0:T(8,128)(2,1)S(1)} %pad_maximum_fusion.2.refs_0_), channel_id=1, source_target_pairs={{0,12},{1,13},{2,14},{3,15},{4,0},{5,1},{6,2},{7,3},{8,4},{9,5},{1... | collective-permute-start | bytes 3145736 | tf_op jit(solution)/shard_map/ppermute | solution.py:45
  44.8 26.9 %collective-permute-start.3 = (bf16[4,256,512]{2,1,0:T(8,128)(2,1)}, bf16[4,256,512]{2,1,0:T(8,128)(2,1)}, u32[]{:S(2)}, u32[]{:S(2)}) collective-permute-start(bf16[4,256,512]{2,1,0:T(8,128)(2,1)} %pad_maximum_fusion.refs_0_), channel_id=1, source_target_pairs={{0,4},{1,5},{2,6},{3,7},{4,8},{5,9},{6,10},{7,11},{8,12},{9,13},{1... | collective-permute-start | bytes 3145736 | tf_op jit(solution)/shard_map/ppermute | solution.py:45
  47.8 27.7 %collective-permute-start.5 = (bf16[4,256,512]{2,1,0:T(8,128)(2,1)}, bf16[4,256,512]{2,1,0:T(8,128)(2,1)}, u32[]{:S(2)}, u32[]{:S(2)}) collective-permute-start(bf16[4,256,512]{2,1,0:T(8,128)(2,1)} %pad_maximum_fusion.refs_0_), channel_id=1, source_target_pairs={{0,12},{1,13},{2,14},{3,15},{4,0},{5,1},{6,2},{7,3},{8,4},{9,5},{1... | collective-permute-start | bytes 3145736 | tf_op jit(solution)/shard_map/ppermute | solution.py:45
  49.5 36.2 %collective-permute-start.10 = (bf16[4,64,2048]{2,1,0:T(8,128)(2,1)}, bf16[4,64,2048]{2,1,0:T(8,128)(2,1)}, u32[]{:S(2)}, u32[]{:S(2)}) collective-permute-start(bf16[4,64,2048]{2,1,0:T(8,128)(2,1)} %pad_maximum_fusion.1), channel_id=1, source_target_pairs={{0,4},{1,5},{2,6},{3,7},{4,8},{5,9},{6,10},{7,11},{8,12},{9,13},{1... | collective-permute-start | bytes 3145736 | tf_op jit(solution)/shard_map/ppermute | solution.py:45
  50.8 3.4 %copy-start.2 = (bf16[512,8192]{1,0:T(8,128)(2,1)S(1)}, bf16[512,8192]{1,0:T(8,128)(2,1)}, u32[]{:S(2)}) copy-start(bf16[512,8192]{1,0:T(8,128)(2,1)} %refs_3_.7) | copy-start | bytes 25165828
  56.4 3.4 %copy-start = (bf16[8192,512]{1,0:T(8,128)(2,1)S(1)}, bf16[8192,512]{1,0:T(8,128)(2,1)}, u32[]{:S(2)}) copy-start(bf16[8192,512]{1,0:T(8,128)(2,1)} %w_ref.3) | copy-start | bytes 25165828
  59.8 3.8 %copy-start.5 = (bf16[2048,512]{1,0:T(8,128)(2,1)S(1)}, bf16[2048,512]{1,0:T(8,128)(2,1)}, u32[]{:S(2)}) copy-start(bf16[2048,512]{1,0:T(8,128)(2,1)} %wk_ref.7) | copy-start | bytes 6291460
  59.8 17.1 %slice-start.2 = ((s8[8388608]{0:T(1024)(128)(4,1)}), s8[4194304]{0:T(1024)(128)(4,1)S(1)}, s32[]{:S(2)}) async-start(s8[8388608]{0:T(1024)(128)(4,1)} %bitcast.85), calls=%async_computation.4 | async-start | bytes 8388608
  63.5 4.0 %copy-start.6 = (bf16[2048,512]{1,0:T(8,128)(2,1)S(1)}, bf16[2048,512]{1,0:T(8,128)(2,1)}, u32[]{:S(2)}) copy-start(bf16[2048,512]{1,0:T(8,128)(2,1)} %wv_ref.7) | copy-start | bytes 6291460
  63.6 13.3 %slice-start.3 = ((s8[8388608]{0:T(1024)(128)(4,1)}), s8[4194304]{0:T(1024)(128)(4,1)S(1)}, s32[]{:S(2)}) async-start(s8[8388608]{0:T(1024)(128)(4,1)} %bitcast.85), calls=%async_computation.5 | async-start | bytes 8388608
  65.7 27.8 %collective-permute-start.12 = (bf16[4,64,2048]{2,1,0:T(8,128)(2,1)}, bf16[4,64,2048]{2,1,0:T(8,128)(2,1)S(1)}, u32[]{:S(2)}, u32[]{:S(2)}) collective-permute-start(bf16[4,64,2048]{2,1,0:T(8,128)(2,1)} %pad_maximum_fusion.1), channel_id=1, source_target_pairs={{0,12},{1,13},{2,14},{3,15},{4,0},{5,1},{6,2},{7,3},{8,4},{9,5},{1... | collective-permute-start | bytes 3145736 | tf_op jit(solution)/shard_map/ppermute | solution.py:45
  70.6 24.6 %collective-permute-start.25 = (bf16[2,256,512]{2,1,0:T(8,128)(2,1)S(1)}, bf16[2,256,512]{2,1,0:T(8,128)(2,1)S(1)}, u32[]{:S(2)}, u32[]{:S(2)}) collective-permute-start(bf16[2,256,512]{2,1,0:T(8,128)(2,1)S(1)} %slice.57), channel_id=1, source_target_pairs={{0,4},{1,5},{2,6},{3,7},{4,8},{5,9},{6,10},{7,11},{8,12},{9,13},{1... | collective-permute-start | bytes 1572872 | tf_op jit(solution)/shard_map/ppermute | solution.py:45
  71.8 26.2 %collective-permute-start.27 = (bf16[2,256,512]{2,1,0:T(8,128)(2,1)S(1)}, bf16[2,256,512]{2,1,0:T(8,128)(2,1)S(1)}, u32[]{:S(2)}, u32[]{:S(2)}) collective-permute-start(bf16[2,256,512]{2,1,0:T(8,128)(2,1)S(1)} %slice.58), channel_id=1, source_target_pairs={{0,12},{1,13},{2,14},{3,15},{4,0},{5,1},{6,2},{7,3},{8,4},{9,5},{1... | collective-permute-start | bytes 1572872 | tf_op jit(solution)/shard_map/ppermute | solution.py:45
  75.6 24.2 %collective-permute-start.4 = (bf16[2,256,512]{2,1,0:T(8,128)(2,1)S(1)}, bf16[2,256,512]{2,1,0:T(8,128)(2,1)S(1)}, u32[]{:S(2)}, u32[]{:S(2)}) collective-permute-start(bf16[2,256,512]{2,1,0:T(8,128)(2,1)S(1)} %slice.53), channel_id=1, source_target_pairs={{0,4},{1,5},{2,6},{3,7},{4,8},{5,9},{6,10},{7,11},{8,12},{9,13},{1... | collective-permute-start | bytes 1572872 | tf_op jit(solution)/shard_map/ppermute | solution.py:45
  75.7 6.0 %slice-start = ((s8[8388608]{0:T(1024)(128)(4,1)}), s8[4194304]{0:T(1024)(128)(4,1)S(1)}, s32[]{:S(2)}) async-start(s8[8388608]{0:T(1024)(128)(4,1)} %bitcast.83), calls=%async_computation.2 | async-start | bytes 8388608
  76.9 4.7 %slice-start.1 = ((s8[8388608]{0:T(1024)(128)(4,1)}), s8[4194304]{0:T(1024)(128)(4,1)S(1)}, s32[]{:S(2)}) async-start(s8[8388608]{0:T(1024)(128)(4,1)} %bitcast.83), calls=%async_computation.3 | async-start | bytes 8388608
  85.7 14.0 %collective-permute-start.6 = (bf16[2,256,512]{2,1,0:T(8,128)(2,1)S(1)}, bf16[2,256,512]{2,1,0:T(8,128)(2,1)S(1)}, u32[]{:S(2)}, u32[]{:S(2)}) collective-permute-start(bf16[2,256,512]{2,1,0:T(8,128)(2,1)S(1)} %slice.54), channel_id=1, source_target_pairs={{0,12},{1,13},{2,14},{3,15},{4,0},{5,1},{6,2},{7,3},{8,4},{9,5},{1... | collective-permute-start | bytes 1572872 | tf_op jit(solution)/shard_map/ppermute | solution.py:45
  93.4 9.8 %collective-permute-start.11 = (bf16[2,64,2048]{2,1,0:T(8,128)(2,1)S(1)}, bf16[2,64,2048]{2,1,0:T(8,128)(2,1)S(1)}, u32[]{:S(2)}, u32[]{:S(2)}) collective-permute-start(bf16[2,64,2048]{2,1,0:T(8,128)(2,1)S(1)} %slice.55), channel_id=1, source_target_pairs={{0,4},{1,5},{2,6},{3,7},{4,8},{5,9},{6,10},{7,11},{8,12},{9,13},{1... | collective-permute-start | bytes 1572872 | tf_op jit(solution)/shard_map/ppermute | solution.py:45
  95.2 9.0 %collective-permute-start.13 = (bf16[2,64,2048]{2,1,0:T(8,128)(2,1)S(1)}, bf16[2,64,2048]{2,1,0:T(8,128)(2,1)S(1)}, u32[]{:S(2)}, u32[]{:S(2)}) collective-permute-start(bf16[2,64,2048]{2,1,0:T(8,128)(2,1)S(1)} %slice.56), channel_id=1, source_target_pairs={{0,12},{1,13},{2,14},{3,15},{4,0},{5,1},{6,2},{7,3},{8,4},{9,5},{1... | collective-permute-start | bytes 1572872 | tf_op jit(solution)/shard_map/ppermute | solution.py:45
  113.8 2.0 copy-start.8
  115.8 16.0 %collective-permute-start.37 = (bf16[128,2048]{1,0:T(8,128)(2,1)S(1)}, bf16[128,2048]{1,0:T(8,128)(2,1)S(1)}, u32[]{:S(2)}, u32[]{:S(2)}) collective-permute-start(bf16[128,2048]{1,0:T(8,128)(2,1)S(1)} %get-tuple-element.62), channel_id=1, source_target_pairs={{0,12},{1,13},{2,14},{3,15},{4,0},{5,1},{6,2},{7,3},{8,4},{9,5},{1... | collective-permute-start | bytes 1572872 | tf_op jit(solution)/shard_map/ppermute | solution.py:45
  119.2 18.3 %collective-permute-start.35 = (bf16[128,2048]{1,0:T(8,128)(2,1)S(1)}, bf16[128,2048]{1,0:T(8,128)(2,1)S(1)}, u32[]{:S(2)}, u32[]{:S(2)}) collective-permute-start(bf16[128,2048]{1,0:T(8,128)(2,1)S(1)} %get-tuple-element.59), channel_id=1, source_target_pairs={{0,4},{1,5},{2,6},{3,7},{4,8},{5,9},{6,10},{7,11},{8,12},{9,13},{1... | collective-permute-start | bytes 1572872 | tf_op jit(solution)/shard_map/ppermute | solution.py:45
  120.7 19.7 %collective-permute-start.28 = (bf16[2,256,512]{2,1,0:T(8,128)(2,1)S(1)}, bf16[2,256,512]{2,1,0:T(8,128)(2,1)S(1)}, u32[]{:S(2)}, u32[]{:S(2)}) collective-permute-start(bf16[2,256,512]{2,1,0:T(8,128)(2,1)S(1)} %get-tuple-element.44), channel_id=1, source_target_pairs={{0,4},{1,5},{2,6},{3,7},{4,8},{5,9},{6,10},{7,11},{8,12},{9,13},{1... | collective-permute-start | bytes 1572872 | tf_op jit(solution)/shard_map/ppermute | solution.py:45
  120.8 19.6 %collective-permute-start.29 = (bf16[2,256,512]{2,1,0:T(8,128)(2,1)S(1)}, bf16[2,256,512]{2,1,0:T(8,128)(2,1)S(1)}, u32[]{:S(2)}, u32[]{:S(2)}) collective-permute-start(bf16[2,256,512]{2,1,0:T(8,128)(2,1)S(1)} %get-tuple-element.45), channel_id=1, source_target_pairs={{0,12},{1,13},{2,14},{3,15},{4,0},{5,1},{6,2},{7,3},{8,4},{9,5},{1... | collective-permute-start | bytes 1572872 | tf_op jit(solution)/shard_map/ppermute | solution.py:45
  131.8 14.7 %collective-permute-start.14 = (bf16[2,256,512]{2,1,0:T(8,128)(2,1)S(1)}, bf16[2,256,512]{2,1,0:T(8,128)(2,1)S(1)}, u32[]{:S(2)}, u32[]{:S(2)}) collective-permute-start(bf16[2,256,512]{2,1,0:T(8,128)(2,1)S(1)} %get-tuple-element.35), channel_id=1, source_target_pairs={{0,4},{1,5},{2,6},{3,7},{4,8},{5,9},{6,10},{7,11},{8,12},{9,13},{1... | collective-permute-start | bytes 1572872 | tf_op jit(solution)/shard_map/ppermute | solution.py:45
  134.8 40.3 %collective-permute-start.38 = (bf16[256,2048]{1,0:T(8,128)(2,1)}, bf16[256,2048]{1,0:T(8,128)(2,1)}, u32[]{:S(2)}, u32[]{:S(2)}) collective-permute-start(bf16[256,2048]{1,0:T(8,128)(2,1)} %shard_map.119), channel_id=1, source_target_pairs={{0,12},{1,13},{2,14},{3,15},{4,0},{5,1},{6,2},{7,3},{8,4},{9,5},{1... | collective-permute-start | bytes 3145736 | tf_op jit(solution)/shard_map/ppermute | solution.py:45
  140.4 37.9 %collective-permute-start.36 = (bf16[256,2048]{1,0:T(8,128)(2,1)}, bf16[256,2048]{1,0:T(8,128)(2,1)}, u32[]{:S(2)}, u32[]{:S(2)}) collective-permute-start(bf16[256,2048]{1,0:T(8,128)(2,1)} %shard_map.118), channel_id=1, source_target_pairs={{0,4},{1,5},{2,6},{3,7},{4,8},{5,9},{6,10},{7,11},{8,12},{9,13},{1... | collective-permute-start | bytes 3145736 | tf_op jit(solution)/shard_map/ppermute | solution.py:45
  143.8 39.8 %collective-permute-start.30 = (bf16[4,256,512]{2,1,0:T(8,128)(2,1)}, bf16[4,256,512]{2,1,0:T(8,128)(2,1)}, u32[]{:S(2)}, u32[]{:S(2)}) collective-permute-start(bf16[4,256,512]{2,1,0:T(8,128)(2,1)} %get-tuple-element.46), channel_id=1, source_target_pairs={{0,4},{1,5},{2,6},{3,7},{4,8},{5,9},{6,10},{7,11},{8,12},{9,13},{1... | collective-permute-start | bytes 3145736 | tf_op jit(solution)/shard_map/ppermute | solution.py:45
  143.8 39.8 %collective-permute-start.31 = (bf16[4,256,512]{2,1,0:T(8,128)(2,1)}, bf16[4,256,512]{2,1,0:T(8,128)(2,1)}, u32[]{:S(2)}, u32[]{:S(2)}) collective-permute-start(bf16[4,256,512]{2,1,0:T(8,128)(2,1)} %get-tuple-element.47), channel_id=1, source_target_pairs={{0,12},{1,13},{2,14},{3,15},{4,0},{5,1},{6,2},{7,3},{8,4},{9,5},{1... | collective-permute-start | bytes 3145736 | tf_op jit(solution)/shard_map/ppermute | solution.py:45
  146.5 19.8 %collective-permute-start.15 = (bf16[2,256,512]{2,1,0:T(8,128)(2,1)}, bf16[2,256,512]{2,1,0:T(8,128)(2,1)}, u32[]{:S(2)}, u32[]{:S(2)}) collective-permute-start(bf16[2,256,512]{2,1,0:T(8,128)(2,1)} %get-tuple-element.36), channel_id=1, source_target_pairs={{0,12},{1,13},{2,14},{3,15},{4,0},{5,1},{6,2},{7,3},{8,4},{9,5},{1... | collective-permute-start | bytes 1572872 | tf_op jit(solution)/shard_map/ppermute | solution.py:45
  166.3 3.4 %copy-start.3 = (bf16[512,8192]{1,0:T(8,128)(2,1)S(1)}, bf16[512,8192]{1,0:T(8,128)(2,1)}, u32[]{:S(2)}) copy-start(bf16[512,8192]{1,0:T(8,128)(2,1)} %refs_3_.7) | copy-start | bytes 25165828
  169.7 8.5 %copy-start.7 = (bf16[2048,512]{1,0:T(8,128)(2,1)S(1)}, bf16[2048,512]{1,0:T(8,128)(2,1)}, u32[]{:S(2)}) copy-start(bf16[2048,512]{1,0:T(8,128)(2,1)} %wv_ref.7) | copy-start | bytes 6291460
  169.7 8.5 %copy-start.9 = (bf16[4,4,16,512]{3,2,1,0:T(8,128)(2,1)S(1)}, bf16[4,4,16,512]{3,2,1,0:T(8,128)(2,1)}, u32[]{:S(2)}) copy-start(bf16[4,4,16,512]{3,2,1,0:T(8,128)(2,1)} %copy-done.8) | copy-start | bytes 786436
  174.7 37.9 %collective-permute-start.16 = (bf16[4,256,512]{2,1,0:T(8,128)(2,1)}, bf16[4,256,512]{2,1,0:T(8,128)(2,1)}, u32[]{:S(2)}, u32[]{:S(2)}) collective-permute-start(bf16[4,256,512]{2,1,0:T(8,128)(2,1)} %get-tuple-element.37), channel_id=1, source_target_pairs={{0,4},{1,5},{2,6},{3,7},{4,8},{5,9},{6,10},{7,11},{8,12},{9,13},{1... | collective-permute-start | bytes 3145736 | tf_op jit(solution)/shard_map/ppermute | solution.py:45
  175.1 37.6 %collective-permute-start.17 = (bf16[4,256,512]{2,1,0:T(8,128)(2,1)}, bf16[4,256,512]{2,1,0:T(8,128)(2,1)}, u32[]{:S(2)}, u32[]{:S(2)}) collective-permute-start(bf16[4,256,512]{2,1,0:T(8,128)(2,1)} %get-tuple-element.38), channel_id=1, source_target_pairs={{0,12},{1,13},{2,14},{3,15},{4,0},{5,1},{6,2},{7,3},{8,4},{9,5},{1... | collective-permute-start | bytes 3145736 | tf_op jit(solution)/shard_map/ppermute | solution.py:45
  182.7 9.0 %collective-permute-start.39 = (bf16[64,2048]{1,0:T(8,128)(2,1)}, bf16[64,2048]{1,0:T(8,128)(2,1)S(1)}, u32[]{:S(2)}, u32[]{:S(2)}) collective-permute-start(bf16[64,2048]{1,0:T(8,128)(2,1)} %get-tuple-element.64), channel_id=1, source_target_pairs={{0,3},{1,0},{2,1},{3,2},{4,7},{5,4},{6,5},{7,6},{8,11},{9,8},{10,9... | collective-permute-start | bytes 786440 | tf_op jit(solution)/shard_map/ppermute | solution.py:41
  183.6 10.4 %collective-permute-start.40 = (bf16[64,2048]{1,0:T(8,128)(2,1)}, bf16[64,2048]{1,0:T(8,128)(2,1)S(1)}, u32[]{:S(2)}, u32[]{:S(2)}) collective-permute-start(bf16[64,2048]{1,0:T(8,128)(2,1)} %get-tuple-element.65), channel_id=1, source_target_pairs={{0,2},{1,3},{2,0},{3,1},{4,6},{5,7},{6,4},{7,5},{8,10},{9,11},{10,... | collective-permute-start | bytes 786440 | tf_op jit(solution)/shard_map/ppermute | solution.py:41
  183.6 12.9 %collective-permute-start.41 = (bf16[64,2048]{1,0:T(8,128)(2,1)}, bf16[64,2048]{1,0:T(8,128)(2,1)S(1)}, u32[]{:S(2)}, u32[]{:S(2)}) collective-permute-start(bf16[64,2048]{1,0:T(8,128)(2,1)} %get-tuple-element.66), channel_id=1, source_target_pairs={{0,1},{1,2},{2,3},{3,0},{4,5},{5,6},{6,7},{7,4},{8,9},{9,10},{10,1... | collective-permute-start | bytes 786440 | tf_op jit(solution)/shard_map/ppermute | solution.py:41
  184.4 3.4 %copy-start.1 = (bf16[8192,512]{1,0:T(8,128)(2,1)S(1)}, bf16[8192,512]{1,0:T(8,128)(2,1)}, u32[]{:S(2)}) copy-start(bf16[8192,512]{1,0:T(8,128)(2,1)} %w_ref.3) | copy-start | bytes 25165828
  191.6 31.7 %collective-permute-start.32 = (bf16[256,512]{1,0:T(8,128)(2,1)S(1)}, bf16[256,512]{1,0:T(8,128)(2,1)S(1)}, u32[]{:S(2)}, u32[]{:S(2)}) collective-permute-start(bf16[256,512]{1,0:T(8,128)(2,1)S(1)} %get-tuple-element.49), channel_id=1, source_target_pairs={{0,3},{1,0},{2,1},{3,2},{4,7},{5,4},{6,5},{7,6},{8,11},{9,8},{10,9... | collective-permute-start | bytes 786440 | tf_op jit(solution)/shard_map/ppermute | solution.py:41
  194.0 30.1 %collective-permute-start.33 = (bf16[256,512]{1,0:T(8,128)(2,1)S(1)}, bf16[256,512]{1,0:T(8,128)(2,1)S(1)}, u32[]{:S(2)}, u32[]{:S(2)}) collective-permute-start(bf16[256,512]{1,0:T(8,128)(2,1)S(1)} %get-tuple-element.50), channel_id=1, source_target_pairs={{0,2},{1,3},{2,0},{3,1},{4,6},{5,7},{6,4},{7,5},{8,10},{9,11},{10,... | collective-permute-start | bytes 786440 | tf_op jit(solution)/shard_map/ppermute | solution.py:41
  196.4 27.7 %collective-permute-start.34 = (bf16[256,512]{1,0:T(8,128)(2,1)S(1)}, bf16[256,512]{1,0:T(8,128)(2,1)S(1)}, u32[]{:S(2)}, u32[]{:S(2)}) collective-permute-start(bf16[256,512]{1,0:T(8,128)(2,1)S(1)} %get-tuple-element.51), channel_id=1, source_target_pairs={{0,1},{1,2},{2,3},{3,0},{4,5},{5,6},{6,7},{7,4},{8,9},{9,10},{10,1... | collective-permute-start | bytes 786440 | tf_op jit(solution)/shard_map/ppermute | solution.py:41
  200.9 32.8 %all-to-all-start.1 = ((bf16[128,8,256]{2,1,0:T(8,128)(2,1)}), bf16[128,8,256]{2,1,0:T(8,128)(2,1)S(1)}, u32[]{:S(2)}, u32[]{:S(2)}) async-start(bf16[128,8,256]{2,1,0:T(8,128)(2,1)} %fusion), calls=%async_computation.1 | async-start | bytes 1048576 | tf_op jit(solution)/shard_map/all_to_all | solution.py:414
  212.6 3.4 %copy-start.4 = (bf16[512,8192]{1,0:T(8,128)(2,1)S(1)}, bf16[512,8192]{1,0:T(8,128)(2,1)}, u32[]{:S(2)}) copy-start(bf16[512,8192]{1,0:T(8,128)(2,1)} %refs_3_.7) | copy-start | bytes 25165828
  219.9 9.5 %collective-permute-start.18 = (bf16[256,512]{1,0:T(8,128)(2,1)S(1)}, bf16[256,512]{1,0:T(8,128)(2,1)S(1)}, u32[]{:S(2)}, u32[]{:S(2)}) collective-permute-start(bf16[256,512]{1,0:T(8,128)(2,1)S(1)} %get-tuple-element.40), channel_id=1, source_target_pairs={{0,3},{1,0},{2,1},{3,2},{4,7},{5,4},{6,5},{7,6},{8,11},{9,8},{10,9... | collective-permute-start | bytes 786440 | tf_op jit(solution)/shard_map/ppermute | solution.py:41
  223.2 7.0 %collective-permute-start.19 = (bf16[256,512]{1,0:T(8,128)(2,1)S(1)}, bf16[256,512]{1,0:T(8,128)(2,1)S(1)}, u32[]{:S(2)}, u32[]{:S(2)}) collective-permute-start(bf16[256,512]{1,0:T(8,128)(2,1)S(1)} %get-tuple-element.41), channel_id=1, source_target_pairs={{0,2},{1,3},{2,0},{3,1},{4,6},{5,7},{6,4},{7,5},{8,10},{9,11},{10,... | collective-permute-start | bytes 786440 | tf_op jit(solution)/shard_map/ppermute | solution.py:41
  223.3 9.5 %collective-permute-start.20 = (bf16[256,512]{1,0:T(8,128)(2,1)S(1)}, bf16[256,512]{1,0:T(8,128)(2,1)S(1)}, u32[]{:S(2)}, u32[]{:S(2)}) collective-permute-start(bf16[256,512]{1,0:T(8,128)(2,1)S(1)} %get-tuple-element.42), channel_id=1, source_target_pairs={{0,1},{1,2},{2,3},{3,0},{4,5},{5,6},{6,7},{7,4},{8,9},{9,10},{10,1... | collective-permute-start | bytes 786440 | tf_op jit(solution)/shard_map/ppermute | solution.py:41

commit v2 on v0

v2 whole, which is shorter than its diff:
```python
import functools

import jax
import jax.numpy as jnp
from jax import lax
from jax.experimental import pallas as pl
from jax.experimental.pallas import tpu as pltpu
from jax.sharding import PartitionSpec as P

HEAD = 128
SPAN = 64
SEQ = 8
SIDE = 4
ENC = SIDE * SIDE
BF = jnp.bfloat16
F32 = jnp.float32
AXES = ("seq", "enc")
MIB = 1024 * 1024
NT = (((1,), (1,)), ((), ()))
NN = (((1,), (0,)), ((), ()))
TN = (((0,), (0,)), ((), ()))


def dot(a, b, dims):
    return lax.dot_general(a, b, dims, preferred_element_type=F32)


def shift_table(long_phase, shift):
    pairs = []
    for seq in range(SEQ):
        for z in range(SIDE):
            for x in range(SIDE):
                if (seq % 2 == 0) == long_phase:
                    to_z, to_x = (z + shift) % SIDE, x
                else:
                    to_z, to_x = z, (x + shift) % SIDE
                pairs.append((seq * ENC + z * SIDE + x, seq * ENC + to_z * SIDE + to_x))
    return pairs


def move_u(value, shift):
    return lax.ppermute(value, AXES, shift_table(False, shift))


def move_v(value, shift):
    return lax.ppermute(value, AXES, shift_table(True, shift))


def relative_index():
    seq, enc = lax.axis_index("seq"), lax.axis_index("enc")
    z, x = enc // SIDE, enc % SIDE
    even = seq % 2 == 0
    u, v = jnp.where(even, x, z), jnp.where(even, z, x)
    k = lax.broadcasted_iota(jnp.int32, (SIDE, SIDE), 0)
    j = lax.broadcasted_iota(jnp.int32, (SIDE, SIDE), 1)
    uu, vv = (u - j) % SIDE, (v - k) % SIDE
    return jnp.where(even, vv * SIDE + uu, uu * SIDE + vv).astype(jnp.int32)


def after(value, *others):
    return lax.optimization_barrier((value, *others))[0]


def stack_kernel(*refs):
    for n, ref in enumerate(refs[:-1]):
        refs[-1][n] = ref[...]


def stack(values):
    return pl.pallas_call(
        stack_kernel,
        out_shape=jax.ShapeDtypeStruct((len(values),) + values[0].shape, BF),
        in_specs=[pl.BlockSpec(memory_space=pltpu.VMEM)] * len(values),
        out_specs=pl.BlockSpec(memory_space=pltpu.VMEM),
        compiler_params=params(4),
        cost_estimate=cost(0, 4 * len(values) * values[0].size),
    )(*values)


def halves_kernel(one_ref, three_ref, low_ref, high_ref):
    low_ref[...] = one_ref[:2]
    high_ref[...] = three_ref[2:]


def halves(one, three):
    half = jax.ShapeDtypeStruct((2,) + one.shape[1:], BF)
    return pl.pallas_call(
        halves_kernel,
        out_shape=[half, half],
        in_specs=[pl.BlockSpec(memory_space=pltpu.VMEM)] * 2,
        out_specs=[pl.BlockSpec(memory_space=pltpu.VMEM)] * 2,
        compiler_params=params(4),
        cost_estimate=cost(0, 4 * one.size),
    )(one, three)


def gather_short(own):
    return [own, move_u(own, 1), move_u(own, 2), move_u(own, -1)]


def gather_long(group):
    return [move_v(group, 1), move_v(group, -1)]


def gather_last(side, *others):
    low, high = halves(*side)
    return [move_v(after(low, *others), 1), move_v(after(high, *others), -1)]


def params(mib):
    return pltpu.CompilerParams(vmem_limit_bytes=mib * MIB)


def in_vmem(count):
    return [pl.BlockSpec(memory_space=pltpu.VMEM)] * count


def cost(flops, bytes_accessed, transcendentals=0):
    return pl.CostEstimate(flops=flops, bytes_accessed=bytes_accessed, transcendentals=transcendentals)


DEPTH = 4


class Stream:
    def __init__(self, index_ref, count, query_ref, output_ref, scratch):
        self.index_ref, self.count = index_ref, count
        self.refs = (query_ref, output_ref)
        self.buffers, self.sems = scratch[:2], scratch[2:]
        for n in range(min(DEPTH - 1, count)):
            self.start(n)

    def copy(self, n, side):
        width = self.buffers[0].shape[1]
        at = pl.ds(pl.multiple_of(self.index_ref[n] * width, width), width)
        source = self.refs[0].at[at, :] if side == 0 else self.refs[1].at[:, at]
        slot = n % DEPTH
        return pltpu.make_async_copy(source, self.buffers[side].at[slot], self.sems[side].at[slot])

    def start(self, n):
        self.copy(n, 0).start()
        self.copy(n, 1).start()

    def blocks(self):
        for n in range(self.count):
            if n + DEPTH - 1 < self.count:
                self.start(n + DEPTH - 1)
            self.copy(n, 0).wait()
            self.copy(n, 1).wait()
            yield n, self.buffers[0].at[n % DEPTH], self.buffers[1].at[n % DEPTH]


def stream_scratch(width):
    return [
        pltpu.VMEM((DEPTH, width, width), BF),
        pltpu.VMEM((DEPTH, width, width), BF),
        pltpu.SemaphoreType.DMA((DEPTH,)),
        pltpu.SemaphoreType.DMA((DEPTH,)),
    ]


def in_hbm(count):
    return [pl.BlockSpec(memory_space=pltpu.HBM)] * count


def kept(*weights):
    return [pltpu.with_memory_space_constraint(weight, pltpu.HBM) for weight in weights]


def gathered_kernel(counts, has_start, index_ref, query_ref, output_ref, *refs):
    x_refs, refs = refs[: len(counts)], refs[len(counts) :]
    start_refs, refs = (refs[:2], refs[2:]) if has_start else (None, refs)
    (q_ref, d_ref), scratch = refs[:2], refs[2:]
    chunks = [x_ref.at[n] for count, x_ref in zip(counts, x_refs) for n in range(count)]
    q = start_refs[0][...] if has_start else None
    d = start_refs[1][...] if has_start else None
    for n, query_block, output_block in Stream(index_ref, len(chunks), query_ref, output_ref, scratch).blocks():
        term = dot(chunks[n][0], query_block[...], NN)
        q = term if q is None else q + term
        term = dot(chunks[n][1], output_block[...], NT)
        d = term if d is None else d + term
    q_ref[...] = q.astype(q_ref.dtype)
    d_ref[...] = d.astype(d_ref.dtype)


def gathered_dots(index, parts, query_weight, output_weight, start, out_type):
    rows, width = parts[0].shape[2:]
    cols = query_weight.shape[1]
    counts = [part.shape[0] for part in parts]
    count = sum(counts)
    return pl.pallas_call(
        functools.partial(gathered_kernel, counts, start is not None),
        out_shape=[jax.ShapeDtypeStruct((rows, cols), out_type)] * 2,
        in_specs=[pl.BlockSpec(memory_space=pltpu.SMEM)]
        + in_hbm(2)
        + in_vmem(len(parts) + (0 if start is None else 2)),
        out_specs=in_vmem(2),
        scratch_shapes=stream_scratch(width),
        compiler_params=params(10),
        cost_estimate=cost(4 * count * rows * width * cols, 4 * count * (rows + cols) * width),
    )(index, *kept(query_weight, output_weight), *parts, *([] if start is None else start))


def far_kernel(index_ref, query_ref, output_ref, c_ref, d_ref, low_ref, high_ref, *scratch):
    for n, query_block, output_block in Stream(index_ref, 4, query_ref, output_ref, scratch).blocks():
        out_ref = low_ref if n < 2 else high_ref
        out_ref[n % 2, 0] = dot(c_ref[...], output_block[...], NN).astype(BF)
        out_ref[n % 2, 1] = dot(d_ref[...], query_block[...], NT).astype(BF)


def side_kernel(index_ref, query_ref, output_ref, c_ref, d_ref, a_ref, b_ref, g3_ref, g1_ref, *scratch):
    for n, query_block, output_block in Stream(index_ref, 8, query_ref, output_ref, scratch).blocks():
        j = n % 4
        out_ref = g3_ref if n < 4 else g1_ref
        part_ref = None
        if n < 4 and j < 2:
            part_ref = a_ref.at[j]
        elif n >= 4 and j >= 2:
            part_ref = b_ref.at[j - 2]
        value = dot(c_ref[...], output_block[...], NN)
        if part_ref is not None:
            value = value + part_ref[0].astype(F32)
        out_ref[j, 0] = value.astype(BF)
        value = dot(d_ref[...], query_block[...], NT)
        if part_ref is not None:
            value = value + part_ref[1].astype(F32)
        out_ref[j, 1] = value.astype(BF)


def near_kernel(index_ref, query_ref, output_ref, c_ref, d_ref, r3_ref, r1_ref, *refs):
    t_refs, scratch = refs[:4], refs[4:]
    for n, query_block, output_block in Stream(index_ref, 4, query_ref, output_ref, scratch).blocks():
        value = dot(c_ref[...], output_block[...], NN)
        t_refs[n][0] = (value + r3_ref[n, 0].astype(F32) + r1_ref[n, 0].astype(F32)).astype(BF)
        value = dot(d_ref[...], query_block[...], NT)
        t_refs[n][1] = (value + r3_ref[n, 1].astype(F32) + r1_ref[n, 1].astype(F32)).astype(BF)


def scatter_sums(index, context, d_queries, query_weight, output_weight, *others):
    rows, inner = context.shape
    width = query_weight.shape[0] // ENC

    def call(kernel, place, extra, out_blocks):
        count = place.shape[0]
        return pl.pallas_call(
            kernel,
            out_shape=[jax.ShapeDtypeStruct(block + (2, rows, width), BF) for block in out_blocks],
            in_specs=[pl.BlockSpec(memory_space=pltpu.SMEM)] + in_hbm(2) + in_vmem(2 + len(extra)),
            out_specs=in_vmem(len(out_blocks)),
            scratch_shapes=stream_scratch(width),
            compiler_params=params(10),
            cost_estimate=cost(4 * count * rows * inner * width, 4 * count * (2 * rows + inner) * width),
        )(place, *kept(query_weight, output_weight), context, d_queries, *extra)

    context = after(context, *others)
    far_low, far_high = call(far_kernel, index[2], [], [(2,), (2,)])
    from_low, from_high = move_v(far_low, 1), move_v(far_high, -1)
    g3, g1 = call(
        side_kernel, jnp.concatenate([index[3], index[1]]), [from_low, from_high], [(4,), (4,)]
    )
    r3, r1 = move_v(g3, 1), move_v(g1, -1)
    pieces = call(near_kernel, index[0], [r3, r1], [()] * 4)
    total = scatter_short(pieces)
    return total[0], total[1], pieces


def scatter_short(pieces, *others):
    t0, t1, t2, t3 = pieces
    q1, q2, q3 = move_u(t1, -1), move_u(t2, 2), move_u(t3, 1)
    t0 = after(t0, *others)
    total = t0.astype(F32) + q1.astype(F32) + q2.astype(F32) + q3.astype(F32)
    return total.astype(BF)


def project_kernel(pairs, key_ref, value_ref, *refs):
    x_refs, (k_ref, v_ref) = refs[:pairs], refs[pairs:]
    x = jnp.concatenate([ref[...].reshape(-1, ref.shape[-1]) for ref in x_refs], axis=0)
    k_ref[...] = dot(x, key_ref[...], NN).astype(BF)
    v_ref[...] = dot(x, value_ref[...], NN).astype(BF)


def project(pairs, key_weight, value_weight):
    features, cols = key_weight.shape
    rows = sum(pair.shape[0] * pair.shape[1] for pair in pairs)
    return pl.pallas_call(
        functools.partial(project_kernel, len(pairs)),
        out_shape=[jax.ShapeDtypeStruct((rows, cols), BF)] * 2,
        in_specs=in_vmem(2 + len(pairs)),
        out_specs=in_vmem(2),
        compiler_params=params(8),
        cost_estimate=cost(4 * rows * features * cols, 4 * (rows + cols) * features),
    )(key_weight, value_weight, *pairs)


def pair_kernel(places, groups, key_ref, value_ref, *refs):
    count = 2 * groups
    d_refs, refs = refs[:count], refs[count:]
    extra_refs, out_refs = refs[: len(places)], refs[len(places) :]
    tile = key_ref.shape[1]
    rows = d_refs[0].shape[0]
    per_group = len(out_refs) // groups
    each = rows // per_group
    for n in range(key_ref.shape[0] // tile):
        cols = slice(n * tile, (n + 1) * tile)
        for g in range(groups):
            total = dot(d_refs[2 * g][...], key_ref[cols, :], NT)
            total = total + dot(d_refs[2 * g + 1][...], value_ref[cols, :], NT)
            for (group, first, size), extra_ref in zip(places, extra_refs):
                if group != g:
                    continue
                part = extra_ref[:, cols].astype(F32)
                if size < rows:
                    zero = jnp.zeros((rows - size, tile), F32)
                    part = jnp.concatenate([zero, part] if first else [part, zero], axis=0)
                total = total + part
            for m in range(per_group):
                out_refs[g * per_group + m][:, cols] = total[m * each : (m + 1) * each].astype(BF)


def pair_dots(grads, key_weight, value_weight, extra, places, per_group):
    groups = len(grads) // 2
    rows, inner = grads[0].shape
    features = key_weight.shape[0]
    return pl.pallas_call(
        functools.partial(pair_kernel, places, groups),
        out_shape=[jax.ShapeDtypeStruct((rows // per_group, features), BF)] * (groups * per_group),
        in_specs=in_vmem(2 + len(grads) + len(extra)),
        out_specs=in_vmem(groups * per_group),
        compiler_params=params(8),
        cost_estimate=cost(4 * groups * rows * inner * features, 4 * (groups * rows + inner) * features),
    )(key_weight, value_weight, *grads, *extra)


def attention_kernel(chunks, q_ref, d_ref, *refs):
    parts = len(chunks)
    keys, values = refs[:parts], refs[parts : 2 * parts]
    context_ref, dq_ref = refs[2 * parts : 2 * parts + 2]
    dk_refs, dv_refs = refs[2 * parts + 2 : 2 * parts + 6], refs[2 * parts + 6 :]
    scale = HEAD ** (-0.5)
    spans = q_ref.shape[0] // SPAN
    own = 256 // ENC
    places = [(part, n * spans * own) for part, count in enumerate(chunks) for n in range(count)]

    def span_rows(refs, c, cols):
        return jnp.concatenate([refs[part][at + c * own : at + (c + 1) * own, cols] for part, at in places], axis=0)

    for c in range(spans):
        rows = slice(c * SPAN, (c + 1) * SPAN)
        heads = [slice(h * HEAD, (h + 1) * HEAD) for h in range(q_ref.shape[1] // HEAD)]
        q, d = [q_ref[rows, cols] for cols in heads], [d_ref[rows, cols] for cols in heads]
        k, v = [span_rows(keys, c, cols) for cols in heads], [span_rows(values, c, cols) for cols in heads]
        scores = [dot(a, b, NT) * scale for a, b in zip(q, k)]
        d_attention = [dot(a, b, NT) for a, b in zip(d, v)]
        exponent = [jnp.exp(a - jnp.max(a, axis=-1, keepdims=True)) for a in scores]
        attention = [a * (1.0 / jnp.sum(a, axis=-1, keepdims=True)) for a in exponent]
        low = [a.astype(BF) for a in attention]
        inner = [jnp.sum(a * b, axis=-1, keepdims=True) for a, b in zip(attention, d_attention)]
        d_scores = [
            (a * (b - c) * scale).astype(BF) for a, b, c in zip(attention, d_attention, inner)
        ]
        for h, cols in enumerate(heads):
            context_ref[rows, cols] = dot(low[h], v[h], NN).astype(BF)
            dq_ref[rows, cols] = dot(d_scores[h], k[h], NN).astype(BF)
        for h, cols in enumerate(heads):
            dk = dot(d_scores[h], q[h], TN).astype(BF)
            dv = dot(low[h], d[h], TN).astype(BF)
            for n in range(ENC):
                at = (n % SIDE) * spans * own + c * own
                dk_refs[n // SIDE][at : at + own, cols] = dk[n * own : (n + 1) * own]
                dv_refs[n // SIDE][at : at + own, cols] = dv[n * own : (n + 1) * own]


def attend(queries, d_context, keys, values):
    rows, cols = queries.shape
    group_rows = sum(k.shape[0] for k in keys) // SIDE
    chunks = [k.shape[0] * ENC // (SIDE * group_rows) for k in keys]
    row_out = jax.ShapeDtypeStruct((rows, cols), BF)
    group = jax.ShapeDtypeStruct((group_rows, cols), BF)
    out = pl.pallas_call(
        functools.partial(attention_kernel, chunks),
        out_shape=[row_out] * 2 + [group] * 8,
        in_specs=in_vmem(2 + 2 * len(keys)),
        out_specs=in_vmem(10),
        compiler_params=params(8),
        cost_estimate=cost(12 * rows * 256 * cols, 20 * 1024 * cols, rows * 1024),
    )(queries, d_context, *keys, *values)
    return out[0], out[1], out[2:6], out[6:]


def on_device(
    hidden,
    query_weight,
    key_weight,
    value_weight,
    output_weight,
    neighbour_states,
    neighbour_slot,
    d_output,
):
    index = relative_index()
    features = key_weight.shape[0]
    local = neighbour_states.shape[2]
    chunk = neighbour_states.shape[1] // ENC
    used = neighbour_slot.size
    slot_shard = neighbour_slot.reshape(-1) // SEQ

    near = gather_short(stack([hidden, d_output]))
    arrived = lax.all_to_all(
        neighbour_states.reshape(SEQ * ENC, chunk, local), AXES, split_axis=0, concat_axis=0, tiled=True
    )
    near = stack([after(near[0], arrived)] + near[1:])
    side = gather_long(near)
    arrived = arrived.reshape(SEQ, ENC, chunk, local)
    picked = jnp.take(arrived, slot_shard, axis=1)
    picked = picked.transpose(1, 2, 0, 3).reshape(used * chunk, features)
    state_near = stack(gather_short(picked))
    state_side = gather_long(state_near)

    q_d = gathered_dots(index[0], [near], query_weight, output_weight, None, F32)
    kv_near = project([state_near], key_weight, value_weight)
    far = gather_last(side, *q_d)
    q_d = gathered_dots(
        jnp.concatenate([index[1], index[3]]), side, query_weight, output_weight, q_d, F32
    )
    state_far = gather_last(state_side, *q_d, *kv_near)
    kv_side = project(state_side, key_weight, value_weight)
    queries, d_context = gathered_dots(index[2], far, query_weight, output_weight, q_d, BF)
    state_far[0] = after(state_far[0], queries, *kv_side)
    kv_far = project(state_far, key_weight, value_weight)
    keys, values = zip(kv_near, kv_side, kv_far)

    context, d_queries, d_keys, d_values = attend(queries, d_context, keys, values)
    grads = {k: [d_keys[n], d_values[n]] for n, k in enumerate((0, 1, 3, 2))}

    def pair(groups, extra, places, outs):
        return pair_dots(sum((grads[k] for k in groups), []), key_weight, value_weight, extra, places, outs)

    half, whole = grads[0][0].shape[0] // 2, grads[0][0].shape[0]
    far_low, far_high = pair([2], [], (), 2)
    from_low, from_high = move_v(far_low, 1), move_v(far_high, -1)
    g3, g1 = pair([3, 1], [from_low, from_high], ((0, 0, half), (1, half, half)), 1)
    r3, r1 = move_v(g3, 1), move_v(g1, -1)
    output, d_hidden, pieces = scatter_sums(index, context, d_queries, query_weight, output_weight, far_low)
    summed = scatter_short(pair([0], [r3, r1], ((0, 0, whole), (0, 0, whole)), 4), *pieces)

    placing = lax.broadcasted_iota(jnp.int32, (ENC, used), 0) == slot_shard[None, :]
    spread = summed.reshape(used, chunk, SEQ, local).transpose(2, 0, 1, 3)
    rank = jnp.argmax(placing, axis=1)
    spread = jnp.take(spread, rank, axis=1)
    spread = jnp.where(jnp.any(placing, axis=1)[None, :, None, None], spread, 0)
    back = lax.all_to_all(
        spread.reshape(SEQ * ENC, chunk, local), AXES, split_axis=0, concat_axis=0, tiled=True
    )
    d_states = back.reshape(neighbour_states.shape)
    return (output, d_hidden, d_states)


def solution(mesh):
    in_specs = (
        P("seq", "enc"),
        P(None, "enc"),
        P(None, "enc"),
        P(None, "enc"),
        P("enc", None),
        P("enc", None, "seq"),
        P("seq", None),
        P("seq", "enc"),
    )
    out_specs = (P("seq", "enc"), P("seq", "enc"), P("enc", None, "seq"))
    return jax.shard_map(
        on_device, mesh=mesh, in_specs=in_specs, out_specs=out_specs, check_vma=False
    )
```

time: 566 us -> 210 us (0.37); the launches traced: 556 us -> 209 us
  waiting for transfers between devices: 358 us -> 78.9 us
  matrix products: 82.1 us -> 0 us
  local copies, waits for them, and re-layouts: 64.7 us -> 5.23 us
  Pallas kernels: 0 us -> 47.8 us
  starting transfers between devices: 6.07 us -> 49.9 us
  between operations: 14.5 us -> 0.94 us
  other arithmetic: 14.8 us -> 3.65 us
  blocking collectives: 15.4 us -> 23 us
    all_gather x3 -> x0, waiting for transfers between devices: 168 us -> none  [the longest x1 74.9 us: on_device(): pooled = lax.all_gather(neighbour_states, 'enc', axis=0, tiled=True)]
    reduce_scatter x2 -> x0, waiting for transfers between devices: 130 us -> none  [the longest x1 81.2 us: on_device(): lax.psum_scatter(input_terms.astype(jnp.bfloat16), 'enc', scatter_dimensi...]
    dot_general x13 -> x0, matrix products: 82.1 us -> none  [the longest x1 13.9 us: on_device(): jnp.dot(flattened, both_weight, preferred_element_type=jnp.float32)]
    ppermute x0 -> x28, waiting for transfers between devices: none -> 64.8 us  [the longest x16 52 us: move_v(): return lax.ppermute(value, AXES, shift_table(True, shift))]
    unnamed x7 -> x0, waiting for transfers between devices: 59.6 us -> none
    pallas_call x0 -> x18, Pallas kernels: none -> 47.8 us  [the longest x3 16.3 us: call(): pl.pallas_call(kernel, out_shape=[jax.ShapeDtypeStruct(block + (2, rows,...]
    ppermute x0 -> x28, starting transfers between devices: none -> 39 us  [the longest x16 22.1 us: move_v(): return lax.ppermute(value, AXES, shift_table(True, shift))]
    unnamed x21 -> x12, local copies, waits for them, and re-layouts: 19.8 us -> 2.79 us
  transfers between devices with their start and end apart: 7 -> 29, of which waited for: 6 -> 12; matrix products, arithmetic and copies ran while one was open for 12% -> 2% of each run, Pallas kernels for 0% -> 18%
where the time goes in v2:
time: 210 us; the launch traced here: 209 us
  waiting for transfers between devices  78.9 us (38%)
  starting transfers between devices  49.9 us (24%)
  Pallas kernels  47.8 us (23%)
  blocking collectives  23 us (11%)
  local copies, waits for them, and re-layouts  5.23 us (2%)
  other arithmetic  3.65 us (2%)
    ppermute x16, waiting for transfers between devices, move_v(): return lax.ppermute(value, AXES, shift_table(True, shift))  52 us
    all_to_all x1, blocking collectives, on_device(): lax.all_to_all(neighbour_states.reshape(SEQ * ENC, chunk, local), AXES, s...  23 us
    ppermute x16, starting transfers between devices, move_v(): return lax.ppermute(value, AXES, shift_table(True, shift))  22.1 us
    ppermute x12, starting transfers between devices, move_u(): return lax.ppermute(value, AXES, shift_table(False, shift))  16.9 us
    pallas_call x3, Pallas kernels, call(): pl.pallas_call(kernel, out_shape=[jax.ShapeDtypeStruct(block + (2, rows,...  16.3 us
    pallas_call x3, Pallas kernels, gathered_dots(): pl.pallas_call(functools.partial(gathered_kernel, counts, start is not No...  14.5 us
    all_to_all x1, waiting for transfers between devices, on_device(): lax.all_to_all(spread.reshape(SEQ * ENC, chunk, local), AXES, split_axis=...  14.1 us
    ppermute x12, waiting for transfers between devices, move_u(): return lax.ppermute(value, AXES, shift_table(False, shift))  12.8 us
  transfers between devices with their start and end apart: 29, of which 12 were waited for; matrix products, arithmetic and copies ran while one was open for 2% of the time, Pallas kernels for 18%

profile of v2, /device:TPU:1, one launch (start us, length us, event | category | flops | bytes accessed | tf_op | source)
XLA Modules:
  0.0 209.4 jit_solution(3648472105367257004)
XLA Ops:
  0.6 0.9 copy-done.2
  1.6 0.9 copy-done.3
  2.6 2.5 %collective-permute-start = (bf16[2,256,512]{2,1,0:T(8,128)(2,1)S(1)}, bf16[2,256,512]{2,1,0:T(8,128)(2,1)S(1)}, u32[]{:S(2)}, u32[]{:S(2)}) collective-permute-start(bf16[2,256,512]{2,1,0:T(8,128)(2,1)S(1)} %shard_map.103.refs_0_), channel_id=1, source_target_pairs={{0,1},{1,2},{2,3},{3,0},{4,5},{5,6},{6,7},{7,4},{8,9},{9,10},{10,1... | collective-permute-start | bytes 1572872 | tf_op jit(solution)/shard_map/ppermute | solution.py:42
  5.1 3.3 %collective-permute-start.1 = (bf16[2,256,512]{2,1,0:T(8,128)(2,1)S(1)}, bf16[2,256,512]{2,1,0:T(8,128)(2,1)S(1)}, u32[]{:S(2)}, u32[]{:S(2)}) collective-permute-start(bf16[2,256,512]{2,1,0:T(8,128)(2,1)S(1)} %shard_map.103.refs_0_), channel_id=1, source_target_pairs={{0,2},{1,3},{2,0},{3,1},{4,6},{5,7},{6,4},{7,5},{8,10},{9,11},{10,... | collective-permute-start | bytes 1572872 | tf_op jit(solution)/shard_map/ppermute | solution.py:42
  8.4 0.7 collective-permute-start.2
  9.1 23.0 %all_to_all.10 = bf16[128,8,256]{2,1,0:T(8,128)(2,1)S(1)} all-to-all(bf16[128,8,256]{2,1,0:T(8,128)(2,1)} %bitcast.38), channel_id=1, replica_groups=mesh['seq'=8,'enc'=16] {'seq','enc'}, dimensions={0} | all-to-all | bytes 1048576 | tf_op jit(solution)/shard_map/all_to_all | solution.py:408
  32.1 1.5 shard_map.104.refs_0_
  33.6 2.1 %collective-permute-start.3 = (bf16[4,2,256,512]{3,2,1,0:T(8,128)(2,1)}, bf16[4,2,256,512]{3,2,1,0:T(8,128)(2,1)S(1)}, u32[]{:S(2)}, u32[]{:S(2)}) collective-permute-start(bf16[4,2,256,512]{3,2,1,0:T(8,128)(2,1)} %shard_map.104.refs_0_), channel_id=1, source_target_pairs={{0,4},{1,5},{2,6},{3,7},{4,8},{5,9},{6,10},{7,11},{8,12},{9,13},{1... | collective-permute-start | bytes 6291464 | tf_op jit(solution)/shard_map/ppermute | solution.py:46
  35.8 0.6 collective-permute-start.4
  36.6 0.6 gather_fusion
  37.2 0.1 broadcast_select_fusion
  37.3 0.2 collective-permute-start.7
  37.5 1.4 collective-permute-start.8
  38.9 1.6 collective-permute-start.9
  40.5 7.6 %collective-permute-done.7.refs_1_ = bf16[64,2048]{1,0:T(8,128)(2,1)S(1)} collective-permute-done((bf16[64,2048]{1,0:T(8,128)(2,1)S(1)}, bf16[64,2048]{1,0:T(8,128)(2,1)S(1)}, u32[]{:S(2)}, u32[]{:S(2)}) %collective-permute-start.7) | collective-permute-done | bytes 262176 | tf_op jit(solution)/shard_map/ppermute | solution.py:42
  48.2 3.3 %collective-permute-done.8.refs_2_ = bf16[64,2048]{1,0:T(8,128)(2,1)S(1)} collective-permute-done((bf16[64,2048]{1,0:T(8,128)(2,1)S(1)}, bf16[64,2048]{1,0:T(8,128)(2,1)S(1)}, u32[]{:S(2)}, u32[]{:S(2)}) %collective-permute-start.8) | collective-permute-done | bytes 262176 | tf_op jit(solution)/shard_map/ppermute | solution.py:42
  51.4 1.9 collective-permute-done.9.refs_3_
  53.4 1.0 collective-permute-start.10
  54.3 1.8 collective-permute-start.11
  56.2 4.5 %shard_map.106 = (f32[256,512]{1,0:T(8,128)S(1)}, f32[256,512]{1,0:T(8,128)S(1)}) custom-call(s32[4]{0:T(128)S(1)} %get-tuple-element.112.index_ref, bf16[8192,512]{1,0:T(8,128)(2,1)} %query_ref.11, bf16[512,8192]{1,0:T(8,128)(2,1)} %output_ref.11, bf16[4,2,256,512]{3,2,1,0:T(8,128)(2,1)} %shard_map.104.refs_0_), custom_call_target="tpu_custom_call" | custom-call | flops 1073741824 | bytes 6291456 | tf_op jit(solution)/shard_map/pallas_call | solution.py:191
  60.8 5.1 %collective-permute-done.3.one_ref.refs_0_ = bf16[4,2,256,512]{3,2,1,0:T(8,128)(2,1)S(1)} collective-permute-done((bf16[4,2,256,512]{3,2,1,0:T(8,128)(2,1)}, bf16[4,2,256,512]{3,2,1,0:T(8,128)(2,1)S(1)}, u32[]{:S(2)}, u32[]{:S(2)}) %collective-permute-start.3) | collective-permute-done | bytes 2097184 | tf_op jit(solution)/shard_map/ppermute | solution.py:46
  65.9 0.9 collective-permute-done.4.three_ref.refs_1_
  66.8 1.7 shard_map.105
  68.5 0.4 collective-permute-start.5
  68.9 2.4 %collective-permute-start.6 = (bf16[2,2,256,512]{3,2,1,0:T(8,128)(2,1)S(1)}, bf16[2,2,256,512]{3,2,1,0:T(8,128)(2,1)S(1)}, u32[]{:S(2)}, u32[]{:S(2)}) collective-permute-start(bf16[2,2,256,512]{3,2,1,0:T(8,128)(2,1)S(1)} %get-tuple-element.60), channel_id=1, source_target_pairs={{0,12},{1,13},{2,14},{3,15},{4,0},{5,1},{6,2},{7,3},{8,4},{9,5},{1... | collective-permute-start | bytes 3145736 | tf_op jit(solution)/shard_map/ppermute | solution.py:46
  71.3 1.3 shard_map.110
  72.6 4.5 %collective-permute-done.10.refs_0_.one_ref = bf16[4,64,2048]{2,1,0:T(8,128)(2,1)S(1)} collective-permute-done((bf16[4,64,2048]{2,1,0:T(8,128)(2,1)S(1)}, bf16[4,64,2048]{2,1,0:T(8,128)(2,1)S(1)}, u32[]{:S(2)}, u32[]{:S(2)}) %collective-permute-start.10) | collective-permute-done | bytes 1048608 | tf_op jit(solution)/shard_map/ppermute | solution.py:46
  77.1 0.9 collective-permute-done.11.refs_1_.three_ref
  78.1 6.2 %shard_map.107 = (f32[256,512]{1,0:T(8,128)S(1)}, f32[256,512]{1,0:T(8,128)S(1)}) custom-call(s32[8]{0:T(128)S(1)} %get-tuple-element.114.index_ref, bf16[8192,512]{1,0:T(8,128)(2,1)} %query_ref.11, bf16[512,8192]{1,0:T(8,128)(2,1)} %output_ref.11, bf16[4,2,256,512]{3,2,1,0:T(8,128)(2,1)S(1)} %collective-permute-done.3.one_ref.refs_0_, ...), custom_call_target="tpu_custom_call" | custom-call | flops 2147483648 | bytes 12582912 | tf_op jit(solution)/shard_map/pallas_call | solution.py:191
  84.3 0.3 collective-permute-start.12
  84.6 2.5 %collective-permute-start.13 = (bf16[2,64,2048]{2,1,0:T(8,128)(2,1)S(1)}, bf16[2,64,2048]{2,1,0:T(8,128)(2,1)S(1)}, u32[]{:S(2)}, u32[]{:S(2)}) collective-permute-start(bf16[2,64,2048]{2,1,0:T(8,128)(2,1)S(1)} %get-tuple-element.73), channel_id=1, source_target_pairs={{0,12},{1,13},{2,14},{3,15},{4,0},{5,1},{6,2},{7,3},{8,4},{9,5},{1... | collective-permute-start | bytes 1572872 | tf_op jit(solution)/shard_map/ppermute | solution.py:46
  87.1 2.3 %shard_map.111 = (bf16[512,512]{1,0:T(8,128)(2,1)S(1)}, bf16[512,512]{1,0:T(8,128)(2,1)S(1)}) custom-call(bf16[2048,512]{1,0:T(8,128)(2,1)S(1)} %copy-done, bf16[2048,512]{1,0:T(8,128)(2,1)S(1)} %copy-done.1, bf16[4,64,2048]{2,1,0:T(8,128)(2,1)S(1)} %collective-permute-done.10.refs_0_.one_ref, bf16[4,64,2048]{2,1,0:T(8,128)(2,1)S(1)} %collective-permute-done.11.refs_1_.three_ref), custom_call_target="tpu_custom_call" | custom-call | flops 2147483648 | bytes 8388608 | tf_op jit(solution)/shard_map/pallas_call | solution.py:285
  89.4 3.7 %shard_map.108 = (bf16[256,512]{1,0:T(8,128)(2,1)S(1)}, bf16[256,512]{1,0:T(8,128)(2,1)S(1)}) custom-call(s32[4]{0:T(128)S(1)} %get-tuple-element.111.index_ref, bf16[8192,512]{1,0:T(8,128)(2,1)} %query_ref.11, bf16[512,8192]{1,0:T(8,128)(2,1)} %output_ref.11, bf16[2,2,256,512]{3,2,1,0:T(8,128)(2,1)S(1)} %collective-permute-done.5.refs_0_, ...), custom_call_target="tpu_custom_call" | custom-call | flops 1073741824 | bytes 6291456 | tf_op jit(solution)/shard_map/pallas_call | solution.py:191
  93.2 0.8 collective-permute-done.12.refs_0_
  94.0 0.9 collective-permute-done.13.refs_1_
  94.8 1.3 shard_map.113
  96.1 2.8 %shard_map.114 = (bf16[256,512]{1,0:T(8,128)(2,1)S(1)}, bf16[256,512]{1,0:T(8,128)(2,1)S(1)}, bf16[256,512]{1,0:T(8,128)(2,1)S(1)}, bf16[256,512]{1,0:T(8,128)(2...) custom-call(bf16[256,512]{1,0:T(8,128)(2,1)S(1)} %get-tuple-element., ...), custom_call_target="tpu_custom_call" | custom-call | flops 402653184 | bytes 10485760 | tf_op jit(solution)/shard_map/pallas_call | solution.py:379
  98.9 1.3 shard_map.115
  100.2 3.6 %shard_map.116 = (bf16[2,2,256,512]{3,2,1,0:T(8,128)(2,1)S(1)}, bf16[2,2,256,512]{3,2,1,0:T(8,128)(2,1)S(1)}) custom-call(s32[4]{0:T(128)S(1)} %get-tuple-element.111.index_ref, bf16[8192,512]{1,0:T(8,128)(2,1)} %query_ref.11, bf16[512,8192]{1,0:T(8,128)(2,1)} %output_ref.11, bf16[256,512]{1,0:T(8,128)(2,1)S(1)} %get-tuple-element.80.c_ref, ...), custom_call_target="tpu_custom_call" | custom-call | flops 1073741824 | bytes 8388608 | tf_op jit(solution)/shard_map/pallas_call | solution.py:245
  103.8 0.3 collective-permute-start.14
  104.0 2.5 %collective-permute-start.15 = (bf16[2,2,256,512]{3,2,1,0:T(8,128)(2,1)S(1)}, bf16[2,2,256,512]{3,2,1,0:T(8,128)(2,1)S(1)}, u32[]{:S(2)}, u32[]{:S(2)}) collective-permute-start(bf16[2,2,256,512]{3,2,1,0:T(8,128)(2,1)S(1)} %get-tuple-element.83), channel_id=1, source_target_pairs={{0,12},{1,13},{2,14},{3,15},{4,0},{5,1},{6,2},{7,3},{8,4},{9,5},{1... | collective-permute-start | bytes 3145736 | tf_op jit(solution)/shard_map/ppermute | solution.py:46
  106.5 2.7 %collective-permute-start.22 = (bf16[128,2048]{1,0:T(8,128)(2,1)S(1)}, bf16[128,2048]{1,0:T(8,128)(2,1)S(1)}, u32[]{:S(2)}, u32[]{:S(2)}) collective-permute-start(bf16[128,2048]{1,0:T(8,128)(2,1)S(1)} %get-tuple-element.97), channel_id=1, source_target_pairs={{0,12},{1,13},{2,14},{3,15},{4,0},{5,1},{6,2},{7,3},{8,4},{9,5},{1... | collective-permute-start | bytes 1572872 | tf_op jit(solution)/shard_map/ppermute | solution.py:46
  109.2 9.8 %collective-permute-done.14.a_ref = bf16[2,2,256,512]{3,2,1,0:T(8,128)(2,1)S(1)} collective-permute-done((bf16[2,2,256,512]{3,2,1,0:T(8,128)(2,1)S(1)}, bf16[2,2,256,512]{3,2,1,0:T(8,128)(2,1)S(1)}, u32[]{:S(2)}, u32[]{:S(2)}) %collective-permute-start.14) | collective-permute-done | bytes 1048608 | tf_op jit(solution)/shard_map/ppermute | solution.py:46
  119.0 7.2 %shard_map.117 = (bf16[4,2,256,512]{3,2,1,0:T(8,128)(2,1)}, bf16[4,2,256,512]{3,2,1,0:T(8,128)(2,1)}) custom-call(s32[8]{0:T(128)S(1)} %get-tuple-element.113.index_ref, bf16[8192,512]{1,0:T(8,128)(2,1)} %query_ref.11, bf16[512,8192]{1,0:T(8,128)(2,1)} %output_ref.11, bf16[256,512]{1,0:T(8,128)(2,1)S(1)} %get-tuple-element.80.c_ref, ...), custom_call_target="tpu_custom_call" | custom-call | flops 2147483648 | bytes 16777216 | tf_op jit(solution)/shard_map/pallas_call | solution.py:245
  126.3 3.0 %collective-permute-start.17 = (bf16[4,2,256,512]{3,2,1,0:T(8,128)(2,1)}, bf16[4,2,256,512]{3,2,1,0:T(8,128)(2,1)}, u32[]{:S(2)}, u32[]{:S(2)}) collective-permute-start(bf16[4,2,256,512]{3,2,1,0:T(8,128)(2,1)} %get-tuple-element.85), channel_id=1, source_target_pairs={{0,12},{1,13},{2,14},{3,15},{4,0},{5,1},{6,2},{7,3},{8,4},{9,5},{1... | collective-permute-start | bytes 6291464 | tf_op jit(solution)/shard_map/ppermute | solution.py:46
  129.3 2.4 %shard_map.119 = (bf16[256,2048]{1,0:T(8,128)(2,1)S(1)}, bf16[256,2048]{1,0:T(8,128)(2,1)S(1)}) custom-call(bf16[2048,512]{1,0:T(8,128)(2,1)S(1)} %copy-done, bf16[2048,512]{1,0:T(8,128)(2,1)S(1)} %copy-done.1, bf16[256,512]{1,0:T(8,128)(2,1)S(1)} %get-tuple-element.93.refs_0_, bf16[256,512]{1,0:T(8,128)(2,1)S(1)} %get-tuple-element.94.refs_1_, ...), custom_call_target="tpu_custom_call" | custom-call | flops 2147483648 | bytes 8388608 | tf_op jit(solution)/shard_map/pallas_call | solution.py:324
  131.8 2.7 %collective-permute-start.24 = (bf16[256,2048]{1,0:T(8,128)(2,1)S(1)}, bf16[256,2048]{1,0:T(8,128)(2,1)S(1)}, u32[]{:S(2)}, u32[]{:S(2)}) collective-permute-start(bf16[256,2048]{1,0:T(8,128)(2,1)S(1)} %get-tuple-element.99), channel_id=1, source_target_pairs={{0,12},{1,13},{2,14},{3,15},{4,0},{5,1},{6,2},{7,3},{8,4},{9,5},{1... | collective-permute-start | bytes 3145736 | tf_op jit(solution)/shard_map/ppermute | solution.py:46
  134.4 0.6 iota_reduce_fusion
  135.0 29.1 %collective-permute-done.23.refs_2_ = bf16[256,2048]{1,0:T(8,128)(2,1)S(1)} collective-permute-done((bf16[256,2048]{1,0:T(8,128)(2,1)S(1)}, bf16[256,2048]{1,0:T(8,128)(2,1)S(1)}, u32[]{:S(2)}, u32[]{:S(2)}) %collective-permute-start.23) | collective-permute-done | bytes 1048608 | tf_op jit(solution)/shard_map/ppermute | solution.py:46
  164.2 2.2 %shard_map.120 = (bf16[64,2048]{1,0:T(8,128)(2,1)S(1)}, bf16[64,2048]{1,0:T(8,128)(2,1)}, bf16[64,2048]{1,0:T(8,128)(2,1)}, bf16[64,2048]{1,0:T(8,128)(2,1)}) custom-call(bf16[2048,512]{1,0:T(8,128)(2,1)S(1)} %copy-done, bf16[2048,512]{1,0:T(8,128)(2,1)S(1)} %copy-done.1, bf16[256,512]{1,0:T(8,128)(2,1)S(1)} %get-tuple-element.91.refs_0_, ...), custom_call_target="tpu_custom_call" | custom-call | flops 1073741824 | bytes 6291456 | tf_op jit(solution)/shard_map/pallas_call | solution.py:324
  166.4 1.3 collective-permute-start.26
  167.7 1.4 collective-permute-start.25
  169.4 5.5 %shard_map.118 = (bf16[2,256,512]{2,1,0:T(8,128)(2,1)S(1)}, bf16[2,256,512]{2,1,0:T(8,128)(2,1)}, bf16[2,256,512]{2,1,0:T(8,128)(2,1)}, bf16[2,256,512]{2,1,0:T(8,128)(2,1)}) custom-call(s32[4]{0:T(128)S(1)} %get-tuple-element.112.index_ref, bf16[8192,512]{1,0:T(8,128)(2,1)} %query_ref.11, bf16[512,8192]{1,0:T(8,128)(2,1)} %output_ref.11, ...), custom_call_target="tpu_custom_call" | custom-call | flops 1073741824 | bytes 8388608 | tf_op jit(solution)/shard_map/pallas_call | solution.py:245
  174.9 0.6 collective-permute-start.20
  175.6 1.9 collective-permute-start.19
  177.4 2.0 collective-permute-start.18
  179.4 1.2 add_convert_fusion.1
  180.7 0.6 gather_fusion.1
  181.4 1.1 fusion
  182.5 10.8 %all-to-all-start.1 = ((bf16[128,8,256]{2,1,0:T(8,128)(2,1)}), bf16[128,8,256]{2,1,0:T(8,128)(2,1)S(1)}, u32[]{:S(2)}, u32[]{:S(2)}) async-start(bf16[128,8,256]{2,1,0:T(8,128)(2,1)} %fusion), calls=%async_computation.1 | async-start | bytes 1048576 | tf_op jit(solution)/shard_map/all_to_all | solution.py:451
  193.3 14.1 %all-to-all-done.1 = bf16[128,8,256]{2,1,0:T(8,128)(2,1)S(1)} async-done(((bf16[128,8,256]{2,1,0:T(8,128)(2,1)}), bf16[128,8,256]{2,1,0:T(8,128)(2,1)S(1)}, u32[]{:S(2)}, u32[]{:S(2)}) %all-to-all-start.1) | async-done | bytes 524320 | tf_op jit(solution)/shard_map/all_to_all | solution.py:451
  207.5 0.3 add_convert_fusion
  207.7 0.8 slice_bitcast_fusion
  208.6 0.8 copy.26
  (54 shorter events, 1.2 us)
Async XLA Ops:
  0.6 1.0 copy-start.2
  1.6 0.9 copy-start.3
  2.6 29.6 %collective-permute-start = (bf16[2,256,512]{2,1,0:T(8,128)(2,1)S(1)}, bf16[2,256,512]{2,1,0:T(8,128)(2,1)S(1)}, u32[]{:S(2)}, u32[]{:S(2)}) collective-permute-start(bf16[2,256,512]{2,1,0:T(8,128)(2,1)S(1)} %shard_map.103.refs_0_), channel_id=1, source_target_pairs={{0,1},{1,2},{2,3},{3,0},{4,5},{5,6},{6,7},{7,4},{8,9},{9,10},{10,1... | collective-permute-start | bytes 1572872 | tf_op jit(solution)/shard_map/ppermute | solution.py:42
  5.1 27.0 %collective-permute-start.1 = (bf16[2,256,512]{2,1,0:T(8,128)(2,1)S(1)}, bf16[2,256,512]{2,1,0:T(8,128)(2,1)S(1)}, u32[]{:S(2)}, u32[]{:S(2)}) collective-permute-start(bf16[2,256,512]{2,1,0:T(8,128)(2,1)S(1)} %shard_map.103.refs_0_), channel_id=1, source_target_pairs={{0,2},{1,3},{2,0},{3,1},{4,6},{5,7},{6,4},{7,5},{8,10},{9,11},{10,... | collective-permute-start | bytes 1572872 | tf_op jit(solution)/shard_map/ppermute | solution.py:42
  8.4 23.7 %collective-permute-start.2 = (bf16[2,256,512]{2,1,0:T(8,128)(2,1)S(1)}, bf16[2,256,512]{2,1,0:T(8,128)(2,1)S(1)}, u32[]{:S(2)}, u32[]{:S(2)}) collective-permute-start(bf16[2,256,512]{2,1,0:T(8,128)(2,1)S(1)} %shard_map.103.refs_0_), channel_id=1, source_target_pairs={{0,3},{1,0},{2,1},{3,2},{4,7},{5,4},{6,5},{7,6},{8,11},{9,8},{10,9... | collective-permute-start | bytes 1572872 | tf_op jit(solution)/shard_map/ppermute | solution.py:42
  32.1 4.2 %copy-start.4 = (s32[4,2]{0,1:T(2,128)S(1)}, s32[4,2]{0,1:T(2,128)}, u32[]{:S(2)}) copy-start(s32[4,2]{0,1:T(2,128)} %param.14) | copy-start | bytes 100
  33.6 32.2 %collective-permute-start.3 = (bf16[4,2,256,512]{3,2,1,0:T(8,128)(2,1)}, bf16[4,2,256,512]{3,2,1,0:T(8,128)(2,1)S(1)}, u32[]{:S(2)}, u32[]{:S(2)}) collective-permute-start(bf16[4,2,256,512]{3,2,1,0:T(8,128)(2,1)} %shard_map.104.refs_0_), channel_id=1, source_target_pairs={{0,4},{1,5},{2,6},{3,7},{4,8},{5,9},{6,10},{7,11},{8,12},{9,13},{1... | collective-permute-start | bytes 6291464 | tf_op jit(solution)/shard_map/ppermute | solution.py:46
  35.8 31.0 %collective-permute-start.4 = (bf16[4,2,256,512]{3,2,1,0:T(8,128)(2,1)}, bf16[4,2,256,512]{3,2,1,0:T(8,128)(2,1)}, u32[]{:S(2)}, u32[]{:S(2)}) collective-permute-start(bf16[4,2,256,512]{3,2,1,0:T(8,128)(2,1)} %shard_map.104.refs_0_), channel_id=1, source_target_pairs={{0,12},{1,13},{2,14},{3,15},{4,0},{5,1},{6,2},{7,3},{8,4},{9,5},{1... | collective-permute-start | bytes 6291464 | tf_op jit(solution)/shard_map/ppermute | solution.py:46
  37.3 10.8 %collective-permute-start.7 = (bf16[64,2048]{1,0:T(8,128)(2,1)S(1)}, bf16[64,2048]{1,0:T(8,128)(2,1)S(1)}, u32[]{:S(2)}, u32[]{:S(2)}) collective-permute-start(bf16[64,2048]{1,0:T(8,128)(2,1)S(1)} %bitcast.29), channel_id=1, source_target_pairs={{0,1},{1,2},{2,3},{3,0},{4,5},{5,6},{6,7},{7,4},{8,9},{9,10},{10,1... | collective-permute-start | bytes 786440 | tf_op jit(solution)/shard_map/ppermute | solution.py:42
  37.5 13.9 %collective-permute-start.8 = (bf16[64,2048]{1,0:T(8,128)(2,1)S(1)}, bf16[64,2048]{1,0:T(8,128)(2,1)S(1)}, u32[]{:S(2)}, u32[]{:S(2)}) collective-permute-start(bf16[64,2048]{1,0:T(8,128)(2,1)S(1)} %bitcast.30), channel_id=1, source_target_pairs={{0,2},{1,3},{2,0},{3,1},{4,6},{5,7},{6,4},{7,5},{8,10},{9,11},{10,... | collective-permute-start | bytes 786440 | tf_op jit(solution)/shard_map/ppermute | solution.py:42
  38.9 14.4 %collective-permute-start.9 = (bf16[64,2048]{1,0:T(8,128)(2,1)S(1)}, bf16[64,2048]{1,0:T(8,128)(2,1)S(1)}, u32[]{:S(2)}, u32[]{:S(2)}) collective-permute-start(bf16[64,2048]{1,0:T(8,128)(2,1)S(1)} %bitcast.31), channel_id=1, source_target_pairs={{0,3},{1,0},{2,1},{3,2},{4,7},{5,4},{6,5},{7,6},{8,11},{9,8},{10,9... | collective-permute-start | bytes 786440 | tf_op jit(solution)/shard_map/ppermute | solution.py:42
  53.4 23.7 %collective-permute-start.10 = (bf16[4,64,2048]{2,1,0:T(8,128)(2,1)S(1)}, bf16[4,64,2048]{2,1,0:T(8,128)(2,1)S(1)}, u32[]{:S(2)}, u32[]{:S(2)}) collective-permute-start(bf16[4,64,2048]{2,1,0:T(8,128)(2,1)S(1)} %shard_map.109.refs_0_), channel_id=1, source_target_pairs={{0,4},{1,5},{2,6},{3,7},{4,8},{5,9},{6,10},{7,11},{8,12},{9,13},{1... | collective-permute-start | bytes 3145736 | tf_op jit(solution)/shard_map/ppermute | solution.py:46
  54.3 23.7 %collective-permute-start.11 = (bf16[4,64,2048]{2,1,0:T(8,128)(2,1)S(1)}, bf16[4,64,2048]{2,1,0:T(8,128)(2,1)S(1)}, u32[]{:S(2)}, u32[]{:S(2)}) collective-permute-start(bf16[4,64,2048]{2,1,0:T(8,128)(2,1)S(1)} %shard_map.109.refs_0_), channel_id=1, source_target_pairs={{0,12},{1,13},{2,14},{3,15},{4,0},{5,1},{6,2},{7,3},{8,4},{9,5},{1... | collective-permute-start | bytes 3145736 | tf_op jit(solution)/shard_map/ppermute | solution.py:46
  60.8 10.5 %copy-start = (bf16[2048,512]{1,0:T(8,128)(2,1)S(1)}, bf16[2048,512]{1,0:T(8,128)(2,1)}, u32[]{:S(2)}) copy-start(bf16[2048,512]{1,0:T(8,128)(2,1)} %key_ref.11) | copy-start | bytes 6291460
  60.8 10.5 %copy-start.1 = (bf16[2048,512]{1,0:T(8,128)(2,1)S(1)}, bf16[2048,512]{1,0:T(8,128)(2,1)}, u32[]{:S(2)}) copy-start(bf16[2048,512]{1,0:T(8,128)(2,1)} %value_ref.11) | copy-start | bytes 6291460
  68.5 20.9 %collective-permute-start.5 = (bf16[2,2,256,512]{3,2,1,0:T(8,128)(2,1)S(1)}, bf16[2,2,256,512]{3,2,1,0:T(8,128)(2,1)S(1)}, u32[]{:S(2)}, u32[]{:S(2)}) collective-permute-start(bf16[2,2,256,512]{3,2,1,0:T(8,128)(2,1)S(1)} %get-tuple-element.58), channel_id=1, source_target_pairs={{0,4},{1,5},{2,6},{3,7},{4,8},{5,9},{6,10},{7,11},{8,12},{9,13},{1... | collective-permute-start | bytes 3145736 | tf_op jit(solution)/shard_map/ppermute | solution.py:46
  68.9 20.6 %collective-permute-start.6 = (bf16[2,2,256,512]{3,2,1,0:T(8,128)(2,1)S(1)}, bf16[2,2,256,512]{3,2,1,0:T(8,128)(2,1)S(1)}, u32[]{:S(2)}, u32[]{:S(2)}) collective-permute-start(bf16[2,2,256,512]{3,2,1,0:T(8,128)(2,1)S(1)} %get-tuple-element.60), channel_id=1, source_target_pairs={{0,12},{1,13},{2,14},{3,15},{4,0},{5,1},{6,2},{7,3},{8,4},{9,5},{1... | collective-permute-start | bytes 3145736 | tf_op jit(solution)/shard_map/ppermute | solution.py:46
  84.3 9.6 %collective-permute-start.12 = (bf16[2,64,2048]{2,1,0:T(8,128)(2,1)S(1)}, bf16[2,64,2048]{2,1,0:T(8,128)(2,1)S(1)}, u32[]{:S(2)}, u32[]{:S(2)}) collective-permute-start(bf16[2,64,2048]{2,1,0:T(8,128)(2,1)S(1)} %get-tuple-element.69), channel_id=1, source_target_pairs={{0,4},{1,5},{2,6},{3,7},{4,8},{5,9},{6,10},{7,11},{8,12},{9,13},{1... | collective-permute-start | bytes 1572872 | tf_op jit(solution)/shard_map/ppermute | solution.py:46
  84.6 10.3 %collective-permute-start.13 = (bf16[2,64,2048]{2,1,0:T(8,128)(2,1)S(1)}, bf16[2,64,2048]{2,1,0:T(8,128)(2,1)S(1)}, u32[]{:S(2)}, u32[]{:S(2)}) collective-permute-start(bf16[2,64,2048]{2,1,0:T(8,128)(2,1)S(1)} %get-tuple-element.73), channel_id=1, source_target_pairs={{0,12},{1,13},{2,14},{3,15},{4,0},{5,1},{6,2},{7,3},{8,4},{9,5},{1... | collective-permute-start | bytes 1572872 | tf_op jit(solution)/shard_map/ppermute | solution.py:46
  103.8 15.2 %collective-permute-start.14 = (bf16[2,2,256,512]{3,2,1,0:T(8,128)(2,1)S(1)}, bf16[2,2,256,512]{3,2,1,0:T(8,128)(2,1)S(1)}, u32[]{:S(2)}, u32[]{:S(2)}) collective-permute-start(bf16[2,2,256,512]{3,2,1,0:T(8,128)(2,1)S(1)} %get-tuple-element.82), channel_id=1, source_target_pairs={{0,4},{1,5},{2,6},{3,7},{4,8},{5,9},{6,10},{7,11},{8,12},{9,13},{1... | collective-permute-start | bytes 3145736 | tf_op jit(solution)/shard_map/ppermute | solution.py:46
  104.0 15.0 %collective-permute-start.15 = (bf16[2,2,256,512]{3,2,1,0:T(8,128)(2,1)S(1)}, bf16[2,2,256,512]{3,2,1,0:T(8,128)(2,1)S(1)}, u32[]{:S(2)}, u32[]{:S(2)}) collective-permute-start(bf16[2,2,256,512]{3,2,1,0:T(8,128)(2,1)S(1)} %get-tuple-element.83), channel_id=1, source_target_pairs={{0,12},{1,13},{2,14},{3,15},{4,0},{5,1},{6,2},{7,3},{8,4},{9,5},{1... | collective-permute-start | bytes 3145736 | tf_op jit(solution)/shard_map/ppermute | solution.py:46
  106.5 22.8 %collective-permute-start.21 = (bf16[128,2048]{1,0:T(8,128)(2,1)S(1)}, bf16[128,2048]{1,0:T(8,128)(2,1)S(1)}, u32[]{:S(2)}, u32[]{:S(2)}) collective-permute-start(bf16[128,2048]{1,0:T(8,128)(2,1)S(1)} %get-tuple-element.79), channel_id=1, source_target_pairs={{0,4},{1,5},{2,6},{3,7},{4,8},{5,9},{6,10},{7,11},{8,12},{9,13},{1... | collective-permute-start | bytes 1572872 | tf_op jit(solution)/shard_map/ppermute | solution.py:46
  106.5 22.8 %collective-permute-start.22 = (bf16[128,2048]{1,0:T(8,128)(2,1)S(1)}, bf16[128,2048]{1,0:T(8,128)(2,1)S(1)}, u32[]{:S(2)}, u32[]{:S(2)}) collective-permute-start(bf16[128,2048]{1,0:T(8,128)(2,1)S(1)} %get-tuple-element.97), channel_id=1, source_target_pairs={{0,12},{1,13},{2,14},{3,15},{4,0},{5,1},{6,2},{7,3},{8,4},{9,5},{1... | collective-permute-start | bytes 1572872 | tf_op jit(solution)/shard_map/ppermute | solution.py:46
  126.2 43.1 %collective-permute-start.16 = (bf16[4,2,256,512]{3,2,1,0:T(8,128)(2,1)}, bf16[4,2,256,512]{3,2,1,0:T(8,128)(2,1)S(1)}, u32[]{:S(2)}, u32[]{:S(2)}) collective-permute-start(bf16[4,2,256,512]{3,2,1,0:T(8,128)(2,1)} %get-tuple-element.84), channel_id=1, source_target_pairs={{0,4},{1,5},{2,6},{3,7},{4,8},{5,9},{6,10},{7,11},{8,12},{9,13},{1... | collective-permute-start | bytes 6291464 | tf_op jit(solution)/shard_map/ppermute | solution.py:46
  126.3 43.1 %collective-permute-start.17 = (bf16[4,2,256,512]{3,2,1,0:T(8,128)(2,1)}, bf16[4,2,256,512]{3,2,1,0:T(8,128)(2,1)}, u32[]{:S(2)}, u32[]{:S(2)}) collective-permute-start(bf16[4,2,256,512]{3,2,1,0:T(8,128)(2,1)} %get-tuple-element.85), channel_id=1, source_target_pairs={{0,12},{1,13},{2,14},{3,15},{4,0},{5,1},{6,2},{7,3},{8,4},{9,5},{1... | collective-permute-start | bytes 6291464 | tf_op jit(solution)/shard_map/ppermute | solution.py:46
  131.7 32.5 %collective-permute-start.23 = (bf16[256,2048]{1,0:T(8,128)(2,1)S(1)}, bf16[256,2048]{1,0:T(8,128)(2,1)S(1)}, u32[]{:S(2)}, u32[]{:S(2)}) collective-permute-start(bf16[256,2048]{1,0:T(8,128)(2,1)S(1)} %get-tuple-element.98), channel_id=1, source_target_pairs={{0,4},{1,5},{2,6},{3,7},{4,8},{5,9},{6,10},{7,11},{8,12},{9,13},{1... | collective-permute-start | bytes 3145736 | tf_op jit(solution)/shard_map/ppermute | solution.py:46
  131.8 32.4 %collective-permute-start.24 = (bf16[256,2048]{1,0:T(8,128)(2,1)S(1)}, bf16[256,2048]{1,0:T(8,128)(2,1)S(1)}, u32[]{:S(2)}, u32[]{:S(2)}) collective-permute-start(bf16[256,2048]{1,0:T(8,128)(2,1)S(1)} %get-tuple-element.99), channel_id=1, source_target_pairs={{0,12},{1,13},{2,14},{3,15},{4,0},{5,1},{6,2},{7,3},{8,4},{9,5},{1... | collective-permute-start | bytes 3145736 | tf_op jit(solution)/shard_map/ppermute | solution.py:46
  166.4 11.0 %collective-permute-start.27 = (bf16[64,2048]{1,0:T(8,128)(2,1)}, bf16[64,2048]{1,0:T(8,128)(2,1)}, u32[]{:S(2)}, u32[]{:S(2)}) collective-permute-start(bf16[64,2048]{1,0:T(8,128)(2,1)} %get-tuple-element.104), channel_id=1, source_target_pairs={{0,1},{1,2},{2,3},{3,0},{4,5},{5,6},{6,7},{7,4},{8,9},{9,10},{10,1... | collective-permute-start | bytes 786440 | tf_op jit(solution)/shard_map/ppermute | solution.py:42
  166.4 13.0 %collective-permute-start.26 = (bf16[64,2048]{1,0:T(8,128)(2,1)}, bf16[64,2048]{1,0:T(8,128)(2,1)}, u32[]{:S(2)}, u32[]{:S(2)}) collective-permute-start(bf16[64,2048]{1,0:T(8,128)(2,1)} %get-tuple-element.103), channel_id=1, source_target_pairs={{0,2},{1,3},{2,0},{3,1},{4,6},{5,7},{6,4},{7,5},{8,10},{9,11},{10,... | collective-permute-start | bytes 786440 | tf_op jit(solution)/shard_map/ppermute | solution.py:42
  167.7 11.7 %collective-permute-start.25 = (bf16[64,2048]{1,0:T(8,128)(2,1)}, bf16[64,2048]{1,0:T(8,128)(2,1)}, u32[]{:S(2)}, u32[]{:S(2)}) collective-permute-start(bf16[64,2048]{1,0:T(8,128)(2,1)} %get-tuple-element.102), channel_id=1, source_target_pairs={{0,3},{1,0},{2,1},{3,2},{4,7},{5,4},{6,5},{7,6},{8,11},{9,8},{10,9... | collective-permute-start | bytes 786440 | tf_op jit(solution)/shard_map/ppermute | solution.py:42
  174.9 32.5 %collective-permute-start.20 = (bf16[2,256,512]{2,1,0:T(8,128)(2,1)}, bf16[2,256,512]{2,1,0:T(8,128)(2,1)S(1)}, u32[]{:S(2)}, u32[]{:S(2)}) collective-permute-start(bf16[2,256,512]{2,1,0:T(8,128)(2,1)} %get-tuple-element.89), channel_id=1, source_target_pairs={{0,1},{1,2},{2,3},{3,0},{4,5},{5,6},{6,7},{7,4},{8,9},{9,10},{10,1... | collective-permute-start | bytes 1572872 | tf_op jit(solution)/shard_map/ppermute | solution.py:42
  175.6 31.9 %collective-permute-start.19 = (bf16[2,256,512]{2,1,0:T(8,128)(2,1)}, bf16[2,256,512]{2,1,0:T(8,128)(2,1)S(1)}, u32[]{:S(2)}, u32[]{:S(2)}) collective-permute-start(bf16[2,256,512]{2,1,0:T(8,128)(2,1)} %get-tuple-element.88), channel_id=1, source_target_pairs={{0,2},{1,3},{2,0},{3,1},{4,6},{5,7},{6,4},{7,5},{8,10},{9,11},{10,... | collective-permute-start | bytes 1572872 | tf_op jit(solution)/shard_map/ppermute | solution.py:42
  177.4 30.0 %collective-permute-start.18 = (bf16[2,256,512]{2,1,0:T(8,128)(2,1)}, bf16[2,256,512]{2,1,0:T(8,128)(2,1)S(1)}, u32[]{:S(2)}, u32[]{:S(2)}) collective-permute-start(bf16[2,256,512]{2,1,0:T(8,128)(2,1)} %get-tuple-element.87), channel_id=1, source_target_pairs={{0,3},{1,0},{2,1},{3,2},{4,7},{5,4},{6,5},{7,6},{8,11},{9,8},{10,9... | collective-permute-start | bytes 1572872 | tf_op jit(solution)/shard_map/ppermute | solution.py:42
  182.5 25.0 %all-to-all-start.1 = ((bf16[128,8,256]{2,1,0:T(8,128)(2,1)}), bf16[128,8,256]{2,1,0:T(8,128)(2,1)S(1)}, u32[]{:S(2)}, u32[]{:S(2)}) async-start(bf16[128,8,256]{2,1,0:T(8,128)(2,1)} %fusion), calls=%async_computation.1 | async-start | bytes 1048576 | tf_op jit(solution)/shard_map/all_to_all | solution.py:451

commit v3 on v2

--- a/solution.py
+++ b/solution.py
@@ -72,9 +72,29 @@
         out_shape=jax.ShapeDtypeStruct((len(values),) + values[0].shape, BF),
         in_specs=[pl.BlockSpec(memory_space=pltpu.VMEM)] * len(values),
         out_specs=pl.BlockSpec(memory_space=pltpu.VMEM),
-        compiler_params=params(4),
+        compiler_params=params(8),
         cost_estimate=cost(0, 4 * len(values) * values[0].size),
     )(*values)
+
+
+def join_kernel(one_ref, two_ref, out_ref, sems):
+    copies = [pltpu.make_async_copy(ref, out_ref.at[n], sems.at[n]) for n, ref in enumerate((one_ref, two_ref))]
+    for copy in copies:
+        copy.start()
+    for copy in copies:
+        copy.wait()
+
+
+def join(one, two):
+    return pl.pallas_call(
+        join_kernel,
+        out_shape=jax.ShapeDtypeStruct((2,) + one.shape, BF),
+        in_specs=in_hbm(2),
+        out_specs=pl.BlockSpec(memory_space=pltpu.VMEM),
+        scratch_shapes=[pltpu.SemaphoreType.DMA((2,))],
+        compiler_params=params(8),
+        cost_estimate=cost(0, 8 * one.size),
+    )(*kept(one, two))
 
 
 def halves_kernel(one_ref, three_ref, low_ref, high_ref):
@@ -89,7 +109,7 @@
         out_shape=[half, half],
         in_specs=[pl.BlockSpec(memory_space=pltpu.VMEM)] * 2,
         out_specs=[pl.BlockSpec(memory_space=pltpu.VMEM)] * 2,
-        compiler_params=params(4),
+        compiler_params=params(8),
         cost_estimate=cost(0, 4 * one.size),
     )(one, three)
 
@@ -116,7 +136,7 @@
 
 
 def cost(flops, bytes_accessed, transcendentals=0):
-    return pl.CostEstimate(flops=flops, bytes_accessed=bytes_accessed, transcendentals=transcendentals)
+    return pl.CostEstimate(flops=flops // 1024, bytes_accessed=bytes_accessed // 1024, transcendentals=0)
 
 
 DEPTH = 4
@@ -196,80 +216,122 @@
         + in_vmem(len(parts) + (0 if start is None else 2)),
         out_specs=in_vmem(2),
         scratch_shapes=stream_scratch(width),
-        compiler_params=params(10),
+        compiler_params=params(8),
         cost_estimate=cost(4 * count * rows * width * cols, 4 * count * (rows + cols) * width),
     )(index, *kept(query_weight, output_weight), *parts, *([] if start is None else start))
 
 
-def far_kernel(index_ref, query_ref, output_ref, c_ref, d_ref, low_ref, high_ref, *scratch):
-    for n, query_block, output_block in Stream(index_ref, 4, query_ref, output_ref, scratch).blocks():
-        out_ref = low_ref if n < 2 else high_ref
-        out_ref[n % 2, 0] = dot(c_ref[...], output_block[...], NN).astype(BF)
-        out_ref[n % 2, 1] = dot(d_ref[...], query_block[...], NT).astype(BF)
-
-
-def side_kernel(index_ref, query_ref, output_ref, c_ref, d_ref, a_ref, b_ref, g3_ref, g1_ref, *scratch):
-    for n, query_block, output_block in Stream(index_ref, 8, query_ref, output_ref, scratch).blocks():
-        j = n % 4
-        out_ref = g3_ref if n < 4 else g1_ref
-        part_ref = None
-        if n < 4 and j < 2:
-            part_ref = a_ref.at[j]
-        elif n >= 4 and j >= 2:
-            part_ref = b_ref.at[j - 2]
-        value = dot(c_ref[...], output_block[...], NN)
-        if part_ref is not None:
-            value = value + part_ref[0].astype(F32)
-        out_ref[j, 0] = value.astype(BF)
-        value = dot(d_ref[...], query_block[...], NT)
-        if part_ref is not None:
-            value = value + part_ref[1].astype(F32)
-        out_ref[j, 1] = value.astype(BF)
-
-
-def near_kernel(index_ref, query_ref, output_ref, c_ref, d_ref, r3_ref, r1_ref, *refs):
-    t_refs, scratch = refs[:4], refs[4:]
-    for n, query_block, output_block in Stream(index_ref, 4, query_ref, output_ref, scratch).blocks():
-        value = dot(c_ref[...], output_block[...], NN)
-        t_refs[n][0] = (value + r3_ref[n, 0].astype(F32) + r1_ref[n, 0].astype(F32)).astype(BF)
-        value = dot(d_ref[...], query_block[...], NT)
-        t_refs[n][1] = (value + r3_ref[n, 1].astype(F32) + r1_ref[n, 1].astype(F32)).astype(BF)
-
-
-def scatter_sums(index, context, d_queries, query_weight, output_weight, *others):
+def terms_kernel(count, index_ref, query_ref, output_ref, c_ref, d_ref, *refs):
+    out_refs, scratch = refs[:-4], refs[-4:]
+    targets = [(ref, at) for ref in out_refs for at in range(0, ref.shape[0], 2)]
+    for n, query_block, output_block in Stream(index_ref, count, query_ref, output_ref, scratch).blocks():
+        out_ref, at = targets[n]
+        out_ref[at] = dot(c_ref[...], output_block[...], NN).astype(BF)
+        out_ref[at + 1] = dot(d_ref[...], query_block[...], NT).astype(BF)
+
+
+def scatter_terms(context, d_queries, query_weight, output_weight):
     rows, inner = context.shape
     width = query_weight.shape[0] // ENC
 
-    def call(kernel, place, extra, out_blocks):
+    def call(place, out_tiles, *others):
         count = place.shape[0]
         return pl.pallas_call(
-            kernel,
-            out_shape=[jax.ShapeDtypeStruct(block + (2, rows, width), BF) for block in out_blocks],
-            in_specs=[pl.BlockSpec(memory_space=pltpu.SMEM)] + in_hbm(2) + in_vmem(2 + len(extra)),
-            out_specs=in_vmem(len(out_blocks)),
+            functools.partial(terms_kernel, count),
+            out_shape=[jax.ShapeDtypeStruct((tiles, rows, width), BF) for tiles in out_tiles],
+            in_specs=[pl.BlockSpec(memory_space=pltpu.SMEM)] + in_hbm(2) + in_vmem(2),
+            out_specs=in_vmem(len(out_tiles)),
             scratch_shapes=stream_scratch(width),
-            compiler_params=params(10),
+            compiler_params=params(8),
             cost_estimate=cost(4 * count * rows * inner * width, 4 * count * (2 * rows + inner) * width),
-        )(place, *kept(query_weight, output_weight), context, d_queries, *extra)
-
-    context = after(context, *others)
-    far_low, far_high = call(far_kernel, index[2], [], [(2,), (2,)])
-    from_low, from_high = move_v(far_low, 1), move_v(far_high, -1)
-    g3, g1 = call(
-        side_kernel, jnp.concatenate([index[3], index[1]]), [from_low, from_high], [(4,), (4,)]
-    )
-    r3, r1 = move_v(g3, 1), move_v(g1, -1)
-    pieces = call(near_kernel, index[0], [r3, r1], [()] * 4)
-    total = scatter_short(pieces)
-    return total[0], total[1], pieces
-
-
-def scatter_short(pieces, *others):
-    t0, t1, t2, t3 = pieces
-    q1, q2, q3 = move_u(t1, -1), move_u(t2, 2), move_u(t3, 1)
-    t0 = after(t0, *others)
-    total = t0.astype(F32) + q1.astype(F32) + q2.astype(F32) + q3.astype(F32)
-    return total.astype(BF)
+        )(place, *kept(query_weight, output_weight), after(context, *others), d_queries)
+
+    return call
+
+
+def plus(*values):
+    return sum(value.astype(F32) for value in values).astype(BF)
+
+
+def pass_on_kernel(g3_ref, g1_ref, low_ref, high_ref, far_low_ref, far_high_ref, up_ref, down_ref):
+    for n in range(2):
+        up_ref[n] = plus(g3_ref[n], low_ref[n])
+        up_ref[n + 2] = g3_ref[n + 2]
+        down_ref[n] = g1_ref[n]
+        down_ref[n + 2] = plus(g1_ref[n + 2], high_ref[n])
+    for n in range(4):
+        up_ref[n + 4] = far_low_ref[n]
+        down_ref[n + 4] = far_high_ref[n]
+
+
+def pass_on(g3, g1, low, high, far_low, far_high):
+    return pl.pallas_call(
+        pass_on_kernel,
+        out_shape=[jax.ShapeDtypeStruct((8,) + g3.shape[1:], BF)] * 2,
+        in_specs=in_vmem(6),
+        out_specs=in_vmem(2),
+        compiler_params=params(8),
+        cost_estimate=cost(g3.size, 8 * g3.size),
+    )(g3, g1, low, high, far_low, far_high)
+
+
+def add_halves_kernel(g3_ref, g1_ref, up_ref, down_ref, out3_ref, out1_ref):
+    for n in range(4):
+        out3_ref[n] = plus(g3_ref[n], up_ref[n + 4])
+        out3_ref[n + 4] = g3_ref[n + 4]
+        out1_ref[n] = g1_ref[n]
+        out1_ref[n + 4] = plus(g1_ref[n + 4], down_ref[n + 4])
+
+
+def add_halves(g3, g1, up, down):
+    return pl.pallas_call(
+        add_halves_kernel,
+        out_shape=[jax.ShapeDtypeStruct(g3.shape, BF)] * 2,
+        in_specs=in_vmem(4),
+        out_specs=in_vmem(2),
+        compiler_params=params(8),
+        cost_estimate=cost(g3.size, 4 * g3.size),
+    )(g3, g1, up, down)
+
+
+def add_pieces_kernel(*refs):
+    r3_ref, r1_ref = refs[4:6]
+    for n in range(4):
+        tiles = refs[n].shape[0]
+        for m in range(tiles):
+            refs[6 + n][m] = plus(refs[n][m], r3_ref[n * tiles + m], r1_ref[n * tiles + m])
+
+
+def add_pieces(pieces, r3, r1):
+    return pl.pallas_call(
+        add_pieces_kernel,
+        out_shape=[jax.ShapeDtypeStruct(pieces[0].shape, BF)] * 4,
+        in_specs=in_vmem(6),
+        out_specs=in_vmem(4),
+        compiler_params=params(8),
+        cost_estimate=cost(8 * r3.size, 8 * r3.size),
+    )(*pieces, r3, r1)
+
+
+def move_pieces(pieces):
+    return move_u(pieces[1], -1), move_u(pieces[2], 2), move_u(pieces[3], 1)
+
+
+def finish_kernel(*refs):
+    for n, ref in enumerate(refs[4:]):
+        ref[...] = plus(*[part[n] for part in refs[:4]])
+
+
+def finish(*parts):
+    tiles = parts[0].shape[0]
+    return pl.pallas_call(
+        finish_kernel,
+        out_shape=[jax.ShapeDtypeStruct(parts[0].shape[1:], BF)] * tiles,
+        in_specs=in_vmem(4),
+        out_specs=in_vmem(tiles),
+        compiler_params=params(8),
+        cost_estimate=cost(4 * parts[0].size, 10 * parts[0].size),
+    )(*parts)
 
 
 def project_kernel(pairs, key_ref, value_ref, *refs):
@@ -292,43 +354,33 @@
     )(key_weight, value_weight, *pairs)
 
 
-def pair_kernel(places, groups, key_ref, value_ref, *refs):
-    count = 2 * groups
-    d_refs, refs = refs[:count], refs[count:]
-    extra_refs, out_refs = refs[: len(places)], refs[len(places) :]
+def pair_kernel(groups, key_ref, value_ref, *refs):
+    d_refs, out_refs = refs[: 2 * groups], refs[2 * groups :]
     tile = key_ref.shape[1]
-    rows = d_refs[0].shape[0]
-    per_group = len(out_refs) // groups
-    each = rows // per_group
+    rows = d_refs[0].shape[0] // SIDE
     for n in range(key_ref.shape[0] // tile):
-        cols = slice(n * tile, (n + 1) * tile)
+        targets = [(ref, m) for ref in out_refs for m in range(ref.shape[0])]
         for g in range(groups):
-            total = dot(d_refs[2 * g][...], key_ref[cols, :], NT)
-            total = total + dot(d_refs[2 * g + 1][...], value_ref[cols, :], NT)
-            for (group, first, size), extra_ref in zip(places, extra_refs):
-                if group != g:
-                    continue
-                part = extra_ref[:, cols].astype(F32)
-                if size < rows:
-                    zero = jnp.zeros((rows - size, tile), F32)
-                    part = jnp.concatenate([zero, part] if first else [part, zero], axis=0)
-                total = total + part
-            for m in range(per_group):
-                out_refs[g * per_group + m][:, cols] = total[m * each : (m + 1) * each].astype(BF)
-
-
-def pair_dots(grads, key_weight, value_weight, extra, places, per_group):
-    groups = len(grads) // 2
+            total = dot(d_refs[2 * g][...], key_ref[n * tile : (n + 1) * tile, :], NT)
+            total = (total + dot(d_refs[2 * g + 1][...], value_ref[n * tile : (n + 1) * tile, :], NT)).astype(BF)
+            for m in range(SIDE):
+                out_ref, at = targets[g * SIDE + m]
+                out_ref[at, n * rows : (n + 1) * rows, :] = total[m * rows : (m + 1) * rows]
+
+
+def pair_dots(grads, key_weight, value_weight, outs):
     rows, inner = grads[0].shape
     features = key_weight.shape[0]
-    return pl.pallas_call(
-        functools.partial(pair_kernel, places, groups),
-        out_shape=[jax.ShapeDtypeStruct((rows // per_group, features), BF)] * (groups * per_group),
-        in_specs=in_vmem(2 + len(grads) + len(extra)),
-        out_specs=in_vmem(groups * per_group),
+    shape = (rows // SIDE * (features // inner), inner)
+    groups = len(grads) // 2
+    return pl.pallas_call(
+        functools.partial(pair_kernel, groups),
+        out_shape=[jax.ShapeDtypeStruct((chunks,) + shape, BF) for chunks in outs],
+        in_specs=in_vmem(2 + len(grads)),
+        out_specs=in_vmem(len(outs)),
         compiler_params=params(8),
         cost_estimate=cost(4 * groups * rows * inner * features, 4 * (groups * rows + inner) * features),
-    )(key_weight, value_weight, *grads, *extra)
+    )(key_weight, value_weight, *grads)
 
 
 def attention_kernel(chunks, q_ref, d_ref, *refs):
@@ -398,13 +450,13 @@
     d_output,
 ):
     index = relative_index()
-    features = key_weight.shape[0]
+    features, cols = key_weight.shape
     local = neighbour_states.shape[2]
     chunk = neighbour_states.shape[1] // ENC
     used = neighbour_slot.size
     slot_shard = neighbour_slot.reshape(-1) // SEQ
 
-    near = gather_short(stack([hidden, d_output]))
+    near = gather_short(join(hidden, d_output))
     arrived = lax.all_to_all(
         neighbour_states.reshape(SEQ * ENC, chunk, local), AXES, split_axis=0, concat_axis=0, tiled=True
     )
@@ -432,24 +484,31 @@
     context, d_queries, d_keys, d_values = attend(queries, d_context, keys, values)
     grads = {k: [d_keys[n], d_values[n]] for n, k in enumerate((0, 1, 3, 2))}
 
-    def pair(groups, extra, places, outs):
-        return pair_dots(sum((grads[k] for k in groups), []), key_weight, value_weight, extra, places, outs)
-
-    half, whole = grads[0][0].shape[0] // 2, grads[0][0].shape[0]
-    far_low, far_high = pair([2], [], (), 2)
-    from_low, from_high = move_v(far_low, 1), move_v(far_high, -1)
-    g3, g1 = pair([3, 1], [from_low, from_high], ((0, 0, half), (1, half, half)), 1)
+    both_terms = scatter_terms(context, d_queries, query_weight, output_weight)
+    far = pair_dots(grads[2], key_weight, value_weight, [2, 2])
+    from_low, from_high = move_v(far[0], 1), move_v(far[1], -1)
+    both_far = both_terms(index[2], [4, 4], far[0])
+    grads[3][0] = after(grads[3][0], *both_far)
+    rest = pair_dots(grads[3] + grads[1] + grads[0], key_weight, value_weight, [4, 4, 1, 1, 1, 1])
+    up, down = pass_on(rest[0], rest[1], from_low, from_high, *both_far)
+    from_up, from_down = move_v(up, 1), move_v(down, -1)
+    both_side = both_terms(jnp.concatenate([index[3], index[1]]), [8, 8], up)
+    g3, g1 = add_halves(*both_side, from_up, from_down)
+    both_near = both_terms(index[0], [2] * 4, g3)
     r3, r1 = move_v(g3, 1), move_v(g1, -1)
-    output, d_hidden, pieces = scatter_sums(index, context, d_queries, query_weight, output_weight, far_low)
-    summed = scatter_short(pair([0], [r3, r1], ((0, 0, whole), (0, 0, whole)), 4), *pieces)
+    pieces = add_pieces(rest[2:], from_up, from_down)
+    (summed,) = finish(pieces[0], *move_pieces(pieces))
+    both_pieces = add_pieces(both_near, after(r3, summed), r1)
+    output, d_hidden = finish(both_pieces[0], *move_pieces(both_pieces))
 
     placing = lax.broadcasted_iota(jnp.int32, (ENC, used), 0) == slot_shard[None, :]
-    spread = summed.reshape(used, chunk, SEQ, local).transpose(2, 0, 1, 3)
+    spread = summed.reshape(-1, used, chunk, cols // local, local).transpose(0, 3, 1, 2, 4)
+    spread = spread.reshape(SEQ, used, chunk, local)
     rank = jnp.argmax(placing, axis=1)
     spread = jnp.take(spread, rank, axis=1)
     spread = jnp.where(jnp.any(placing, axis=1)[None, :, None, None], spread, 0)
     back = lax.all_to_all(
-        spread.reshape(SEQ * ENC, chunk, local), AXES, split_axis=0, concat_axis=0, tiled=True
+        after(spread, *both_pieces).reshape(SEQ * ENC, chunk, local), AXES, split_axis=0, concat_axis=0, tiled=True
     )
     d_states = back.reshape(neighbour_states.shape)
     return (output, d_hidden, d_states)

time: 210 us -> 206 us (0.981)
  blocking collectives: 23 us -> 49.6 us
  starting transfers between devices: 49.9 us -> 31.2 us
  waiting for transfers between devices: 78.9 us -> 65.2 us
  Pallas kernels: 47.8 us -> 50.5 us
  other arithmetic: 3.65 us -> 1.15 us
    all_to_all x0 -> x1, blocking collectives: none -> 26.6 us  [on_device(): lax.all_to_all(after(spread, *both_pieces).reshape(SEQ * ENC, chunk, loca...]
    all_to_all x1 -> x0, waiting for transfers between devices: 14.1 us -> none  [on_device(): lax.all_to_all(spread.reshape(SEQ * ENC, chunk, local), AXES, split_axis=...]
    all_to_all x1 -> x0, starting transfers between devices: 10.8 us -> none  [on_device(): lax.all_to_all(spread.reshape(SEQ * ENC, chunk, local), AXES, split_axis=...]
    ppermute x12, waiting for transfers between devices: 12.8 us -> 19.2 us  [move_u(): return lax.ppermute(value, AXES, shift_table(False, shift))]
    ppermute x16 -> x14, waiting for transfers between devices: 52 us -> 46.1 us  [move_v(): return lax.ppermute(value, AXES, shift_table(True, shift))]
    ppermute x12, starting transfers between devices: 16.9 us -> 12.8 us  [move_u(): return lax.ppermute(value, AXES, shift_table(False, shift))]
    ppermute x16 -> x14, starting transfers between devices: 22.1 us -> 18.4 us  [move_v(): return lax.ppermute(value, AXES, shift_table(True, shift))]
    pallas_call x6 -> x12, Pallas kernels: 22.2 us -> 25 us  [the longest x3 12.5 us: call(): pl.pallas_call(functools.partial(terms_kernel, count), out_shape=[jax.Sha...]
  transfers between devices with their start and end apart: 29 -> 26, of which waited for: 12 -> 14; matrix products, arithmetic and copies ran while one was open for 2% -> 2% of each run, Pallas kernels for 18% -> 18%
where the time goes in v3:
time: 206 us; the launch traced here: 205 us
  waiting for transfers between devices  65.2 us (32%)
  Pallas kernels  50.5 us (25%)
  blocking collectives  49.6 us (24%)
  starting transfers between devices  31.2 us (15%)
  local copies, waits for them, and re-layouts  6.77 us (3%)
    ppermute x14, waiting for transfers between devices, move_v(): return lax.ppermute(value, AXES, shift_table(True, shift))  46.1 us
    all_to_all x1, blocking collectives, on_device(): lax.all_to_all(after(spread, *both_pieces).reshape(SEQ * ENC, chunk, loca...  26.6 us
    all_to_all x1, blocking collectives, on_device(): lax.all_to_all(neighbour_states.reshape(SEQ * ENC, chunk, local), AXES, s...  23 us
    ppermute x12, waiting for transfers between devices, move_u(): return lax.ppermute(value, AXES, shift_table(False, shift))  19.2 us
    ppermute x14, starting transfers between devices, move_v(): return lax.ppermute(value, AXES, shift_table(True, shift))  18.4 us
    pallas_call x3, Pallas kernels, gathered_dots(): pl.pallas_call(functools.partial(gathered_kernel, counts, start is not No...  14.5 us
    ppermute x12, starting transfers between devices, move_u(): return lax.ppermute(value, AXES, shift_table(False, shift))  12.8 us
    pallas_call x3, Pallas kernels, call(): pl.pallas_call(functools.partial(terms_kernel, count), out_shape=[jax.Sha...  12.5 us
  transfers between devices with their start and end apart: 26, of which 14 were waited for; matrix products, arithmetic and copies ran while one was open for 2% of the time, Pallas kernels for 18%

profile of v3, /device:TPU:1, one launch (start us, length us, event | category | flops | bytes accessed | tf_op | source)
XLA Modules:
  0.0 205.3 jit_solution(11921757575558609929)
XLA Ops:
  0.6 1.0 shard_map.103.refs_0_
  1.7 2.5 %collective-permute-start = (bf16[2,256,512]{2,1,0:T(8,128)(2,1)S(1)}, bf16[2,256,512]{2,1,0:T(8,128)(2,1)S(1)}, u32[]{:S(2)}, u32[]{:S(2)}) collective-permute-start(bf16[2,256,512]{2,1,0:T(8,128)(2,1)S(1)} %shard_map.103.refs_0_), channel_id=1, source_target_pairs={{0,1},{1,2},{2,3},{3,0},{4,5},{5,6},{6,7},{7,4},{8,9},{9,10},{10,1... | collective-permute-start | bytes 1572872 | tf_op jit(solution)/shard_map/ppermute | solution.py:42
  4.2 3.3 %collective-permute-start.1 = (bf16[2,256,512]{2,1,0:T(8,128)(2,1)S(1)}, bf16[2,256,512]{2,1,0:T(8,128)(2,1)S(1)}, u32[]{:S(2)}, u32[]{:S(2)}) collective-permute-start(bf16[2,256,512]{2,1,0:T(8,128)(2,1)S(1)} %shard_map.103.refs_0_), channel_id=1, source_target_pairs={{0,2},{1,3},{2,0},{3,1},{4,6},{5,7},{6,4},{7,5},{8,10},{9,11},{10,... | collective-permute-start | bytes 1572872 | tf_op jit(solution)/shard_map/ppermute | solution.py:42
  7.5 0.7 collective-permute-start.2
  8.3 23.0 %all_to_all.10 = bf16[128,8,256]{2,1,0:T(8,128)(2,1)S(1)} all-to-all(bf16[128,8,256]{2,1,0:T(8,128)(2,1)} %bitcast.32), channel_id=1, replica_groups=mesh['seq'=8,'enc'=16] {'seq','enc'}, dimensions={0} | all-to-all | bytes 1048576 | tf_op jit(solution)/shard_map/all_to_all | solution.py:460
  31.3 1.5 shard_map.104.refs_0_
  32.8 2.1 %collective-permute-start.3 = (bf16[4,2,256,512]{3,2,1,0:T(8,128)(2,1)}, bf16[4,2,256,512]{3,2,1,0:T(8,128)(2,1)S(1)}, u32[]{:S(2)}, u32[]{:S(2)}) collective-permute-start(bf16[4,2,256,512]{3,2,1,0:T(8,128)(2,1)} %shard_map.104.refs_0_), channel_id=1, source_target_pairs={{0,4},{1,5},{2,6},{3,7},{4,8},{5,9},{6,10},{7,11},{8,12},{9,13},{1... | collective-permute-start | bytes 6291464 | tf_op jit(solution)/shard_map/ppermute | solution.py:46
  34.9 0.6 collective-permute-start.4
  35.7 0.6 gather_fusion
  36.6 1.4 collective-permute-start.8
  38.0 1.6 collective-permute-start.9
  39.6 7.6 %collective-permute-done.7.refs_1_ = bf16[64,2048]{1,0:T(8,128)(2,1)S(1)} collective-permute-done((bf16[64,2048]{1,0:T(8,128)(2,1)S(1)}, bf16[64,2048]{1,0:T(8,128)(2,1)S(1)}, u32[]{:S(2)}, u32[]{:S(2)}) %collective-permute-start.7) | collective-permute-done | bytes 262176 | tf_op jit(solution)/shard_map/ppermute | solution.py:42
  47.3 3.3 %collective-permute-done.8.refs_2_ = bf16[64,2048]{1,0:T(8,128)(2,1)S(1)} collective-permute-done((bf16[64,2048]{1,0:T(8,128)(2,1)S(1)}, bf16[64,2048]{1,0:T(8,128)(2,1)S(1)}, u32[]{:S(2)}, u32[]{:S(2)}) %collective-permute-start.8) | collective-permute-done | bytes 262176 | tf_op jit(solution)/shard_map/ppermute | solution.py:42
  50.5 1.9 collective-permute-done.9.refs_3_
  52.5 1.0 collective-permute-start.10
  53.4 1.8 collective-permute-start.11
  55.3 4.6 %shard_map.106 = (f32[256,512]{1,0:T(8,128)S(1)}, f32[256,512]{1,0:T(8,128)S(1)}) custom-call(s32[4]{0:T(128)S(1)} %get-tuple-element.146.index_ref, bf16[8192,512]{1,0:T(8,128)(2,1)} %query_ref.11, bf16[512,8192]{1,0:T(8,128)(2,1)} %output_ref.11, bf16[4,2,256,512]{3,2,1,0:T(8,128)(2,1)} %shard_map.104.refs_0_), custom_call_target="tpu_custom_call" | custom-call | flops 1048576 | bytes 6144 | tf_op jit(solution)/shard_map/pallas_call | solution.py:211
  59.9 5.1 %collective-permute-done.3.one_ref.refs_0_ = bf16[4,2,256,512]{3,2,1,0:T(8,128)(2,1)S(1)} collective-permute-done((bf16[4,2,256,512]{3,2,1,0:T(8,128)(2,1)}, bf16[4,2,256,512]{3,2,1,0:T(8,128)(2,1)S(1)}, u32[]{:S(2)}, u32[]{:S(2)}) %collective-permute-start.3) | collective-permute-done | bytes 2097184 | tf_op jit(solution)/shard_map/ppermute | solution.py:46
  65.0 0.9 collective-permute-done.4.three_ref.refs_1_
  65.9 1.7 shard_map.105
  67.6 1.9 collective-permute-start.6
  69.5 1.2 shard_map.110
  70.8 5.4 %collective-permute-done.10.refs_0_.one_ref = bf16[4,64,2048]{2,1,0:T(8,128)(2,1)S(1)} collective-permute-done((bf16[4,64,2048]{2,1,0:T(8,128)(2,1)S(1)}, bf16[4,64,2048]{2,1,0:T(8,128)(2,1)S(1)}, u32[]{:S(2)}, u32[]{:S(2)}) %collective-permute-start.10) | collective-permute-done | bytes 1048608 | tf_op jit(solution)/shard_map/ppermute | solution.py:46
  76.2 0.9 collective-permute-done.11.refs_1_.three_ref
  77.2 6.3 %shard_map.107 = (f32[256,512]{1,0:T(8,128)S(1)}, f32[256,512]{1,0:T(8,128)S(1)}) custom-call(s32[8]{0:T(128)S(1)} %get-tuple-element.148.index_ref, bf16[8192,512]{1,0:T(8,128)(2,1)} %query_ref.11, bf16[512,8192]{1,0:T(8,128)(2,1)} %output_ref.11, bf16[4,2,256,512]{3,2,1,0:T(8,128)(2,1)S(1)} %collective-permute-done.3.one_ref.refs_0_, ...), custom_call_target="tpu_custom_call" | custom-call | flops 2097152 | bytes 12288 | tf_op jit(solution)/shard_map/pallas_call | solution.py:211
  83.7 2.5 %collective-permute-start.13 = (bf16[2,64,2048]{2,1,0:T(8,128)(2,1)S(1)}, bf16[2,64,2048]{2,1,0:T(8,128)(2,1)S(1)}, u32[]{:S(2)}, u32[]{:S(2)}) collective-permute-start(bf16[2,64,2048]{2,1,0:T(8,128)(2,1)S(1)} %get-tuple-element.91), channel_id=1, source_target_pairs={{0,12},{1,13},{2,14},{3,15},{4,0},{5,1},{6,2},{7,3},{8,4},{9,5},{1... | collective-permute-start | bytes 1572872 | tf_op jit(solution)/shard_map/ppermute | solution.py:46
  86.2 2.3 %shard_map.111 = (bf16[512,512]{1,0:T(8,128)(2,1)S(1)}, bf16[512,512]{1,0:T(8,128)(2,1)S(1)}) custom-call(bf16[2048,512]{1,0:T(8,128)(2,1)S(1)} %copy-done, bf16[2048,512]{1,0:T(8,128)(2,1)S(1)} %copy-done.1, bf16[4,64,2048]{2,1,0:T(8,128)(2,1)S(1)} %collective-permute-done.10.refs_0_.one_ref, bf16[4,64,2048]{2,1,0:T(8,128)(2,1)S(1)} %collective-permute-done.11.refs_1_.three_ref), custom_call_target="tpu_custom_call" | custom-call | flops 2097152 | bytes 8192 | tf_op jit(solution)/shard_map/pallas_call | solution.py:347
  88.5 3.7 %shard_map.108 = (bf16[256,512]{1,0:T(8,128)(2,1)S(1)}, bf16[256,512]{1,0:T(8,128)(2,1)S(1)}) custom-call(s32[4]{0:T(128)S(1)} %get-tuple-element.145.index_ref, bf16[8192,512]{1,0:T(8,128)(2,1)} %query_ref.11, bf16[512,8192]{1,0:T(8,128)(2,1)} %output_ref.11, bf16[2,2,256,512]{3,2,1,0:T(8,128)(2,1)S(1)} %collective-permute-done.5.refs_0_, ...), custom_call_target="tpu_custom_call" | custom-call | flops 1048576 | bytes 6144 | tf_op jit(solution)/shard_map/pallas_call | solution.py:211
  92.2 0.8 collective-permute-done.12.refs_0_
  93.1 0.9 collective-permute-done.13.refs_1_
  94.0 1.3 shard_map.113
  95.2 2.8 %shard_map.114 = (bf16[256,512]{1,0:T(8,128)(2,1)S(1)}, bf16[256,512]{1,0:T(8,128)(2,1)S(1)}, bf16[256,512]{1,0:T(8,128)(2,1)S(1)}, bf16[256,512]{1,0:T(8,128)(2...) custom-call(bf16[256,512]{1,0:T(8,128)(2,1)S(1)} %get-tuple-element., ...), custom_call_target="tpu_custom_call" | custom-call | flops 393216 | bytes 10240 | tf_op jit(solution)/shard_map/pallas_call | solution.py:431
  98.0 1.3 shard_map.115
  99.5 2.5 %collective-permute-start.15 = (bf16[2,256,512]{2,1,0:T(8,128)(2,1)S(1)}, bf16[2,256,512]{2,1,0:T(8,128)(2,1)S(1)}, u32[]{:S(2)}, u32[]{:S(2)}) collective-permute-start(bf16[2,256,512]{2,1,0:T(8,128)(2,1)S(1)} %get-tuple-element.111), channel_id=1, source_target_pairs={{0,12},{1,13},{2,14},{3,15},{4,0},{5,1},{6,2},{7,3},{8,4},{9,5},{1... | collective-permute-start | bytes 1572872 | tf_op jit(solution)/shard_map/ppermute | solution.py:46
  102.0 3.6 %shard_map.116 = (bf16[4,256,512]{2,1,0:T(8,128)(2,1)S(1)}, bf16[4,256,512]{2,1,0:T(8,128)(2,1)S(1)}) custom-call(s32[4]{0:T(128)S(1)} %get-tuple-element.145.index_ref, bf16[8192,512]{1,0:T(8,128)(2,1)} %query_ref.11, bf16[512,8192]{1,0:T(8,128)(2,1)} %output_ref.11, bf16[256,512]{1,0:T(8,128)(2,1)S(1)} %get-tuple-element.118.c_ref, ...), custom_call_target="tpu_custom_call" | custom-call | flops 1048576 | bytes 8192 | tf_op jit(solution)/shard_map/pallas_call | solution.py:239
  105.6 3.5 %shard_map.117 = (bf16[4,256,512]{2,1,0:T(8,128)(2,1)S(1)}, bf16[4,256,512]{2,1,0:T(8,128)(2,1)S(1)}, bf16[1,256,512]{2,1,0:T(8,128)(2,1)S(1)}, bf16[1,256,512]{...) custom-call(bf16[2048,512]{1,0:T(8,128)(2,1)S(1)} %copy-done, ...), custom_call_target="tpu_custom_call" | custom-call | flops 3145728 | bytes 10240 | tf_op jit(solution)/shard_map/pallas_call | solution.py:376
  109.1 0.4 shard_map.118
  109.5 2.8 %collective-permute-start.17 = (bf16[8,256,512]{2,1,0:T(8,128)(2,1)S(1)}, bf16[8,256,512]{2,1,0:T(8,128)(2,1)S(1)}, u32[]{:S(2)}, u32[]{:S(2)}) collective-permute-start(bf16[8,256,512]{2,1,0:T(8,128)(2,1)S(1)} %get-tuple-element.116), channel_id=1, source_target_pairs={{0,12},{1,13},{2,14},{3,15},{4,0},{5,1},{6,2},{7,3},{8,4},{9,5},{1... | collective-permute-start | bytes 6291464 | tf_op jit(solution)/shard_map/ppermute | solution.py:46
  112.3 5.3 %shard_map.119 = (bf16[8,256,512]{2,1,0:T(8,128)(2,1)S(1)}, bf16[8,256,512]{2,1,0:T(8,128)(2,1)S(1)}) custom-call(s32[8]{0:T(128)S(1)} %get-tuple-element.147.index_ref, bf16[8192,512]{1,0:T(8,128)(2,1)} %query_ref.11, bf16[512,8192]{1,0:T(8,128)(2,1)} %output_ref.11, bf16[256,512]{1,0:T(8,128)(2,1)S(1)} %get-tuple-element.118.c_ref, ...), custom_call_target="tpu_custom_call" | custom-call | flops 2097152 | bytes 16384 | tf_op jit(solution)/shard_map/pallas_call | solution.py:239
  117.6 18.3 %collective-permute-done.16.up_ref.refs_4_ = bf16[8,256,512]{2,1,0:T(8,128)(2,1)S(1)} collective-permute-done((bf16[8,256,512]{2,1,0:T(8,128)(2,1)S(1)}, bf16[8,256,512]{2,1,0:T(8,128)(2,1)S(1)}, u32[]{:S(2)}, u32[]{:S(2)}) %collective-permute-start.16) | collective-permute-done | bytes 2097184 | tf_op jit(solution)/shard_map/ppermute | solution.py:46
  135.9 2.5 %shard_map.120 = (bf16[8,256,512]{2,1,0:T(8,128)(2,1)}, bf16[8,256,512]{2,1,0:T(8,128)(2,1)}) custom-call(bf16[8,256,512]{2,1,0:T(8,128)(2,1)S(1)} %get-tuple-element.114.g3_ref, bf16[8,256,512]{2,1,0:T(8,128)(2,1)S(1)} %get-tuple-element.115.g1_ref, bf16[8,256,512]{2,1,0:T(8,128)(2,1)S(1)} %collective-permute-done.16.up_ref.refs_4_, ...), custom_call_target="tpu_custom_call" | custom-call | flops 1024 | bytes 4096 | tf_op jit(solution)/shard_map/pallas_call | solution.py:287
  138.5 0.7 collective-permute-start.18
  139.1 2.1 %collective-permute-start.22 = (bf16[8,256,512]{2,1,0:T(8,128)(2,1)}, bf16[8,256,512]{2,1,0:T(8,128)(2,1)}, u32[]{:S(2)}, u32[]{:S(2)}) collective-permute-start(bf16[8,256,512]{2,1,0:T(8,128)(2,1)} %get-tuple-element.132), channel_id=1, source_target_pairs={{0,12},{1,13},{2,14},{3,15},{4,0},{5,1},{6,2},{7,3},{8,4},{9,5},{1... | collective-permute-start | bytes 6291464 | tf_op jit(solution)/shard_map/ppermute | solution.py:46
  141.3 0.6 iota_reduce_fusion
  141.9 0.4 shard_map.122
  142.5 0.7 collective-permute-start.20
  143.2 0.6 collective-permute-start.21
  143.9 3.6 %shard_map.121 = (bf16[2,256,512]{2,1,0:T(8,128)(2,1)S(1)}, bf16[2,256,512]{2,1,0:T(8,128)(2,1)S(1)}, bf16[2,256,512]{2,1,0:T(8,128)(2,1)S(1)}, bf16[2,256,512]{2,1,0:T(8,128)(2,1)S(1)}) custom-call(s32[4]{0:T(128)S(1)} %get-tuple-element.146.index_ref, bf16[8192,512]{1,0:T(8,128)(2,1)} %query_ref.11, bf16[512,8192]{1,0:T(8,128)(2,1)} %output_ref.11, ...), custom_call_target="tpu_custom_call" | custom-call | flops 1048576 | bytes 8192 | tf_op jit(solution)/shard_map/pallas_call | solution.py:239
  147.5 0.8 copy-done.2
  148.3 0.8 copy-done.4
  149.0 0.6 collective-permute-done.19.refs_1_
  149.7 2.1 %collective-permute-done.20.refs_2_ = bf16[1,256,512]{2,1,0:T(8,128)(2,1)S(1)} collective-permute-done((bf16[1,256,512]{2,1,0:T(8,128)(2,1)S(1)}, bf16[1,256,512]{2,1,0:T(8,128)(2,1)S(1)}, u32[]{:S(2)}, u32[]{:S(2)}) %collective-permute-start.20) | collective-permute-done | bytes 262176 | tf_op jit(solution)/shard_map/ppermute | solution.py:42
  151.7 3.7 %collective-permute-done.21.refs_3_ = bf16[1,256,512]{2,1,0:T(8,128)(2,1)S(1)} collective-permute-done((bf16[1,256,512]{2,1,0:T(8,128)(2,1)S(1)}, bf16[1,256,512]{2,1,0:T(8,128)(2,1)S(1)}, u32[]{:S(2)}, u32[]{:S(2)}) %collective-permute-start.21) | collective-permute-done | bytes 262176 | tf_op jit(solution)/shard_map/ppermute | solution.py:42
  155.6 1.4 gather_fusion.1
  157.0 13.8 %collective-permute-done.18.refs_4_ = bf16[8,256,512]{2,1,0:T(8,128)(2,1)S(1)} collective-permute-done((bf16[8,256,512]{2,1,0:T(8,128)(2,1)}, bf16[8,256,512]{2,1,0:T(8,128)(2,1)S(1)}, u32[]{:S(2)}, u32[]{:S(2)}) %collective-permute-start.18) | collective-permute-done | bytes 2097184 | tf_op jit(solution)/shard_map/ppermute | solution.py:46
  170.8 1.0 copy-done.3
  171.8 1.0 copy-done.5
  172.9 2.4 %shard_map.124 = (bf16[2,256,512]{2,1,0:T(8,128)(2,1)S(1)}, bf16[2,256,512]{2,1,0:T(8,128)(2,1)S(1)}, bf16[2,256,512]{2,1,0:T(8,128)(2,1)S(1)}, bf16[2,256,512]{2,1,0:T(8,128)(2,1)S(1)}) custom-call(bf16[2,256,512]{2,1,0:T(8,128)(2,1)S(1)} %get-tuple-element.119.refs_0_, bf16[2,256,512]{2,1,0:T(8,128)(2,1)S(1)} %get-tuple-element.120.refs_1_, ...), custom_call_target="tpu_custom_call" | custom-call | flops 8192 | bytes 8192 | tf_op jit(solution)/shard_map/pallas_call | solution.py:306
  175.3 0.3 collective-permute-start.23
  175.6 0.3 collective-permute-start.24
  175.9 0.9 collective-permute-start.25
  177.0 26.6 %all_to_all.11 = bf16[128,8,256]{2,1,0:T(8,128)(2,1)S(1)} all-to-all(bf16[128,8,256]{2,1,0:T(8,128)(2,1)S(1)} %bitcast.30), channel_id=1, replica_groups=mesh['seq'=8,'enc'=16] {'seq','enc'}, dimensions={0} | all-to-all | bytes 1048576 | tf_op jit(solution)/shard_map/all_to_all | solution.py:510
  203.6 1.0 shard_map.125
  204.5 0.8 copy.25
  (53 shorter events, 2.2 us)
Async XLA Ops:
  1.7 29.6 %collective-permute-start = (bf16[2,256,512]{2,1,0:T(8,128)(2,1)S(1)}, bf16[2,256,512]{2,1,0:T(8,128)(2,1)S(1)}, u32[]{:S(2)}, u32[]{:S(2)}) collective-permute-start(bf16[2,256,512]{2,1,0:T(8,128)(2,1)S(1)} %shard_map.103.refs_0_), channel_id=1, source_target_pairs={{0,1},{1,2},{2,3},{3,0},{4,5},{5,6},{6,7},{7,4},{8,9},{9,10},{10,1... | collective-permute-start | bytes 1572872 | tf_op jit(solution)/shard_map/ppermute | solution.py:42
  4.2 27.0 %collective-permute-start.1 = (bf16[2,256,512]{2,1,0:T(8,128)(2,1)S(1)}, bf16[2,256,512]{2,1,0:T(8,128)(2,1)S(1)}, u32[]{:S(2)}, u32[]{:S(2)}) collective-permute-start(bf16[2,256,512]{2,1,0:T(8,128)(2,1)S(1)} %shard_map.103.refs_0_), channel_id=1, source_target_pairs={{0,2},{1,3},{2,0},{3,1},{4,6},{5,7},{6,4},{7,5},{8,10},{9,11},{10,... | collective-permute-start | bytes 1572872 | tf_op jit(solution)/shard_map/ppermute | solution.py:42
  7.5 23.7 %collective-permute-start.2 = (bf16[2,256,512]{2,1,0:T(8,128)(2,1)S(1)}, bf16[2,256,512]{2,1,0:T(8,128)(2,1)S(1)}, u32[]{:S(2)}, u32[]{:S(2)}) collective-permute-start(bf16[2,256,512]{2,1,0:T(8,128)(2,1)S(1)} %shard_map.103.refs_0_), channel_id=1, source_target_pairs={{0,3},{1,0},{2,1},{3,2},{4,7},{5,4},{6,5},{7,6},{8,11},{9,8},{10,9... | collective-permute-start | bytes 1572872 | tf_op jit(solution)/shard_map/ppermute | solution.py:42
  31.2 4.2 %copy-start.7 = (s32[4,2]{0,1:T(2,128)S(1)}, s32[4,2]{0,1:T(2,128)}, u32[]{:S(2)}) copy-start(s32[4,2]{0,1:T(2,128)} %param.14) | copy-start | bytes 100
  32.8 32.2 %collective-permute-start.3 = (bf16[4,2,256,512]{3,2,1,0:T(8,128)(2,1)}, bf16[4,2,256,512]{3,2,1,0:T(8,128)(2,1)S(1)}, u32[]{:S(2)}, u32[]{:S(2)}) collective-permute-start(bf16[4,2,256,512]{3,2,1,0:T(8,128)(2,1)} %shard_map.104.refs_0_), channel_id=1, source_target_pairs={{0,4},{1,5},{2,6},{3,7},{4,8},{5,9},{6,10},{7,11},{8,12},{9,13},{1... | collective-permute-start | bytes 6291464 | tf_op jit(solution)/shard_map/ppermute | solution.py:46
  34.9 31.0 %collective-permute-start.4 = (bf16[4,2,256,512]{3,2,1,0:T(8,128)(2,1)}, bf16[4,2,256,512]{3,2,1,0:T(8,128)(2,1)}, u32[]{:S(2)}, u32[]{:S(2)}) collective-permute-start(bf16[4,2,256,512]{3,2,1,0:T(8,128)(2,1)} %shard_map.104.refs_0_), channel_id=1, source_target_pairs={{0,12},{1,13},{2,14},{3,15},{4,0},{5,1},{6,2},{7,3},{8,4},{9,5},{1... | collective-permute-start | bytes 6291464 | tf_op jit(solution)/shard_map/ppermute | solution.py:46
  36.4 10.8 %collective-permute-start.7 = (bf16[64,2048]{1,0:T(8,128)(2,1)S(1)}, bf16[64,2048]{1,0:T(8,128)(2,1)S(1)}, u32[]{:S(2)}, u32[]{:S(2)}) collective-permute-start(bf16[64,2048]{1,0:T(8,128)(2,1)S(1)} %bitcast.24), channel_id=1, source_target_pairs={{0,1},{1,2},{2,3},{3,0},{4,5},{5,6},{6,7},{7,4},{8,9},{9,10},{10,1... | collective-permute-start | bytes 786440 | tf_op jit(solution)/shard_map/ppermute | solution.py:42
  36.6 13.9 %collective-permute-start.8 = (bf16[64,2048]{1,0:T(8,128)(2,1)S(1)}, bf16[64,2048]{1,0:T(8,128)(2,1)S(1)}, u32[]{:S(2)}, u32[]{:S(2)}) collective-permute-start(bf16[64,2048]{1,0:T(8,128)(2,1)S(1)} %bitcast.25), channel_id=1, source_target_pairs={{0,2},{1,3},{2,0},{3,1},{4,6},{5,7},{6,4},{7,5},{8,10},{9,11},{10,... | collective-permute-start | bytes 786440 | tf_op jit(solution)/shard_map/ppermute | solution.py:42
  38.0 14.4 %collective-permute-start.9 = (bf16[64,2048]{1,0:T(8,128)(2,1)S(1)}, bf16[64,2048]{1,0:T(8,128)(2,1)S(1)}, u32[]{:S(2)}, u32[]{:S(2)}) collective-permute-start(bf16[64,2048]{1,0:T(8,128)(2,1)S(1)} %bitcast.26), channel_id=1, source_target_pairs={{0,3},{1,0},{2,1},{3,2},{4,7},{5,4},{6,5},{7,6},{8,11},{9,8},{10,9... | collective-permute-start | bytes 786440 | tf_op jit(solution)/shard_map/ppermute | solution.py:42
  52.5 23.7 %collective-permute-start.10 = (bf16[4,64,2048]{2,1,0:T(8,128)(2,1)S(1)}, bf16[4,64,2048]{2,1,0:T(8,128)(2,1)S(1)}, u32[]{:S(2)}, u32[]{:S(2)}) collective-permute-start(bf16[4,64,2048]{2,1,0:T(8,128)(2,1)S(1)} %shard_map.109.refs_0_), channel_id=1, source_target_pairs={{0,4},{1,5},{2,6},{3,7},{4,8},{5,9},{6,10},{7,11},{8,12},{9,13},{1... | collective-permute-start | bytes 3145736 | tf_op jit(solution)/shard_map/ppermute | solution.py:46
  53.4 23.7 %collective-permute-start.11 = (bf16[4,64,2048]{2,1,0:T(8,128)(2,1)S(1)}, bf16[4,64,2048]{2,1,0:T(8,128)(2,1)S(1)}, u32[]{:S(2)}, u32[]{:S(2)}) collective-permute-start(bf16[4,64,2048]{2,1,0:T(8,128)(2,1)S(1)} %shard_map.109.refs_0_), channel_id=1, source_target_pairs={{0,12},{1,13},{2,14},{3,15},{4,0},{5,1},{6,2},{7,3},{8,4},{9,5},{1... | collective-permute-start | bytes 3145736 | tf_op jit(solution)/shard_map/ppermute | solution.py:46
  59.9 9.7 %copy-start = (bf16[2048,512]{1,0:T(8,128)(2,1)S(1)}, bf16[2048,512]{1,0:T(8,128)(2,1)}, u32[]{:S(2)}) copy-start(bf16[2048,512]{1,0:T(8,128)(2,1)} %key_ref.9) | copy-start | bytes 6291460
  59.9 9.7 %copy-start.1 = (bf16[2048,512]{1,0:T(8,128)(2,1)S(1)}, bf16[2048,512]{1,0:T(8,128)(2,1)}, u32[]{:S(2)}) copy-start(bf16[2048,512]{1,0:T(8,128)(2,1)} %value_ref.9) | copy-start | bytes 6291460
  67.6 20.9 %collective-permute-start.6 = (bf16[2,2,256,512]{3,2,1,0:T(8,128)(2,1)S(1)}, bf16[2,2,256,512]{3,2,1,0:T(8,128)(2,1)S(1)}, u32[]{:S(2)}, u32[]{:S(2)}) collective-permute-start(bf16[2,2,256,512]{3,2,1,0:T(8,128)(2,1)S(1)} %get-tuple-element.78), channel_id=1, source_target_pairs={{0,12},{1,13},{2,14},{3,15},{4,0},{5,1},{6,2},{7,3},{8,4},{9,5},{1... | collective-permute-start | bytes 3145736 | tf_op jit(solution)/shard_map/ppermute | solution.py:46
  69.5 19.1 %collective-permute-start.5 = (bf16[2,2,256,512]{3,2,1,0:T(8,128)(2,1)S(1)}, bf16[2,2,256,512]{3,2,1,0:T(8,128)(2,1)S(1)}, u32[]{:S(2)}, u32[]{:S(2)}) collective-permute-start(bf16[2,2,256,512]{3,2,1,0:T(8,128)(2,1)S(1)} %get-tuple-element.76), channel_id=1, source_target_pairs={{0,4},{1,5},{2,6},{3,7},{4,8},{5,9},{6,10},{7,11},{8,12},{9,13},{1... | collective-permute-start | bytes 3145736 | tf_op jit(solution)/shard_map/ppermute | solution.py:46
  83.4 9.6 %collective-permute-start.12 = (bf16[2,64,2048]{2,1,0:T(8,128)(2,1)S(1)}, bf16[2,64,2048]{2,1,0:T(8,128)(2,1)S(1)}, u32[]{:S(2)}, u32[]{:S(2)}) collective-permute-start(bf16[2,64,2048]{2,1,0:T(8,128)(2,1)S(1)} %get-tuple-element.87), channel_id=1, source_target_pairs={{0,4},{1,5},{2,6},{3,7},{4,8},{5,9},{6,10},{7,11},{8,12},{9,13},{1... | collective-permute-start | bytes 1572872 | tf_op jit(solution)/shard_map/ppermute | solution.py:46
  83.7 10.3 %collective-permute-start.13 = (bf16[2,64,2048]{2,1,0:T(8,128)(2,1)S(1)}, bf16[2,64,2048]{2,1,0:T(8,128)(2,1)S(1)}, u32[]{:S(2)}, u32[]{:S(2)}) collective-permute-start(bf16[2,64,2048]{2,1,0:T(8,128)(2,1)S(1)} %get-tuple-element.91), channel_id=1, source_target_pairs={{0,12},{1,13},{2,14},{3,15},{4,0},{5,1},{6,2},{7,3},{8,4},{9,5},{1... | collective-permute-start | bytes 1572872 | tf_op jit(solution)/shard_map/ppermute | solution.py:46
  99.3 9.8 %collective-permute-start.14 = (bf16[2,256,512]{2,1,0:T(8,128)(2,1)S(1)}, bf16[2,256,512]{2,1,0:T(8,128)(2,1)S(1)}, u32[]{:S(2)}, u32[]{:S(2)}) collective-permute-start(bf16[2,256,512]{2,1,0:T(8,128)(2,1)S(1)} %get-tuple-element.98), channel_id=1, source_target_pairs={{0,4},{1,5},{2,6},{3,7},{4,8},{5,9},{6,10},{7,11},{8,12},{9,13},{1... | collective-permute-start | bytes 1572872 | tf_op jit(solution)/shard_map/ppermute | solution.py:46
  99.5 9.5 %collective-permute-start.15 = (bf16[2,256,512]{2,1,0:T(8,128)(2,1)S(1)}, bf16[2,256,512]{2,1,0:T(8,128)(2,1)S(1)}, u32[]{:S(2)}, u32[]{:S(2)}) collective-permute-start(bf16[2,256,512]{2,1,0:T(8,128)(2,1)S(1)} %get-tuple-element.111), channel_id=1, source_target_pairs={{0,12},{1,13},{2,14},{3,15},{4,0},{5,1},{6,2},{7,3},{8,4},{9,5},{1... | collective-permute-start | bytes 1572872 | tf_op jit(solution)/shard_map/ppermute | solution.py:46
  109.5 26.5 %collective-permute-start.16 = (bf16[8,256,512]{2,1,0:T(8,128)(2,1)S(1)}, bf16[8,256,512]{2,1,0:T(8,128)(2,1)S(1)}, u32[]{:S(2)}, u32[]{:S(2)}) collective-permute-start(bf16[8,256,512]{2,1,0:T(8,128)(2,1)S(1)} %get-tuple-element.112), channel_id=1, source_target_pairs={{0,4},{1,5},{2,6},{3,7},{4,8},{5,9},{6,10},{7,11},{8,12},{9,13},{1... | collective-permute-start | bytes 6291464 | tf_op jit(solution)/shard_map/ppermute | solution.py:46
  109.5 26.4 %collective-permute-start.17 = (bf16[8,256,512]{2,1,0:T(8,128)(2,1)S(1)}, bf16[8,256,512]{2,1,0:T(8,128)(2,1)S(1)}, u32[]{:S(2)}, u32[]{:S(2)}) collective-permute-start(bf16[8,256,512]{2,1,0:T(8,128)(2,1)S(1)} %get-tuple-element.116), channel_id=1, source_target_pairs={{0,12},{1,13},{2,14},{3,15},{4,0},{5,1},{6,2},{7,3},{8,4},{9,5},{1... | collective-permute-start | bytes 6291464 | tf_op jit(solution)/shard_map/ppermute | solution.py:46
  138.5 32.3 %collective-permute-start.18 = (bf16[8,256,512]{2,1,0:T(8,128)(2,1)}, bf16[8,256,512]{2,1,0:T(8,128)(2,1)S(1)}, u32[]{:S(2)}, u32[]{:S(2)}) collective-permute-start(bf16[8,256,512]{2,1,0:T(8,128)(2,1)} %get-tuple-element.117), channel_id=1, source_target_pairs={{0,4},{1,5},{2,6},{3,7},{4,8},{5,9},{6,10},{7,11},{8,12},{9,13},{1... | collective-permute-start | bytes 6291464 | tf_op jit(solution)/shard_map/ppermute | solution.py:46
  139.1 31.7 %collective-permute-start.22 = (bf16[8,256,512]{2,1,0:T(8,128)(2,1)}, bf16[8,256,512]{2,1,0:T(8,128)(2,1)}, u32[]{:S(2)}, u32[]{:S(2)}) collective-permute-start(bf16[8,256,512]{2,1,0:T(8,128)(2,1)} %get-tuple-element.132), channel_id=1, source_target_pairs={{0,12},{1,13},{2,14},{3,15},{4,0},{5,1},{6,2},{7,3},{8,4},{9,5},{1... | collective-permute-start | bytes 6291464 | tf_op jit(solution)/shard_map/ppermute | solution.py:46
  142.3 7.3 %collective-permute-start.19 = (bf16[1,256,512]{2,1,0:T(8,128)(2,1)S(1)}, bf16[1,256,512]{2,1,0:T(8,128)(2,1)S(1)}, u32[]{:S(2)}, u32[]{:S(2)}) collective-permute-start(bf16[1,256,512]{2,1,0:T(8,128)(2,1)S(1)} %get-tuple-element.128), channel_id=1, source_target_pairs={{0,3},{1,0},{2,1},{3,2},{4,7},{5,4},{6,5},{7,6},{8,11},{9,8},{10,9... | collective-permute-start | bytes 786440 | tf_op jit(solution)/shard_map/ppermute | solution.py:42
  142.5 9.2 %collective-permute-start.20 = (bf16[1,256,512]{2,1,0:T(8,128)(2,1)S(1)}, bf16[1,256,512]{2,1,0:T(8,128)(2,1)S(1)}, u32[]{:S(2)}, u32[]{:S(2)}) collective-permute-start(bf16[1,256,512]{2,1,0:T(8,128)(2,1)S(1)} %get-tuple-element.129), channel_id=1, source_target_pairs={{0,2},{1,3},{2,0},{3,1},{4,6},{5,7},{6,4},{7,5},{8,10},{9,11},{10,... | collective-permute-start | bytes 786440 | tf_op jit(solution)/shard_map/ppermute | solution.py:42
  143.2 12.2 %collective-permute-start.21 = (bf16[1,256,512]{2,1,0:T(8,128)(2,1)S(1)}, bf16[1,256,512]{2,1,0:T(8,128)(2,1)S(1)}, u32[]{:S(2)}, u32[]{:S(2)}) collective-permute-start(bf16[1,256,512]{2,1,0:T(8,128)(2,1)S(1)} %get-tuple-element.130), channel_id=1, source_target_pairs={{0,1},{1,2},{2,3},{3,0},{4,5},{5,6},{6,7},{7,4},{8,9},{9,10},{10,1... | collective-permute-start | bytes 786440 | tf_op jit(solution)/shard_map/ppermute | solution.py:42
  147.5 0.8 copy-start.2
  148.2 0.8 copy-start.4
  170.8 1.0 copy-start.3
  171.8 1.0 copy-start.5
  172.9 3.9 %copy-start.6 = (bf16[16,8,8,256]{3,2,1,0:T(8,128)(2,1)S(1)}, bf16[16,8,8,256]{3,2,1,0:T(8,128)(2,1)}, u32[]{:S(2)}) copy-start(bf16[16,8,8,256]{3,2,1,0:T(8,128)(2,1)} %gather_fusion.1) | copy-start | bytes 1572868
  175.3 28.3 %collective-permute-start.23 = (bf16[2,256,512]{2,1,0:T(8,128)(2,1)S(1)}, bf16[2,256,512]{2,1,0:T(8,128)(2,1)S(1)}, u32[]{:S(2)}, u32[]{:S(2)}) collective-permute-start(bf16[2,256,512]{2,1,0:T(8,128)(2,1)S(1)} %get-tuple-element.134), channel_id=1, source_target_pairs={{0,3},{1,0},{2,1},{3,2},{4,7},{5,4},{6,5},{7,6},{8,11},{9,8},{10,9... | collective-permute-start | bytes 1572872 | tf_op jit(solution)/shard_map/ppermute | solution.py:42
  175.6 28.0 %collective-permute-start.24 = (bf16[2,256,512]{2,1,0:T(8,128)(2,1)S(1)}, bf16[2,256,512]{2,1,0:T(8,128)(2,1)S(1)}, u32[]{:S(2)}, u32[]{:S(2)}) collective-permute-start(bf16[2,256,512]{2,1,0:T(8,128)(2,1)S(1)} %get-tuple-element.135), channel_id=1, source_target_pairs={{0,2},{1,3},{2,0},{3,1},{4,6},{5,7},{6,4},{7,5},{8,10},{9,11},{10,... | collective-permute-start | bytes 1572872 | tf_op jit(solution)/shard_map/ppermute | solution.py:42
  175.9 27.7 %collective-permute-start.25 = (bf16[2,256,512]{2,1,0:T(8,128)(2,1)S(1)}, bf16[2,256,512]{2,1,0:T(8,128)(2,1)S(1)}, u32[]{:S(2)}, u32[]{:S(2)}) collective-permute-start(bf16[2,256,512]{2,1,0:T(8,128)(2,1)S(1)} %get-tuple-element.136), channel_id=1, source_target_pairs={{0,1},{1,2},{2,3},{3,0},{4,5},{5,6},{6,7},{7,4},{8,9},{9,10},{10,1... | collective-permute-start | bytes 1572872 | tf_op jit(solution)/shard_map/ppermute | solution.py:42

commit v4 on v3

--- a/solution.py
+++ b/solution.py
@@ -98,12 +98,13 @@
 
 
 def halves_kernel(one_ref, three_ref, low_ref, high_ref):
-    low_ref[...] = one_ref[:2]
-    high_ref[...] = three_ref[2:]
+    half = low_ref.shape[0]
+    low_ref[...] = one_ref[:half]
+    high_ref[...] = three_ref[half:]
 
 
 def halves(one, three):
-    half = jax.ShapeDtypeStruct((2,) + one.shape[1:], BF)
+    half = jax.ShapeDtypeStruct((one.shape[0] // 2,) + one.shape[1:], BF)
     return pl.pallas_call(
         halves_kernel,
         out_shape=[half, half],
@@ -116,6 +117,29 @@
 
 def gather_short(own):
     return [own, move_u(own, 1), move_u(own, 2), move_u(own, -1)]
+
+
+def ring_kernel(own_ref, one_ref, low_ref, high_ref, three_ref, out_ref):
+    out_ref[0] = own_ref[...]
+    out_ref[1] = one_ref[...]
+    out_ref[2, :1] = low_ref[...]
+    out_ref[2, 1:] = high_ref[...]
+    out_ref[3] = three_ref[...]
+
+
+def gather_ring(own):
+    own = own.reshape((2, own.shape[0] // 2) + own.shape[1:])
+    one, three = move_u(own, 1), move_u(own, -1)
+    low, high = halves(one, three)
+    group = pl.pallas_call(
+        ring_kernel,
+        out_shape=jax.ShapeDtypeStruct((SIDE,) + own.shape, BF),
+        in_specs=in_vmem(5),
+        out_specs=pl.BlockSpec(memory_space=pltpu.VMEM),
+        compiler_params=params(8),
+        cost_estimate=cost(0, 16 * own.size),
+    )(own, one, move_u(low, 1), move_u(high, -1), three)
+    return group.reshape(SIDE, 2 * own.shape[1], own.shape[2])
 
 
 def gather_long(group):
@@ -275,23 +299,22 @@
     )(g3, g1, low, high, far_low, far_high)
 
 
-def add_halves_kernel(g3_ref, g1_ref, up_ref, down_ref, out3_ref, out1_ref):
+def add_half_kernel(first, x_ref, part_ref, out_ref):
     for n in range(4):
-        out3_ref[n] = plus(g3_ref[n], up_ref[n + 4])
-        out3_ref[n + 4] = g3_ref[n + 4]
-        out1_ref[n] = g1_ref[n]
-        out1_ref[n + 4] = plus(g1_ref[n + 4], down_ref[n + 4])
-
-
-def add_halves(g3, g1, up, down):
-    return pl.pallas_call(
-        add_halves_kernel,
-        out_shape=[jax.ShapeDtypeStruct(g3.shape, BF)] * 2,
-        in_specs=in_vmem(4),
-        out_specs=in_vmem(2),
-        compiler_params=params(8),
-        cost_estimate=cost(g3.size, 4 * g3.size),
-    )(g3, g1, up, down)
+        at, other = (n, n + 4) if first else (n + 4, n)
+        out_ref[at] = plus(x_ref[at], part_ref[n + 4])
+        out_ref[other] = x_ref[other]
+
+
+def add_half(x, part, first):
+    return pl.pallas_call(
+        functools.partial(add_half_kernel, first),
+        out_shape=jax.ShapeDtypeStruct(x.shape, BF),
+        in_specs=in_vmem(2),
+        out_specs=pl.BlockSpec(memory_space=pltpu.VMEM),
+        compiler_params=params(8),
+        cost_estimate=cost(x.size, 4 * x.size),
+    )(x, part)
 
 
 def add_pieces_kernel(*refs):
@@ -465,7 +488,7 @@
     arrived = arrived.reshape(SEQ, ENC, chunk, local)
     picked = jnp.take(arrived, slot_shard, axis=1)
     picked = picked.transpose(1, 2, 0, 3).reshape(used * chunk, features)
-    state_near = stack(gather_short(picked))
+    state_near = gather_ring(picked)
     state_side = gather_long(state_near)
 
     q_d = gathered_dots(index[0], [near], query_weight, output_weight, None, F32)
@@ -493,11 +516,12 @@
     up, down = pass_on(rest[0], rest[1], from_low, from_high, *both_far)
     from_up, from_down = move_v(up, 1), move_v(down, -1)
     both_side = both_terms(jnp.concatenate([index[3], index[1]]), [8, 8], up)
-    g3, g1 = add_halves(*both_side, from_up, from_down)
-    both_near = both_terms(index[0], [2] * 4, g3)
+    pieces = add_pieces(rest[2:], from_up, from_down)
+    g3 = add_half(both_side[0], after(from_up, *pieces), True)
+    g1 = add_half(both_side[1], after(from_down, g3), False)
     r3, r1 = move_v(g3, 1), move_v(g1, -1)
-    pieces = add_pieces(rest[2:], from_up, from_down)
     (summed,) = finish(pieces[0], *move_pieces(pieces))
+    both_near = both_terms(index[0], [2] * 4, g3, summed)
     both_pieces = add_pieces(both_near, after(r3, summed), r1)
     output, d_hidden = finish(both_pieces[0], *move_pieces(both_pieces))
 

time: 206 us -> 205 us (level)
  waiting for transfers between devices: 65.2 us -> 70.8 us
  starting transfers between devices: 31.2 us -> 25.8 us
  local copies, waits for them, and re-layouts: 6.77 us -> 2.32 us
  blocking collectives: 49.6 us -> 52.6 us
    ppermute x12 -> x13, waiting for transfers between devices: 19.2 us -> 24.5 us  [move_u(): return lax.ppermute(value, AXES, shift_table(False, shift))]
    ppermute x14, starting transfers between devices: 18.4 us -> 13.2 us  [move_v(): return lax.ppermute(value, AXES, shift_table(True, shift))]
    unnamed x18 -> x8, local copies, waits for them, and re-layouts: 4.56 us -> 0.9 us
    all_to_all x1, blocking collectives: 23 us -> 26.3 us  [on_device(): lax.all_to_all(neighbour_states.reshape(SEQ * ENC, chunk, local), AXES, s...]
    ppermute x12 -> x13, starting transfers between devices: 12.8 us -> 12.6 us  [move_u(): return lax.ppermute(value, AXES, shift_table(False, shift))]
  transfers between devices with their start and end apart: 26 -> 27, of which waited for: 14 -> 16; matrix products, arithmetic and copies ran while one was open for 2% -> 1% of each run, Pallas kernels for 18% -> 18%
where the time goes in v4:
time: 205 us
  waiting for transfers between devices  70.8 us (35%)
  blocking collectives  52.6 us (26%)
  Pallas kernels  51.1 us (25%)
  starting transfers between devices  25.8 us (13%)
  local copies, waits for them, and re-layouts  2.32 us (1%)
    ppermute x14, waiting for transfers between devices, move_v(): return lax.ppermute(value, AXES, shift_table(True, shift))  46.4 us
    all_to_all x1, blocking collectives, on_device(): lax.all_to_all(after(spread, *both_pieces).reshape(SEQ * ENC, chunk, loca...  26.3 us
    all_to_all x1, blocking collectives, on_device(): lax.all_to_all(neighbour_states.reshape(SEQ * ENC, chunk, local), AXES, s...  26.3 us
    ppermute x13, waiting for transfers between devices, move_u(): return lax.ppermute(value, AXES, shift_table(False, shift))  24.5 us
    pallas_call x3, Pallas kernels, gathered_dots(): pl.pallas_call(functools.partial(gathered_kernel, counts, start is not No...  14.5 us
    ppermute x14, starting transfers between devices, move_v(): return lax.ppermute(value, AXES, shift_table(True, shift))  13.2 us
    ppermute x13, starting transfers between devices, move_u(): return lax.ppermute(value, AXES, shift_table(False, shift))  12.6 us
    pallas_call x3, Pallas kernels, call(): pl.pallas_call(functools.partial(terms_kernel, count), out_shape=[jax.Sha...  12.5 us
  transfers between devices with their start and end apart: 27, of which 16 were waited for; matrix products, arithmetic and copies ran while one was open for 1% of the time, Pallas kernels for 18%

profile of v4, /device:TPU:1, one launch (start us, length us, event | category | flops | bytes accessed | tf_op | source)
XLA Modules:
  0.0 204.8 jit_solution(17082688010896924976)
XLA Ops:
  0.6 1.0 shard_map.103.refs_0_
  1.7 4.7 %collective-permute-start.2 = (bf16[2,256,512]{2,1,0:T(8,128)(2,1)S(1)}, bf16[2,256,512]{2,1,0:T(8,128)(2,1)S(1)}, u32[]{:S(2)}, u32[]{:S(2)}) collective-permute-start(bf16[2,256,512]{2,1,0:T(8,128)(2,1)S(1)} %shard_map.103.refs_0_), channel_id=1, source_target_pairs={{0,3},{1,0},{2,1},{3,2},{4,7},{5,4},{6,5},{7,6},{8,11},{9,8},{10,9... | collective-permute-start | bytes 1572872 | tf_op jit(solution)/shard_map/ppermute | solution.py:42
  6.3 0.7 collective-permute-start
  7.0 26.3 %all_to_all.10 = bf16[128,8,256]{2,1,0:T(8,128)(2,1)S(1)} all-to-all(bf16[128,8,256]{2,1,0:T(8,128)(2,1)} %bitcast.35), channel_id=1, replica_groups=mesh['seq'=8,'enc'=16] {'seq','enc'}, dimensions={0} | all-to-all | bytes 1048576 | tf_op jit(solution)/shard_map/all_to_all | solution.py:483
  33.4 1.5 shard_map.104.refs_0_
  34.9 1.5 collective-permute-start.3
  36.6 0.6 gather_fusion
  37.3 0.2 collective-permute-start.8
  37.6 1.3 collective-permute-start.7
  38.9 7.0 %collective-permute-done.8.three_ref = bf16[2,32,2048]{2,1,0:T(8,128)(2,1)S(1)} collective-permute-done((bf16[2,32,2048]{2,1,0:T(8,128)(2,1)S(1)}, bf16[2,32,2048]{2,1,0:T(8,128)(2,1)S(1)}, u32[]{:S(2)}, u32[]{:S(2)}) %collective-permute-start.8) | collective-permute-done | bytes 262176 | tf_op jit(solution)/shard_map/ppermute | solution.py:42
  45.9 1.3 collective-permute-done.7.one_ref
  47.2 0.2 collective-permute-start.9
  47.4 2.6 %collective-permute-start.10 = (bf16[1,32,2048]{2,1,0:T(8,128)(2,1)S(1)}, bf16[1,32,2048]{2,1,0:T(8,128)(2,1)S(1)}, u32[]{:S(2)}, u32[]{:S(2)}) collective-permute-start(bf16[1,32,2048]{2,1,0:T(8,128)(2,1)S(1)} %get-tuple-element.86), channel_id=1, source_target_pairs={{0,3},{1,0},{2,1},{3,2},{4,7},{5,4},{6,5},{7,6},{8,11},{9,8},{10,9... | collective-permute-start | bytes 393224 | tf_op jit(solution)/shard_map/ppermute | solution.py:42
  50.0 4.2 %collective-permute-done.9.low_ref = bf16[1,32,2048]{2,1,0:T(8,128)(2,1)S(1)} collective-permute-done((bf16[1,32,2048]{2,1,0:T(8,128)(2,1)S(1)}, bf16[1,32,2048]{2,1,0:T(8,128)(2,1)S(1)}, u32[]{:S(2)}, u32[]{:S(2)}) %collective-permute-start.9) | collective-permute-done | bytes 131104 | tf_op jit(solution)/shard_map/ppermute | solution.py:42
  54.3 1.4 collective-permute-start.12
  55.9 4.6 %shard_map.106 = (f32[256,512]{1,0:T(8,128)S(1)}, f32[256,512]{1,0:T(8,128)S(1)}) custom-call(s32[4]{0:T(128)S(1)} %get-tuple-element.150.index_ref, bf16[8192,512]{1,0:T(8,128)(2,1)} %query_ref.11, bf16[512,8192]{1,0:T(8,128)(2,1)} %output_ref.11, bf16[4,2,256,512]{3,2,1,0:T(8,128)(2,1)} %shard_map.104.refs_0_), custom_call_target="tpu_custom_call" | custom-call | flops 1048576 | bytes 6144 | tf_op jit(solution)/shard_map/pallas_call | solution.py:235
  60.5 4.1 %collective-permute-done.4.three_ref.refs_1_ = bf16[4,2,256,512]{3,2,1,0:T(8,128)(2,1)S(1)} collective-permute-done((bf16[4,2,256,512]{3,2,1,0:T(8,128)(2,1)}, bf16[4,2,256,512]{3,2,1,0:T(8,128)(2,1)S(1)}, u32[]{:S(2)}, u32[]{:S(2)}) %collective-permute-start.4) | collective-permute-done | bytes 2097184 | tf_op jit(solution)/shard_map/ppermute | solution.py:46
  64.6 1.2 collective-permute-done.3.one_ref.refs_0_
  65.8 1.7 shard_map.105
  67.6 1.5 collective-permute-start.5
  69.1 1.2 shard_map.111
  70.4 5.3 %collective-permute-done.12.refs_1_.three_ref = bf16[4,64,2048]{2,1,0:T(8,128)(2,1)S(1)} collective-permute-done((bf16[4,64,2048]{2,1,0:T(8,128)(2,1)S(1)}, bf16[4,64,2048]{2,1,0:T(8,128)(2,1)S(1)}, u32[]{:S(2)}, u32[]{:S(2)}) %collective-permute-start.12) | collective-permute-done | bytes 1048608 | tf_op jit(solution)/shard_map/ppermute | solution.py:46
  75.7 1.2 collective-permute-done.11.refs_0_.one_ref
  77.0 6.2 %shard_map.107 = (f32[256,512]{1,0:T(8,128)S(1)}, f32[256,512]{1,0:T(8,128)S(1)}) custom-call(s32[8]{0:T(128)S(1)} %get-tuple-element.152.index_ref, bf16[8192,512]{1,0:T(8,128)(2,1)} %query_ref.11, bf16[512,8192]{1,0:T(8,128)(2,1)} %output_ref.11, bf16[4,2,256,512]{3,2,1,0:T(8,128)(2,1)} %collective-permute-done.3.one_ref.refs_0_, ...), custom_call_target="tpu_custom_call" | custom-call | flops 2097152 | bytes 12288 | tf_op jit(solution)/shard_map/pallas_call | solution.py:235
  83.2 0.3 collective-permute-start.13
  83.6 2.4 %collective-permute-start.14 = (bf16[2,64,2048]{2,1,0:T(8,128)(2,1)S(1)}, bf16[2,64,2048]{2,1,0:T(8,128)(2,1)S(1)}, u32[]{:S(2)}, u32[]{:S(2)}) collective-permute-start(bf16[2,64,2048]{2,1,0:T(8,128)(2,1)S(1)} %get-tuple-element.95), channel_id=1, source_target_pairs={{0,12},{1,13},{2,14},{3,15},{4,0},{5,1},{6,2},{7,3},{8,4},{9,5},{1... | collective-permute-start | bytes 1572872 | tf_op jit(solution)/shard_map/ppermute | solution.py:46
  86.0 2.3 %shard_map.112 = (bf16[512,512]{1,0:T(8,128)(2,1)S(1)}, bf16[512,512]{1,0:T(8,128)(2,1)S(1)}) custom-call(bf16[2048,512]{1,0:T(8,128)(2,1)S(1)} %copy-done, bf16[2048,512]{1,0:T(8,128)(2,1)S(1)} %copy-done.1, bf16[4,64,2048]{2,1,0:T(8,128)(2,1)S(1)} %collective-permute-done.11.refs_0_.one_ref, bf16[4,64,2048]{2,1,0:T(8,128)(2,1)S(1)} %collective-permute-done.12.refs_1_.three_ref), custom_call_target="tpu_custom_call" | custom-call | flops 2097152 | bytes 8192 | tf_op jit(solution)/shard_map/pallas_call | solution.py:370
  88.3 3.7 %shard_map.108 = (bf16[256,512]{1,0:T(8,128)(2,1)S(1)}, bf16[256,512]{1,0:T(8,128)(2,1)S(1)}) custom-call(s32[4]{0:T(128)S(1)} %get-tuple-element.149.index_ref, bf16[8192,512]{1,0:T(8,128)(2,1)} %query_ref.11, bf16[512,8192]{1,0:T(8,128)(2,1)} %output_ref.11, bf16[2,2,256,512]{3,2,1,0:T(8,128)(2,1)S(1)} %collective-permute-done.5.refs_0_, ...), custom_call_target="tpu_custom_call" | custom-call | flops 1048576 | bytes 6144 | tf_op jit(solution)/shard_map/pallas_call | solution.py:235
  92.1 1.7 collective-permute-done.13.refs_0_
  93.8 1.3 shard_map.114
  95.0 2.8 %shard_map.115 = (bf16[256,512]{1,0:T(8,128)(2,1)S(1)}, bf16[256,512]{1,0:T(8,128)(2,1)S(1)}, bf16[256,512]{1,0:T(8,128)(2,1)S(1)}, bf16[256,512]{1,0:T(8,128)(2...) custom-call(bf16[256,512]{1,0:T(8,128)(2,1)S(1)} %get-tuple-element., ...), custom_call_target="tpu_custom_call" | custom-call | flops 393216 | bytes 10240 | tf_op jit(solution)/shard_map/pallas_call | solution.py:454
  97.8 1.3 shard_map.116
  99.1 1.7 collective-permute-start.16
  100.8 3.6 %shard_map.117 = (bf16[4,256,512]{2,1,0:T(8,128)(2,1)S(1)}, bf16[4,256,512]{2,1,0:T(8,128)(2,1)S(1)}) custom-call(s32[4]{0:T(128)S(1)} %get-tuple-element.149.index_ref, bf16[8192,512]{1,0:T(8,128)(2,1)} %query_ref.11, bf16[512,8192]{1,0:T(8,128)(2,1)} %output_ref.11, bf16[256,512]{1,0:T(8,128)(2,1)S(1)} %get-tuple-element.129.c_ref, ...), custom_call_target="tpu_custom_call" | custom-call | flops 1048576 | bytes 8192 | tf_op jit(solution)/shard_map/pallas_call | solution.py:263
  104.4 3.5 %shard_map.118 = (bf16[4,256,512]{2,1,0:T(8,128)(2,1)S(1)}, bf16[4,256,512]{2,1,0:T(8,128)(2,1)S(1)}, bf16[1,256,512]{2,1,0:T(8,128)(2,1)S(1)}, bf16[1,256,512]{...) custom-call(bf16[2048,512]{1,0:T(8,128)(2,1)S(1)} %copy-done, ...), custom_call_target="tpu_custom_call" | custom-call | flops 3145728 | bytes 10240 | tf_op jit(solution)/shard_map/pallas_call | solution.py:399
  107.8 2.5 %collective-permute-done.15.low_ref = bf16[2,256,512]{2,1,0:T(8,128)(2,1)S(1)} collective-permute-done((bf16[2,256,512]{2,1,0:T(8,128)(2,1)S(1)}, bf16[2,256,512]{2,1,0:T(8,128)(2,1)S(1)}, u32[]{:S(2)}, u32[]{:S(2)}) %collective-permute-start.15) | collective-permute-done | bytes 524320 | tf_op jit(solution)/shard_map/ppermute | solution.py:46
  110.3 0.4 shard_map.119
  110.7 0.3 collective-permute-start.18
  111.0 1.3 collective-permute-start.17
  112.2 5.3 %shard_map.120 = (bf16[8,256,512]{2,1,0:T(8,128)(2,1)S(1)}, bf16[8,256,512]{2,1,0:T(8,128)(2,1)S(1)}) custom-call(s32[8]{0:T(128)S(1)} %get-tuple-element.151.index_ref, bf16[8192,512]{1,0:T(8,128)(2,1)} %query_ref.11, bf16[512,8192]{1,0:T(8,128)(2,1)} %output_ref.11, bf16[256,512]{1,0:T(8,128)(2,1)S(1)} %get-tuple-element.129.c_ref, ...), custom_call_target="tpu_custom_call" | custom-call | flops 2097152 | bytes 16384 | tf_op jit(solution)/shard_map/pallas_call | solution.py:263
  117.6 18.4 %collective-permute-done.18.refs_5_.part_ref = bf16[8,256,512]{2,1,0:T(8,128)(2,1)S(1)} collective-permute-done((bf16[8,256,512]{2,1,0:T(8,128)(2,1)S(1)}, bf16[8,256,512]{2,1,0:T(8,128)(2,1)S(1)}, u32[]{:S(2)}, u32[]{:S(2)}) %collective-permute-start.18) | collective-permute-done | bytes 2097184 | tf_op jit(solution)/shard_map/ppermute | solution.py:46
  135.9 1.5 collective-permute-done.17.refs_4_.part_ref
  137.4 0.4 shard_map.121
  137.8 1.6 shard_map.122
  139.4 1.6 shard_map.125
  141.0 2.7 %collective-permute-start.23 = (bf16[8,256,512]{2,1,0:T(8,128)(2,1)}, bf16[8,256,512]{2,1,0:T(8,128)(2,1)}, u32[]{:S(2)}, u32[]{:S(2)}) collective-permute-start(bf16[8,256,512]{2,1,0:T(8,128)(2,1)} %shard_map.125), channel_id=1, source_target_pairs={{0,12},{1,13},{2,14},{3,15},{4,0},{5,1},{6,2},{7,3},{8,4},{9,5},{1... | collective-permute-start | bytes 6291464 | tf_op jit(solution)/shard_map/ppermute | solution.py:46
  143.8 0.6 iota_reduce_fusion
  144.4 0.3 collective-permute-start.19
  144.7 1.1 collective-permute-start.20
  145.9 4.0 %collective-permute-done.19.refs_1_ = bf16[1,256,512]{2,1,0:T(8,128)(2,1)S(1)} collective-permute-done((bf16[1,256,512]{2,1,0:T(8,128)(2,1)S(1)}, bf16[1,256,512]{2,1,0:T(8,128)(2,1)S(1)}, u32[]{:S(2)}, u32[]{:S(2)}) %collective-permute-start.19) | collective-permute-done | bytes 262176 | tf_op jit(solution)/shard_map/ppermute | solution.py:42
  149.9 4.4 %collective-permute-done.20.refs_2_ = bf16[1,256,512]{2,1,0:T(8,128)(2,1)S(1)} collective-permute-done((bf16[1,256,512]{2,1,0:T(8,128)(2,1)S(1)}, bf16[1,256,512]{2,1,0:T(8,128)(2,1)S(1)}, u32[]{:S(2)}, u32[]{:S(2)}) %collective-permute-start.20) | collective-permute-done | bytes 262176 | tf_op jit(solution)/shard_map/ppermute | solution.py:42
  154.3 3.5 %collective-permute-done.21.refs_3_ = bf16[1,256,512]{2,1,0:T(8,128)(2,1)S(1)} collective-permute-done((bf16[1,256,512]{2,1,0:T(8,128)(2,1)S(1)}, bf16[1,256,512]{2,1,0:T(8,128)(2,1)S(1)}, u32[]{:S(2)}, u32[]{:S(2)}) %collective-permute-start.21) | collective-permute-done | bytes 262176 | tf_op jit(solution)/shard_map/ppermute | solution.py:42
  157.8 0.1 shard_map.123
  158.0 0.6 gather_fusion.1
  158.6 3.6 %shard_map.124 = (bf16[2,256,512]{2,1,0:T(8,128)(2,1)S(1)}, bf16[2,256,512]{2,1,0:T(8,128)(2,1)S(1)}, bf16[2,256,512]{2,1,0:T(8,128)(2,1)S(1)}, bf16[2,256,512]{2,1,0:T(8,128)(2,1)S(1)}) custom-call(s32[4]{0:T(128)S(1)} %get-tuple-element.150.index_ref, bf16[8192,512]{1,0:T(8,128)(2,1)} %query_ref.11, bf16[512,8192]{1,0:T(8,128)(2,1)} %output_ref.11, ...), custom_call_target="tpu_custom_call" | custom-call | flops 1048576 | bytes 8192 | tf_op jit(solution)/shard_map/pallas_call | solution.py:263
  162.2 9.5 %collective-permute-done.22.refs_4_ = bf16[8,256,512]{2,1,0:T(8,128)(2,1)S(1)} collective-permute-done((bf16[8,256,512]{2,1,0:T(8,128)(2,1)}, bf16[8,256,512]{2,1,0:T(8,128)(2,1)S(1)}, u32[]{:S(2)}, u32[]{:S(2)}) %collective-permute-start.22) | collective-permute-done | bytes 2097184 | tf_op jit(solution)/shard_map/ppermute | solution.py:46
  171.7 1.0 collective-permute-done.23.refs_5_
  172.6 2.3 %shard_map.126 = (bf16[2,256,512]{2,1,0:T(8,128)(2,1)S(1)}, bf16[2,256,512]{2,1,0:T(8,128)(2,1)S(1)}, bf16[2,256,512]{2,1,0:T(8,128)(2,1)S(1)}, bf16[2,256,512]{2,1,0:T(8,128)(2,1)S(1)}) custom-call(bf16[2,256,512]{2,1,0:T(8,128)(2,1)S(1)} %get-tuple-element.130.refs_0_, bf16[2,256,512]{2,1,0:T(8,128)(2,1)S(1)} %get-tuple-element.131.refs_1_, ...), custom_call_target="tpu_custom_call" | custom-call | flops 8192 | bytes 8192 | tf_op jit(solution)/shard_map/pallas_call | solution.py:329
  175.0 0.4 collective-permute-start.24
  175.4 1.1 collective-permute-start.25
  176.5 0.1 select_bitcast_fusion
  176.7 26.3 %all_to_all.11 = bf16[128,8,256]{2,1,0:T(8,128)(2,1)S(1)} all-to-all(bf16[128,8,256]{2,1,0:T(8,128)(2,1)S(1)} %bitcast.33), channel_id=1, replica_groups=mesh['seq'=8,'enc'=16] {'seq','enc'}, dimensions={0} | all-to-all | bytes 1048576 | tf_op jit(solution)/shard_map/all_to_all | solution.py:534
  203.0 1.0 shard_map.127
  204.0 0.8 copy.25
  (47 shorter events, 1.2 us)
Async XLA Ops:
  1.7 31.7 %collective-permute-start.2 = (bf16[2,256,512]{2,1,0:T(8,128)(2,1)S(1)}, bf16[2,256,512]{2,1,0:T(8,128)(2,1)S(1)}, u32[]{:S(2)}, u32[]{:S(2)}) collective-permute-start(bf16[2,256,512]{2,1,0:T(8,128)(2,1)S(1)} %shard_map.103.refs_0_), channel_id=1, source_target_pairs={{0,3},{1,0},{2,1},{3,2},{4,7},{5,4},{6,5},{7,6},{8,11},{9,8},{10,9... | collective-permute-start | bytes 1572872 | tf_op jit(solution)/shard_map/ppermute | solution.py:42
  6.3 27.0 %collective-permute-start.1 = (bf16[2,256,512]{2,1,0:T(8,128)(2,1)S(1)}, bf16[2,256,512]{2,1,0:T(8,128)(2,1)S(1)}, u32[]{:S(2)}, u32[]{:S(2)}) collective-permute-start(bf16[2,256,512]{2,1,0:T(8,128)(2,1)S(1)} %shard_map.103.refs_0_), channel_id=1, source_target_pairs={{0,2},{1,3},{2,0},{3,1},{4,6},{5,7},{6,4},{7,5},{8,10},{9,11},{10,... | collective-permute-start | bytes 1572872 | tf_op jit(solution)/shard_map/ppermute | solution.py:42
  6.3 27.0 %collective-permute-start = (bf16[2,256,512]{2,1,0:T(8,128)(2,1)S(1)}, bf16[2,256,512]{2,1,0:T(8,128)(2,1)S(1)}, u32[]{:S(2)}, u32[]{:S(2)}) collective-permute-start(bf16[2,256,512]{2,1,0:T(8,128)(2,1)S(1)} %shard_map.103.refs_0_), channel_id=1, source_target_pairs={{0,1},{1,2},{2,3},{3,0},{4,5},{5,6},{6,7},{7,4},{8,9},{9,10},{10,1... | collective-permute-start | bytes 1572872 | tf_op jit(solution)/shard_map/ppermute | solution.py:42
  33.4 3.0 %copy-start.2 = (s32[4,2]{0,1:T(2,128)S(1)}, s32[4,2]{0,1:T(2,128)}, u32[]{:S(2)}) copy-start(s32[4,2]{0,1:T(2,128)} %param.14) | copy-start | bytes 100
  34.9 29.7 %collective-permute-start.4 = (bf16[4,2,256,512]{3,2,1,0:T(8,128)(2,1)}, bf16[4,2,256,512]{3,2,1,0:T(8,128)(2,1)S(1)}, u32[]{:S(2)}, u32[]{:S(2)}) collective-permute-start(bf16[4,2,256,512]{3,2,1,0:T(8,128)(2,1)} %shard_map.104.refs_0_), channel_id=1, source_target_pairs={{0,12},{1,13},{2,14},{3,15},{4,0},{5,1},{6,2},{7,3},{8,4},{9,5},{1... | collective-permute-start | bytes 6291464 | tf_op jit(solution)/shard_map/ppermute | solution.py:46
  34.9 30.9 %collective-permute-start.3 = (bf16[4,2,256,512]{3,2,1,0:T(8,128)(2,1)}, bf16[4,2,256,512]{3,2,1,0:T(8,128)(2,1)}, u32[]{:S(2)}, u32[]{:S(2)}) collective-permute-start(bf16[4,2,256,512]{3,2,1,0:T(8,128)(2,1)} %shard_map.104.refs_0_), channel_id=1, source_target_pairs={{0,4},{1,5},{2,6},{3,7},{4,8},{5,9},{6,10},{7,11},{8,12},{9,13},{1... | collective-permute-start | bytes 6291464 | tf_op jit(solution)/shard_map/ppermute | solution.py:46
  37.3 8.6 %collective-permute-start.8 = (bf16[2,32,2048]{2,1,0:T(8,128)(2,1)S(1)}, bf16[2,32,2048]{2,1,0:T(8,128)(2,1)S(1)}, u32[]{:S(2)}, u32[]{:S(2)}) collective-permute-start(bf16[2,32,2048]{2,1,0:T(8,128)(2,1)S(1)} %bitcast.28), channel_id=1, source_target_pairs={{0,3},{1,0},{2,1},{3,2},{4,7},{5,4},{6,5},{7,6},{8,11},{9,8},{10,9... | collective-permute-start | bytes 786440 | tf_op jit(solution)/shard_map/ppermute | solution.py:42
  37.6 9.6 %collective-permute-start.7 = (bf16[2,32,2048]{2,1,0:T(8,128)(2,1)S(1)}, bf16[2,32,2048]{2,1,0:T(8,128)(2,1)S(1)}, u32[]{:S(2)}, u32[]{:S(2)}) collective-permute-start(bf16[2,32,2048]{2,1,0:T(8,128)(2,1)S(1)} %bitcast.29), channel_id=1, source_target_pairs={{0,1},{1,2},{2,3},{3,0},{4,5},{5,6},{6,7},{7,4},{8,9},{9,10},{10,1... | collective-permute-start | bytes 786440 | tf_op jit(solution)/shard_map/ppermute | solution.py:42
  47.2 7.0 %collective-permute-start.9 = (bf16[1,32,2048]{2,1,0:T(8,128)(2,1)S(1)}, bf16[1,32,2048]{2,1,0:T(8,128)(2,1)S(1)}, u32[]{:S(2)}, u32[]{:S(2)}) collective-permute-start(bf16[1,32,2048]{2,1,0:T(8,128)(2,1)S(1)} %get-tuple-element.85), channel_id=1, source_target_pairs={{0,1},{1,2},{2,3},{3,0},{4,5},{5,6},{6,7},{7,4},{8,9},{9,10},{10,1... | collective-permute-start | bytes 393224 | tf_op jit(solution)/shard_map/ppermute | solution.py:42
  47.4 6.8 %collective-permute-start.10 = (bf16[1,32,2048]{2,1,0:T(8,128)(2,1)S(1)}, bf16[1,32,2048]{2,1,0:T(8,128)(2,1)S(1)}, u32[]{:S(2)}, u32[]{:S(2)}) collective-permute-start(bf16[1,32,2048]{2,1,0:T(8,128)(2,1)S(1)} %get-tuple-element.86), channel_id=1, source_target_pairs={{0,3},{1,0},{2,1},{3,2},{4,7},{5,4},{6,5},{7,6},{8,11},{9,8},{10,9... | collective-permute-start | bytes 393224 | tf_op jit(solution)/shard_map/ppermute | solution.py:42
  54.3 21.4 %collective-permute-start.12 = (bf16[4,64,2048]{2,1,0:T(8,128)(2,1)S(1)}, bf16[4,64,2048]{2,1,0:T(8,128)(2,1)S(1)}, u32[]{:S(2)}, u32[]{:S(2)}) collective-permute-start(bf16[4,64,2048]{2,1,0:T(8,128)(2,1)S(1)} %bitcast.24), channel_id=1, source_target_pairs={{0,12},{1,13},{2,14},{3,15},{4,0},{5,1},{6,2},{7,3},{8,4},{9,5},{1... | collective-permute-start | bytes 3145736 | tf_op jit(solution)/shard_map/ppermute | solution.py:46
  55.7 21.3 %collective-permute-start.11 = (bf16[4,64,2048]{2,1,0:T(8,128)(2,1)S(1)}, bf16[4,64,2048]{2,1,0:T(8,128)(2,1)S(1)}, u32[]{:S(2)}, u32[]{:S(2)}) collective-permute-start(bf16[4,64,2048]{2,1,0:T(8,128)(2,1)S(1)} %bitcast.25), channel_id=1, source_target_pairs={{0,4},{1,5},{2,6},{3,7},{4,8},{5,9},{6,10},{7,11},{8,12},{9,13},{1... | collective-permute-start | bytes 3145736 | tf_op jit(solution)/shard_map/ppermute | solution.py:46
  60.4 8.7 %copy-start = (bf16[2048,512]{1,0:T(8,128)(2,1)S(1)}, bf16[2048,512]{1,0:T(8,128)(2,1)}, u32[]{:S(2)}) copy-start(bf16[2048,512]{1,0:T(8,128)(2,1)} %key_ref.9) | copy-start | bytes 6291460
  60.5 8.7 %copy-start.1 = (bf16[2048,512]{1,0:T(8,128)(2,1)S(1)}, bf16[2048,512]{1,0:T(8,128)(2,1)}, u32[]{:S(2)}) copy-start(bf16[2048,512]{1,0:T(8,128)(2,1)} %value_ref.9) | copy-start | bytes 6291460
  67.5 20.8 %collective-permute-start.6 = (bf16[2,2,256,512]{3,2,1,0:T(8,128)(2,1)S(1)}, bf16[2,2,256,512]{3,2,1,0:T(8,128)(2,1)S(1)}, u32[]{:S(2)}, u32[]{:S(2)}) collective-permute-start(bf16[2,2,256,512]{3,2,1,0:T(8,128)(2,1)S(1)} %get-tuple-element.80), channel_id=1, source_target_pairs={{0,12},{1,13},{2,14},{3,15},{4,0},{5,1},{6,2},{7,3},{8,4},{9,5},{1... | collective-permute-start | bytes 3145736 | tf_op jit(solution)/shard_map/ppermute | solution.py:46
  67.6 20.7 %collective-permute-start.5 = (bf16[2,2,256,512]{3,2,1,0:T(8,128)(2,1)S(1)}, bf16[2,2,256,512]{3,2,1,0:T(8,128)(2,1)S(1)}, u32[]{:S(2)}, u32[]{:S(2)}) collective-permute-start(bf16[2,2,256,512]{3,2,1,0:T(8,128)(2,1)S(1)} %get-tuple-element.78), channel_id=1, source_target_pairs={{0,4},{1,5},{2,6},{3,7},{4,8},{5,9},{6,10},{7,11},{8,12},{9,13},{1... | collective-permute-start | bytes 3145736 | tf_op jit(solution)/shard_map/ppermute | solution.py:46
  83.2 10.5 %collective-permute-start.13 = (bf16[2,64,2048]{2,1,0:T(8,128)(2,1)S(1)}, bf16[2,64,2048]{2,1,0:T(8,128)(2,1)S(1)}, u32[]{:S(2)}, u32[]{:S(2)}) collective-permute-start(bf16[2,64,2048]{2,1,0:T(8,128)(2,1)S(1)} %get-tuple-element.91), channel_id=1, source_target_pairs={{0,4},{1,5},{2,6},{3,7},{4,8},{5,9},{6,10},{7,11},{8,12},{9,13},{1... | collective-permute-start | bytes 1572872 | tf_op jit(solution)/shard_map/ppermute | solution.py:46
  83.6 10.2 %collective-permute-start.14 = (bf16[2,64,2048]{2,1,0:T(8,128)(2,1)S(1)}, bf16[2,64,2048]{2,1,0:T(8,128)(2,1)S(1)}, u32[]{:S(2)}, u32[]{:S(2)}) collective-permute-start(bf16[2,64,2048]{2,1,0:T(8,128)(2,1)S(1)} %get-tuple-element.95), channel_id=1, source_target_pairs={{0,12},{1,13},{2,14},{3,15},{4,0},{5,1},{6,2},{7,3},{8,4},{9,5},{1... | collective-permute-start | bytes 1572872 | tf_op jit(solution)/shard_map/ppermute | solution.py:46
  99.1 8.7 %collective-permute-start.16 = (bf16[2,256,512]{2,1,0:T(8,128)(2,1)S(1)}, bf16[2,256,512]{2,1,0:T(8,128)(2,1)S(1)}, u32[]{:S(2)}, u32[]{:S(2)}) collective-permute-start(bf16[2,256,512]{2,1,0:T(8,128)(2,1)S(1)} %get-tuple-element.115), channel_id=1, source_target_pairs={{0,12},{1,13},{2,14},{3,15},{4,0},{5,1},{6,2},{7,3},{8,4},{9,5},{1... | collective-permute-start | bytes 1572872 | tf_op jit(solution)/shard_map/ppermute | solution.py:46
  100.8 9.5 %collective-permute-start.15 = (bf16[2,256,512]{2,1,0:T(8,128)(2,1)S(1)}, bf16[2,256,512]{2,1,0:T(8,128)(2,1)S(1)}, u32[]{:S(2)}, u32[]{:S(2)}) collective-permute-start(bf16[2,256,512]{2,1,0:T(8,128)(2,1)S(1)} %get-tuple-element.102), channel_id=1, source_target_pairs={{0,4},{1,5},{2,6},{3,7},{4,8},{5,9},{6,10},{7,11},{8,12},{9,13},{1... | collective-permute-start | bytes 1572872 | tf_op jit(solution)/shard_map/ppermute | solution.py:46
  110.7 25.2 %collective-permute-start.18 = (bf16[8,256,512]{2,1,0:T(8,128)(2,1)S(1)}, bf16[8,256,512]{2,1,0:T(8,128)(2,1)S(1)}, u32[]{:S(2)}, u32[]{:S(2)}) collective-permute-start(bf16[8,256,512]{2,1,0:T(8,128)(2,1)S(1)} %get-tuple-element.123), channel_id=1, source_target_pairs={{0,12},{1,13},{2,14},{3,15},{4,0},{5,1},{6,2},{7,3},{8,4},{9,5},{1... | collective-permute-start | bytes 6291464 | tf_op jit(solution)/shard_map/ppermute | solution.py:46
  111.0 26.5 %collective-permute-start.17 = (bf16[8,256,512]{2,1,0:T(8,128)(2,1)S(1)}, bf16[8,256,512]{2,1,0:T(8,128)(2,1)S(1)}, u32[]{:S(2)}, u32[]{:S(2)}) collective-permute-start(bf16[8,256,512]{2,1,0:T(8,128)(2,1)S(1)} %get-tuple-element.116), channel_id=1, source_target_pairs={{0,4},{1,5},{2,6},{3,7},{4,8},{5,9},{6,10},{7,11},{8,12},{9,13},{1... | collective-permute-start | bytes 6291464 | tf_op jit(solution)/shard_map/ppermute | solution.py:46
  139.4 32.2 %collective-permute-start.22 = (bf16[8,256,512]{2,1,0:T(8,128)(2,1)}, bf16[8,256,512]{2,1,0:T(8,128)(2,1)S(1)}, u32[]{:S(2)}, u32[]{:S(2)}) collective-permute-start(bf16[8,256,512]{2,1,0:T(8,128)(2,1)} %shard_map.122), channel_id=1, source_target_pairs={{0,4},{1,5},{2,6},{3,7},{4,8},{5,9},{6,10},{7,11},{8,12},{9,13},{1... | collective-permute-start | bytes 6291464 | tf_op jit(solution)/shard_map/ppermute | solution.py:46
  141.0 31.6 %collective-permute-start.23 = (bf16[8,256,512]{2,1,0:T(8,128)(2,1)}, bf16[8,256,512]{2,1,0:T(8,128)(2,1)}, u32[]{:S(2)}, u32[]{:S(2)}) collective-permute-start(bf16[8,256,512]{2,1,0:T(8,128)(2,1)} %shard_map.125), channel_id=1, source_target_pairs={{0,12},{1,13},{2,14},{3,15},{4,0},{5,1},{6,2},{7,3},{8,4},{9,5},{1... | collective-permute-start | bytes 6291464 | tf_op jit(solution)/shard_map/ppermute | solution.py:46
  144.4 5.5 %collective-permute-start.19 = (bf16[1,256,512]{2,1,0:T(8,128)(2,1)S(1)}, bf16[1,256,512]{2,1,0:T(8,128)(2,1)S(1)}, u32[]{:S(2)}, u32[]{:S(2)}) collective-permute-start(bf16[1,256,512]{2,1,0:T(8,128)(2,1)S(1)} %get-tuple-element.125), channel_id=1, source_target_pairs={{0,3},{1,0},{2,1},{3,2},{4,7},{5,4},{6,5},{7,6},{8,11},{9,8},{10,9... | collective-permute-start | bytes 786440 | tf_op jit(solution)/shard_map/ppermute | solution.py:42
  144.7 9.6 %collective-permute-start.20 = (bf16[1,256,512]{2,1,0:T(8,128)(2,1)S(1)}, bf16[1,256,512]{2,1,0:T(8,128)(2,1)S(1)}, u32[]{:S(2)}, u32[]{:S(2)}) collective-permute-start(bf16[1,256,512]{2,1,0:T(8,128)(2,1)S(1)} %get-tuple-element.126), channel_id=1, source_target_pairs={{0,2},{1,3},{2,0},{3,1},{4,6},{5,7},{6,4},{7,5},{8,10},{9,11},{10,... | collective-permute-start | bytes 786440 | tf_op jit(solution)/shard_map/ppermute | solution.py:42
  145.8 12.0 %collective-permute-start.21 = (bf16[1,256,512]{2,1,0:T(8,128)(2,1)S(1)}, bf16[1,256,512]{2,1,0:T(8,128)(2,1)S(1)}, u32[]{:S(2)}, u32[]{:S(2)}) collective-permute-start(bf16[1,256,512]{2,1,0:T(8,128)(2,1)S(1)} %get-tuple-element.127), channel_id=1, source_target_pairs={{0,1},{1,2},{2,3},{3,0},{4,5},{5,6},{6,7},{7,4},{8,9},{9,10},{10,1... | collective-permute-start | bytes 786440 | tf_op jit(solution)/shard_map/ppermute | solution.py:42
  175.0 28.0 %collective-permute-start.24 = (bf16[2,256,512]{2,1,0:T(8,128)(2,1)S(1)}, bf16[2,256,512]{2,1,0:T(8,128)(2,1)S(1)}, u32[]{:S(2)}, u32[]{:S(2)}) collective-permute-start(bf16[2,256,512]{2,1,0:T(8,128)(2,1)S(1)} %get-tuple-element.138), channel_id=1, source_target_pairs={{0,3},{1,0},{2,1},{3,2},{4,7},{5,4},{6,5},{7,6},{8,11},{9,8},{10,9... | collective-permute-start | bytes 1572872 | tf_op jit(solution)/shard_map/ppermute | solution.py:42
  175.4 27.6 %collective-permute-start.25 = (bf16[2,256,512]{2,1,0:T(8,128)(2,1)S(1)}, bf16[2,256,512]{2,1,0:T(8,128)(2,1)S(1)}, u32[]{:S(2)}, u32[]{:S(2)}) collective-permute-start(bf16[2,256,512]{2,1,0:T(8,128)(2,1)S(1)} %get-tuple-element.139), channel_id=1, source_target_pairs={{0,2},{1,3},{2,0},{3,1},{4,6},{5,7},{6,4},{7,5},{8,10},{9,11},{10,... | collective-permute-start | bytes 1572872 | tf_op jit(solution)/shard_map/ppermute | solution.py:42
  176.5 26.5 %collective-permute-start.26 = (bf16[2,256,512]{2,1,0:T(8,128)(2,1)S(1)}, bf16[2,256,512]{2,1,0:T(8,128)(2,1)S(1)}, u32[]{:S(2)}, u32[]{:S(2)}) collective-permute-start(bf16[2,256,512]{2,1,0:T(8,128)(2,1)S(1)} %get-tuple-element.140), channel_id=1, source_target_pairs={{0,1},{1,2},{2,3},{3,0},{4,5},{5,6},{6,7},{7,4},{8,9},{9,10},{10,1... | collective-permute-start | bytes 1572872 | tf_op jit(solution)/shard_map/ppermute | solution.py:42

commit v5 on v4

--- a/solution.py
+++ b/solution.py
@@ -483,7 +483,7 @@
     arrived = lax.all_to_all(
         neighbour_states.reshape(SEQ * ENC, chunk, local), AXES, split_axis=0, concat_axis=0, tiled=True
     )
-    near = stack([after(near[0], arrived)] + near[1:])
+    near = after(stack(near), arrived)
     side = gather_long(near)
     arrived = arrived.reshape(SEQ, ENC, chunk, local)
     picked = jnp.take(arrived, slot_shard, axis=1)

time: 205 us -> 204 us (level)
  blocking collectives: 52.6 us -> 26.3 us
  waiting for transfers between devices: 70.8 us -> 86.6 us
  starting transfers between devices: 25.8 us -> 35.9 us
  Pallas kernels: 51.1 us -> 48.8 us
    all_to_all x1 -> x0, blocking collectives: 26.3 us -> none  [on_device(): lax.all_to_all(neighbour_states.reshape(SEQ * ENC, chunk, local), AXES, s...]
    all_to_all x0 -> x1, waiting for transfers between devices: none -> 10.4 us  [on_device(): lax.all_to_all(neighbour_states.reshape(SEQ * ENC, chunk, local), AXES, s...]
    all_to_all x0 -> x1, starting transfers between devices: none -> 9.98 us  [on_device(): lax.all_to_all(neighbour_states.reshape(SEQ * ENC, chunk, local), AXES, s...]
    ppermute x13, waiting for transfers between devices: 24.5 us -> 28.9 us  [move_u(): return lax.ppermute(value, AXES, shift_table(False, shift))]
  transfers between devices with their start and end apart: 27 -> 28, of which waited for: 16 -> 19; matrix products, arithmetic and copies ran while one was open for 1% -> 1% of each run, Pallas kernels for 18% -> 18%
where the time goes in v5:
time: 204 us; the launch traced here: 203 us
  waiting for transfers between devices  86.6 us (42%)
  Pallas kernels  48.8 us (24%)
  starting transfers between devices  35.9 us (18%)
  blocking collectives  26.3 us (13%)
  local copies, waits for them, and re-layouts  3.68 us (2%)
    ppermute x14, waiting for transfers between devices, move_v(): return lax.ppermute(value, AXES, shift_table(True, shift))  47.3 us
    ppermute x13, waiting for transfers between devices, move_u(): return lax.ppermute(value, AXES, shift_table(False, shift))  28.9 us
    all_to_all x1, blocking collectives, on_device(): lax.all_to_all(after(spread, *both_pieces).reshape(SEQ * ENC, chunk, loca...  26.3 us
    pallas_call x3, Pallas kernels, gathered_dots(): pl.pallas_call(functools.partial(gathered_kernel, counts, start is not No...  13.5 us
    ppermute x14, starting transfers between devices, move_v(): return lax.ppermute(value, AXES, shift_table(True, shift))  13.2 us
    ppermute x13, starting transfers between devices, move_u(): return lax.ppermute(value, AXES, shift_table(False, shift))  12.7 us
    pallas_call x3, Pallas kernels, call(): pl.pallas_call(functools.partial(terms_kernel, count), out_shape=[jax.Sha...  12.4 us
    all_to_all x1, waiting for transfers between devices, on_device(): lax.all_to_all(neighbour_states.reshape(SEQ * ENC, chunk, local), AXES, s...  10.4 us
  transfers between devices with their start and end apart: 28, of which 19 were waited for; matrix products, arithmetic and copies ran while one was open for 1% of the time, Pallas kernels for 18%

profile of v5, /device:TPU:1, one launch (start us, length us, event | category | flops | bytes accessed | tf_op | source)
XLA Modules:
  0.0 203.3 jit_solution(18424170104817576381)
XLA Ops:
  0.6 1.0 shard_map.103.refs_0_
  1.7 4.7 %collective-permute-start.2 = (bf16[2,256,512]{2,1,0:T(8,128)(2,1)S(1)}, bf16[2,256,512]{2,1,0:T(8,128)(2,1)S(1)}, u32[]{:S(2)}, u32[]{:S(2)}) collective-permute-start(bf16[2,256,512]{2,1,0:T(8,128)(2,1)S(1)} %shard_map.103.refs_0_), channel_id=1, source_target_pairs={{0,3},{1,0},{2,1},{3,2},{4,7},{5,4},{6,5},{7,6},{8,11},{9,8},{10,9... | collective-permute-start | bytes 1572872 | tf_op jit(solution)/shard_map/ppermute | solution.py:42
  6.3 0.7 collective-permute-start
  7.0 10.0 %all-to-all-start = ((bf16[128,8,256]{2,1,0:T(8,128)(2,1)}), bf16[128,8,256]{2,1,0:T(8,128)(2,1)S(1)}, u32[]{:S(2)}, u32[]{:S(2)}) async-start(bf16[128,8,256]{2,1,0:T(8,128)(2,1)} %bitcast.35), calls=%async_computation | async-start | bytes 1048576 | tf_op jit(solution)/shard_map/all_to_all | solution.py:483
  17.0 1.0 collective-permute-done.2.refs_3_
  18.1 3.4 %collective-permute-done.refs_1_ = bf16[2,256,512]{2,1,0:T(8,128)(2,1)S(1)} collective-permute-done((bf16[2,256,512]{2,1,0:T(8,128)(2,1)S(1)}, bf16[2,256,512]{2,1,0:T(8,128)(2,1)S(1)}, u32[]{:S(2)}, u32[]{:S(2)}) %collective-permute-start) | collective-permute-done | bytes 524320 | tf_op jit(solution)/shard_map/ppermute | solution.py:42
  21.6 1.3 copy-done.2
  23.0 10.4 %all-to-all-done = bf16[128,8,256]{2,1,0:T(8,128)(2,1)S(1)} async-done(((bf16[128,8,256]{2,1,0:T(8,128)(2,1)}), bf16[128,8,256]{2,1,0:T(8,128)(2,1)S(1)}, u32[]{:S(2)}, u32[]{:S(2)}) %all-to-all-start) | async-done | bytes 524320 | tf_op jit(solution)/shard_map/all_to_all | solution.py:483
  33.4 1.5 collective-permute-start.3
  35.1 0.6 gather_fusion
  35.8 0.2 collective-permute-start.8
  36.0 1.3 collective-permute-start.7
  37.4 7.0 %collective-permute-done.8.three_ref = bf16[2,32,2048]{2,1,0:T(8,128)(2,1)S(1)} collective-permute-done((bf16[2,32,2048]{2,1,0:T(8,128)(2,1)S(1)}, bf16[2,32,2048]{2,1,0:T(8,128)(2,1)S(1)}, u32[]{:S(2)}, u32[]{:S(2)}) %collective-permute-start.8) | collective-permute-done | bytes 262176 | tf_op jit(solution)/shard_map/ppermute | solution.py:42
  44.4 1.3 collective-permute-done.7.one_ref
  45.9 2.6 %collective-permute-start.10 = (bf16[1,32,2048]{2,1,0:T(8,128)(2,1)S(1)}, bf16[1,32,2048]{2,1,0:T(8,128)(2,1)S(1)}, u32[]{:S(2)}, u32[]{:S(2)}) collective-permute-start(bf16[1,32,2048]{2,1,0:T(8,128)(2,1)S(1)} %get-tuple-element.86), channel_id=1, source_target_pairs={{0,3},{1,0},{2,1},{3,2},{4,7},{5,4},{6,5},{7,6},{8,11},{9,8},{10,9... | collective-permute-start | bytes 393224 | tf_op jit(solution)/shard_map/ppermute | solution.py:42
  48.5 4.2 %collective-permute-done.9.low_ref = bf16[1,32,2048]{2,1,0:T(8,128)(2,1)S(1)} collective-permute-done((bf16[1,32,2048]{2,1,0:T(8,128)(2,1)S(1)}, bf16[1,32,2048]{2,1,0:T(8,128)(2,1)S(1)}, u32[]{:S(2)}, u32[]{:S(2)}) %collective-permute-start.9) | collective-permute-done | bytes 131104 | tf_op jit(solution)/shard_map/ppermute | solution.py:42
  52.7 1.4 collective-permute-start.12
  54.4 3.5 %shard_map.106 = (f32[256,512]{1,0:T(8,128)S(1)}, f32[256,512]{1,0:T(8,128)S(1)}) custom-call(s32[4]{0:T(128)S(1)} %get-tuple-element.150.index_ref, bf16[8192,512]{1,0:T(8,128)(2,1)} %query_ref.11, bf16[512,8192]{1,0:T(8,128)(2,1)} %output_ref.11, bf16[4,2,256,512]{3,2,1,0:T(8,128)(2,1)S(1)} %copy-done.3), custom_call_target="tpu_custom_call" | custom-call | flops 1048576 | bytes 6144 | tf_op jit(solution)/shard_map/pallas_call | solution.py:235
  57.9 5.2 %collective-permute-done.4.three_ref.refs_1_ = bf16[4,2,256,512]{3,2,1,0:T(8,128)(2,1)S(1)} collective-permute-done((bf16[4,2,256,512]{3,2,1,0:T(8,128)(2,1)}, bf16[4,2,256,512]{3,2,1,0:T(8,128)(2,1)S(1)}, u32[]{:S(2)}, u32[]{:S(2)}) %collective-permute-start.4) | collective-permute-done | bytes 2097184 | tf_op jit(solution)/shard_map/ppermute | solution.py:46
  63.1 1.2 collective-permute-done.3.one_ref.refs_0_
  64.3 1.7 shard_map.105
  66.1 1.5 collective-permute-start.5
  67.6 1.3 shard_map.111
  68.9 5.3 %collective-permute-done.12.refs_1_.three_ref = bf16[4,64,2048]{2,1,0:T(8,128)(2,1)S(1)} collective-permute-done((bf16[4,64,2048]{2,1,0:T(8,128)(2,1)S(1)}, bf16[4,64,2048]{2,1,0:T(8,128)(2,1)S(1)}, u32[]{:S(2)}, u32[]{:S(2)}) %collective-permute-start.12) | collective-permute-done | bytes 1048608 | tf_op jit(solution)/shard_map/ppermute | solution.py:46
  74.2 1.2 collective-permute-done.11.refs_0_.one_ref
  75.5 6.3 %shard_map.107 = (f32[256,512]{1,0:T(8,128)S(1)}, f32[256,512]{1,0:T(8,128)S(1)}) custom-call(s32[8]{0:T(128)S(1)} %get-tuple-element.152.index_ref, bf16[8192,512]{1,0:T(8,128)(2,1)} %query_ref.11, bf16[512,8192]{1,0:T(8,128)(2,1)} %output_ref.11, bf16[4,2,256,512]{3,2,1,0:T(8,128)(2,1)} %collective-permute-done.3.one_ref.refs_0_, ...), custom_call_target="tpu_custom_call" | custom-call | flops 2097152 | bytes 12288 | tf_op jit(solution)/shard_map/pallas_call | solution.py:235
  81.7 0.3 collective-permute-start.13
  82.1 2.4 %collective-permute-start.14 = (bf16[2,64,2048]{2,1,0:T(8,128)(2,1)S(1)}, bf16[2,64,2048]{2,1,0:T(8,128)(2,1)S(1)}, u32[]{:S(2)}, u32[]{:S(2)}) collective-permute-start(bf16[2,64,2048]{2,1,0:T(8,128)(2,1)S(1)} %get-tuple-element.95), channel_id=1, source_target_pairs={{0,12},{1,13},{2,14},{3,15},{4,0},{5,1},{6,2},{7,3},{8,4},{9,5},{1... | collective-permute-start | bytes 1572872 | tf_op jit(solution)/shard_map/ppermute | solution.py:46
  84.5 2.3 %shard_map.112 = (bf16[512,512]{1,0:T(8,128)(2,1)S(1)}, bf16[512,512]{1,0:T(8,128)(2,1)S(1)}) custom-call(bf16[2048,512]{1,0:T(8,128)(2,1)S(1)} %copy-done, bf16[2048,512]{1,0:T(8,128)(2,1)S(1)} %copy-done.1, bf16[4,64,2048]{2,1,0:T(8,128)(2,1)S(1)} %collective-permute-done.11.refs_0_.one_ref, bf16[4,64,2048]{2,1,0:T(8,128)(2,1)S(1)} %collective-permute-done.12.refs_1_.three_ref), custom_call_target="tpu_custom_call" | custom-call | flops 2097152 | bytes 8192 | tf_op jit(solution)/shard_map/pallas_call | solution.py:370
  86.8 3.7 %shard_map.108 = (bf16[256,512]{1,0:T(8,128)(2,1)S(1)}, bf16[256,512]{1,0:T(8,128)(2,1)S(1)}) custom-call(s32[4]{0:T(128)S(1)} %get-tuple-element.149.index_ref, bf16[8192,512]{1,0:T(8,128)(2,1)} %query_ref.11, bf16[512,8192]{1,0:T(8,128)(2,1)} %output_ref.11, bf16[2,2,256,512]{3,2,1,0:T(8,128)(2,1)S(1)} %collective-permute-done.5.refs_0_, ...), custom_call_target="tpu_custom_call" | custom-call | flops 1048576 | bytes 6144 | tf_op jit(solution)/shard_map/pallas_call | solution.py:235
  90.6 1.7 collective-permute-done.13.refs_0_
  92.3 1.3 shard_map.114
  93.5 2.8 %shard_map.115 = (bf16[256,512]{1,0:T(8,128)(2,1)S(1)}, bf16[256,512]{1,0:T(8,128)(2,1)S(1)}, bf16[256,512]{1,0:T(8,128)(2,1)S(1)}, bf16[256,512]{1,0:T(8,128)(2...) custom-call(bf16[256,512]{1,0:T(8,128)(2,1)S(1)} %get-tuple-element., ...), custom_call_target="tpu_custom_call" | custom-call | flops 393216 | bytes 10240 | tf_op jit(solution)/shard_map/pallas_call | solution.py:454
  96.3 1.3 shard_map.116
  97.6 1.7 collective-permute-start.16
  99.3 3.6 %shard_map.117 = (bf16[4,256,512]{2,1,0:T(8,128)(2,1)S(1)}, bf16[4,256,512]{2,1,0:T(8,128)(2,1)S(1)}) custom-call(s32[4]{0:T(128)S(1)} %get-tuple-element.149.index_ref, bf16[8192,512]{1,0:T(8,128)(2,1)} %query_ref.11, bf16[512,8192]{1,0:T(8,128)(2,1)} %output_ref.11, bf16[256,512]{1,0:T(8,128)(2,1)S(1)} %get-tuple-element.129.c_ref, ...), custom_call_target="tpu_custom_call" | custom-call | flops 1048576 | bytes 8192 | tf_op jit(solution)/shard_map/pallas_call | solution.py:263
  102.9 3.5 %shard_map.118 = (bf16[4,256,512]{2,1,0:T(8,128)(2,1)S(1)}, bf16[4,256,512]{2,1,0:T(8,128)(2,1)S(1)}, bf16[1,256,512]{2,1,0:T(8,128)(2,1)S(1)}, bf16[1,256,512]{...) custom-call(bf16[2048,512]{1,0:T(8,128)(2,1)S(1)} %copy-done, ...), custom_call_target="tpu_custom_call" | custom-call | flops 3145728 | bytes 10240 | tf_op jit(solution)/shard_map/pallas_call | solution.py:399
  106.4 2.4 %collective-permute-done.15.low_ref = bf16[2,256,512]{2,1,0:T(8,128)(2,1)S(1)} collective-permute-done((bf16[2,256,512]{2,1,0:T(8,128)(2,1)S(1)}, bf16[2,256,512]{2,1,0:T(8,128)(2,1)S(1)}, u32[]{:S(2)}, u32[]{:S(2)}) %collective-permute-start.15) | collective-permute-done | bytes 524320 | tf_op jit(solution)/shard_map/ppermute | solution.py:46
  108.8 0.4 shard_map.119
  109.2 0.3 collective-permute-start.18
  109.6 1.2 collective-permute-start.17
  110.8 5.3 %shard_map.120 = (bf16[8,256,512]{2,1,0:T(8,128)(2,1)S(1)}, bf16[8,256,512]{2,1,0:T(8,128)(2,1)S(1)}) custom-call(s32[8]{0:T(128)S(1)} %get-tuple-element.151.index_ref, bf16[8192,512]{1,0:T(8,128)(2,1)} %query_ref.11, bf16[512,8192]{1,0:T(8,128)(2,1)} %output_ref.11, bf16[256,512]{1,0:T(8,128)(2,1)S(1)} %get-tuple-element.129.c_ref, ...), custom_call_target="tpu_custom_call" | custom-call | flops 2097152 | bytes 16384 | tf_op jit(solution)/shard_map/pallas_call | solution.py:263
  116.1 18.4 %collective-permute-done.18.refs_5_.part_ref = bf16[8,256,512]{2,1,0:T(8,128)(2,1)S(1)} collective-permute-done((bf16[8,256,512]{2,1,0:T(8,128)(2,1)S(1)}, bf16[8,256,512]{2,1,0:T(8,128)(2,1)S(1)}, u32[]{:S(2)}, u32[]{:S(2)}) %collective-permute-start.18) | collective-permute-done | bytes 2097184 | tf_op jit(solution)/shard_map/ppermute | solution.py:46
  134.5 1.5 collective-permute-done.17.refs_4_.part_ref
  136.0 0.4 shard_map.121
  136.4 1.6 shard_map.122
  138.0 1.6 shard_map.125
  139.6 2.7 %collective-permute-start.23 = (bf16[8,256,512]{2,1,0:T(8,128)(2,1)}, bf16[8,256,512]{2,1,0:T(8,128)(2,1)}, u32[]{:S(2)}, u32[]{:S(2)}) collective-permute-start(bf16[8,256,512]{2,1,0:T(8,128)(2,1)} %shard_map.125), channel_id=1, source_target_pairs={{0,12},{1,13},{2,14},{3,15},{4,0},{5,1},{6,2},{7,3},{8,4},{9,5},{1... | collective-permute-start | bytes 6291464 | tf_op jit(solution)/shard_map/ppermute | solution.py:46
  142.3 0.6 iota_reduce_fusion
  142.9 0.3 collective-permute-start.19
  143.3 1.2 collective-permute-start.20
  144.5 4.0 %collective-permute-done.19.refs_1_ = bf16[1,256,512]{2,1,0:T(8,128)(2,1)S(1)} collective-permute-done((bf16[1,256,512]{2,1,0:T(8,128)(2,1)S(1)}, bf16[1,256,512]{2,1,0:T(8,128)(2,1)S(1)}, u32[]{:S(2)}, u32[]{:S(2)}) %collective-permute-start.19) | collective-permute-done | bytes 262176 | tf_op jit(solution)/shard_map/ppermute | solution.py:42
  148.5 4.4 %collective-permute-done.20.refs_2_ = bf16[1,256,512]{2,1,0:T(8,128)(2,1)S(1)} collective-permute-done((bf16[1,256,512]{2,1,0:T(8,128)(2,1)S(1)}, bf16[1,256,512]{2,1,0:T(8,128)(2,1)S(1)}, u32[]{:S(2)}, u32[]{:S(2)}) %collective-permute-start.20) | collective-permute-done | bytes 262176 | tf_op jit(solution)/shard_map/ppermute | solution.py:42
  152.9 3.5 %collective-permute-done.21.refs_3_ = bf16[1,256,512]{2,1,0:T(8,128)(2,1)S(1)} collective-permute-done((bf16[1,256,512]{2,1,0:T(8,128)(2,1)S(1)}, bf16[1,256,512]{2,1,0:T(8,128)(2,1)S(1)}, u32[]{:S(2)}, u32[]{:S(2)}) %collective-permute-start.21) | collective-permute-done | bytes 262176 | tf_op jit(solution)/shard_map/ppermute | solution.py:42
  156.6 0.6 gather_fusion.1
  157.2 3.6 %shard_map.124 = (bf16[2,256,512]{2,1,0:T(8,128)(2,1)S(1)}, bf16[2,256,512]{2,1,0:T(8,128)(2,1)S(1)}, bf16[2,256,512]{2,1,0:T(8,128)(2,1)S(1)}, bf16[2,256,512]{2,1,0:T(8,128)(2,1)S(1)}) custom-call(s32[4]{0:T(128)S(1)} %get-tuple-element.150.index_ref, bf16[8192,512]{1,0:T(8,128)(2,1)} %query_ref.11, bf16[512,8192]{1,0:T(8,128)(2,1)} %output_ref.11, ...), custom_call_target="tpu_custom_call" | custom-call | flops 1048576 | bytes 8192 | tf_op jit(solution)/shard_map/pallas_call | solution.py:263
  160.8 9.4 %collective-permute-done.22.refs_4_ = bf16[8,256,512]{2,1,0:T(8,128)(2,1)S(1)} collective-permute-done((bf16[8,256,512]{2,1,0:T(8,128)(2,1)}, bf16[8,256,512]{2,1,0:T(8,128)(2,1)S(1)}, u32[]{:S(2)}, u32[]{:S(2)}) %collective-permute-start.22) | collective-permute-done | bytes 2097184 | tf_op jit(solution)/shard_map/ppermute | solution.py:46
  170.2 1.0 collective-permute-done.23.refs_5_
  171.2 2.3 %shard_map.126 = (bf16[2,256,512]{2,1,0:T(8,128)(2,1)S(1)}, bf16[2,256,512]{2,1,0:T(8,128)(2,1)S(1)}, bf16[2,256,512]{2,1,0:T(8,128)(2,1)S(1)}, bf16[2,256,512]{2,1,0:T(8,128)(2,1)S(1)}) custom-call(bf16[2,256,512]{2,1,0:T(8,128)(2,1)S(1)} %get-tuple-element.130.refs_0_, bf16[2,256,512]{2,1,0:T(8,128)(2,1)S(1)} %get-tuple-element.131.refs_1_, ...), custom_call_target="tpu_custom_call" | custom-call | flops 8192 | bytes 8192 | tf_op jit(solution)/shard_map/pallas_call | solution.py:329
  173.5 0.4 collective-permute-start.24
  173.9 1.2 collective-permute-start.25
  175.3 26.3 %all_to_all.10 = bf16[128,8,256]{2,1,0:T(8,128)(2,1)S(1)} all-to-all(bf16[128,8,256]{2,1,0:T(8,128)(2,1)S(1)} %bitcast.33), channel_id=1, replica_groups=mesh['seq'=8,'enc'=16] {'seq','enc'}, dimensions={0} | all-to-all | bytes 1048576 | tf_op jit(solution)/shard_map/all_to_all | solution.py:534
  201.6 1.0 shard_map.127
  202.5 0.8 copy.25
  (52 shorter events, 1.7 us)
Async XLA Ops:
  1.7 16.4 %collective-permute-start.2 = (bf16[2,256,512]{2,1,0:T(8,128)(2,1)S(1)}, bf16[2,256,512]{2,1,0:T(8,128)(2,1)S(1)}, u32[]{:S(2)}, u32[]{:S(2)}) collective-permute-start(bf16[2,256,512]{2,1,0:T(8,128)(2,1)S(1)} %shard_map.103.refs_0_), channel_id=1, source_target_pairs={{0,3},{1,0},{2,1},{3,2},{4,7},{5,4},{6,5},{7,6},{8,11},{9,8},{10,9... | collective-permute-start | bytes 1572872 | tf_op jit(solution)/shard_map/ppermute | solution.py:42
  6.3 11.7 %collective-permute-start.1 = (bf16[2,256,512]{2,1,0:T(8,128)(2,1)S(1)}, bf16[2,256,512]{2,1,0:T(8,128)(2,1)S(1)}, u32[]{:S(2)}, u32[]{:S(2)}) collective-permute-start(bf16[2,256,512]{2,1,0:T(8,128)(2,1)S(1)} %shard_map.103.refs_0_), channel_id=1, source_target_pairs={{0,2},{1,3},{2,0},{3,1},{4,6},{5,7},{6,4},{7,5},{8,10},{9,11},{10,... | collective-permute-start | bytes 1572872 | tf_op jit(solution)/shard_map/ppermute | solution.py:42
  6.3 15.2 %collective-permute-start = (bf16[2,256,512]{2,1,0:T(8,128)(2,1)S(1)}, bf16[2,256,512]{2,1,0:T(8,128)(2,1)S(1)}, u32[]{:S(2)}, u32[]{:S(2)}) collective-permute-start(bf16[2,256,512]{2,1,0:T(8,128)(2,1)S(1)} %shard_map.103.refs_0_), channel_id=1, source_target_pairs={{0,1},{1,2},{2,3},{3,0},{4,5},{5,6},{6,7},{7,4},{8,9},{9,10},{10,1... | collective-permute-start | bytes 1572872 | tf_op jit(solution)/shard_map/ppermute | solution.py:42
  7.0 26.3 %all-to-all-start = ((bf16[128,8,256]{2,1,0:T(8,128)(2,1)}), bf16[128,8,256]{2,1,0:T(8,128)(2,1)S(1)}, u32[]{:S(2)}, u32[]{:S(2)}) async-start(bf16[128,8,256]{2,1,0:T(8,128)(2,1)} %bitcast.35), calls=%async_computation | async-start | bytes 1048576 | tf_op jit(solution)/shard_map/all_to_all | solution.py:483
  17.0 17.8 %copy-start.4 = (s32[4,2]{0,1:T(2,128)S(1)}, s32[4,2]{0,1:T(2,128)}, u32[]{:S(2)}) copy-start(s32[4,2]{0,1:T(2,128)} %param.14) | copy-start | bytes 100
  21.6 1.4 copy-start.2
  33.4 29.7 %collective-permute-start.4 = (bf16[4,2,256,512]{3,2,1,0:T(8,128)(2,1)}, bf16[4,2,256,512]{3,2,1,0:T(8,128)(2,1)S(1)}, u32[]{:S(2)}, u32[]{:S(2)}) collective-permute-start(bf16[4,2,256,512]{3,2,1,0:T(8,128)(2,1)} %copy-done.2), channel_id=1, source_target_pairs={{0,12},{1,13},{2,14},{3,15},{4,0},{5,1},{6,2},{7,3},{8,4},{9,5},{1... | collective-permute-start | bytes 6291464 | tf_op jit(solution)/shard_map/ppermute | solution.py:46
  33.4 30.9 %collective-permute-start.3 = (bf16[4,2,256,512]{3,2,1,0:T(8,128)(2,1)}, bf16[4,2,256,512]{3,2,1,0:T(8,128)(2,1)}, u32[]{:S(2)}, u32[]{:S(2)}) collective-permute-start(bf16[4,2,256,512]{3,2,1,0:T(8,128)(2,1)} %copy-done.2), channel_id=1, source_target_pairs={{0,4},{1,5},{2,6},{3,7},{4,8},{5,9},{6,10},{7,11},{8,12},{9,13},{1... | collective-permute-start | bytes 6291464 | tf_op jit(solution)/shard_map/ppermute | solution.py:46
  35.8 8.6 %collective-permute-start.8 = (bf16[2,32,2048]{2,1,0:T(8,128)(2,1)S(1)}, bf16[2,32,2048]{2,1,0:T(8,128)(2,1)S(1)}, u32[]{:S(2)}, u32[]{:S(2)}) collective-permute-start(bf16[2,32,2048]{2,1,0:T(8,128)(2,1)S(1)} %bitcast.28), channel_id=1, source_target_pairs={{0,3},{1,0},{2,1},{3,2},{4,7},{5,4},{6,5},{7,6},{8,11},{9,8},{10,9... | collective-permute-start | bytes 786440 | tf_op jit(solution)/shard_map/ppermute | solution.py:42
  36.0 9.6 %collective-permute-start.7 = (bf16[2,32,2048]{2,1,0:T(8,128)(2,1)S(1)}, bf16[2,32,2048]{2,1,0:T(8,128)(2,1)S(1)}, u32[]{:S(2)}, u32[]{:S(2)}) collective-permute-start(bf16[2,32,2048]{2,1,0:T(8,128)(2,1)S(1)} %bitcast.29), channel_id=1, source_target_pairs={{0,1},{1,2},{2,3},{3,0},{4,5},{5,6},{6,7},{7,4},{8,9},{9,10},{10,1... | collective-permute-start | bytes 786440 | tf_op jit(solution)/shard_map/ppermute | solution.py:42
  45.7 7.0 %collective-permute-start.9 = (bf16[1,32,2048]{2,1,0:T(8,128)(2,1)S(1)}, bf16[1,32,2048]{2,1,0:T(8,128)(2,1)S(1)}, u32[]{:S(2)}, u32[]{:S(2)}) collective-permute-start(bf16[1,32,2048]{2,1,0:T(8,128)(2,1)S(1)} %get-tuple-element.85), channel_id=1, source_target_pairs={{0,1},{1,2},{2,3},{3,0},{4,5},{5,6},{6,7},{7,4},{8,9},{9,10},{10,1... | collective-permute-start | bytes 393224 | tf_op jit(solution)/shard_map/ppermute | solution.py:42
  45.9 6.8 %collective-permute-start.10 = (bf16[1,32,2048]{2,1,0:T(8,128)(2,1)S(1)}, bf16[1,32,2048]{2,1,0:T(8,128)(2,1)S(1)}, u32[]{:S(2)}, u32[]{:S(2)}) collective-permute-start(bf16[1,32,2048]{2,1,0:T(8,128)(2,1)S(1)} %get-tuple-element.86), channel_id=1, source_target_pairs={{0,3},{1,0},{2,1},{3,2},{4,7},{5,4},{6,5},{7,6},{8,11},{9,8},{10,9... | collective-permute-start | bytes 393224 | tf_op jit(solution)/shard_map/ppermute | solution.py:42
  48.5 5.9 %copy-start.3 = (bf16[4,2,256,512]{3,2,1,0:T(8,128)(2,1)S(1)}, bf16[4,2,256,512]{3,2,1,0:T(8,128)(2,1)}, u32[]{:S(2)}) copy-start(bf16[4,2,256,512]{3,2,1,0:T(8,128)(2,1)} %copy-done.2) | copy-start | bytes 6291460
  52.7 21.4 %collective-permute-start.12 = (bf16[4,64,2048]{2,1,0:T(8,128)(2,1)S(1)}, bf16[4,64,2048]{2,1,0:T(8,128)(2,1)S(1)}, u32[]{:S(2)}, u32[]{:S(2)}) collective-permute-start(bf16[4,64,2048]{2,1,0:T(8,128)(2,1)S(1)} %bitcast.24), channel_id=1, source_target_pairs={{0,12},{1,13},{2,14},{3,15},{4,0},{5,1},{6,2},{7,3},{8,4},{9,5},{1... | collective-permute-start | bytes 3145736 | tf_op jit(solution)/shard_map/ppermute | solution.py:46
  54.2 21.3 %collective-permute-start.11 = (bf16[4,64,2048]{2,1,0:T(8,128)(2,1)S(1)}, bf16[4,64,2048]{2,1,0:T(8,128)(2,1)S(1)}, u32[]{:S(2)}, u32[]{:S(2)}) collective-permute-start(bf16[4,64,2048]{2,1,0:T(8,128)(2,1)S(1)} %bitcast.25), channel_id=1, source_target_pairs={{0,4},{1,5},{2,6},{3,7},{4,8},{5,9},{6,10},{7,11},{8,12},{9,13},{1... | collective-permute-start | bytes 3145736 | tf_op jit(solution)/shard_map/ppermute | solution.py:46
  57.9 9.8 %copy-start = (bf16[2048,512]{1,0:T(8,128)(2,1)S(1)}, bf16[2048,512]{1,0:T(8,128)(2,1)}, u32[]{:S(2)}) copy-start(bf16[2048,512]{1,0:T(8,128)(2,1)} %key_ref.9) | copy-start | bytes 6291460
  57.9 9.7 %copy-start.1 = (bf16[2048,512]{1,0:T(8,128)(2,1)S(1)}, bf16[2048,512]{1,0:T(8,128)(2,1)}, u32[]{:S(2)}) copy-start(bf16[2048,512]{1,0:T(8,128)(2,1)} %value_ref.9) | copy-start | bytes 6291460
  66.0 20.8 %collective-permute-start.6 = (bf16[2,2,256,512]{3,2,1,0:T(8,128)(2,1)S(1)}, bf16[2,2,256,512]{3,2,1,0:T(8,128)(2,1)S(1)}, u32[]{:S(2)}, u32[]{:S(2)}) collective-permute-start(bf16[2,2,256,512]{3,2,1,0:T(8,128)(2,1)S(1)} %get-tuple-element.80), channel_id=1, source_target_pairs={{0,12},{1,13},{2,14},{3,15},{4,0},{5,1},{6,2},{7,3},{8,4},{9,5},{1... | collective-permute-start | bytes 3145736 | tf_op jit(solution)/shard_map/ppermute | solution.py:46
  66.1 20.7 %collective-permute-start.5 = (bf16[2,2,256,512]{3,2,1,0:T(8,128)(2,1)S(1)}, bf16[2,2,256,512]{3,2,1,0:T(8,128)(2,1)S(1)}, u32[]{:S(2)}, u32[]{:S(2)}) collective-permute-start(bf16[2,2,256,512]{3,2,1,0:T(8,128)(2,1)S(1)} %get-tuple-element.78), channel_id=1, source_target_pairs={{0,4},{1,5},{2,6},{3,7},{4,8},{5,9},{6,10},{7,11},{8,12},{9,13},{1... | collective-permute-start | bytes 3145736 | tf_op jit(solution)/shard_map/ppermute | solution.py:46
  81.7 10.5 %collective-permute-start.13 = (bf16[2,64,2048]{2,1,0:T(8,128)(2,1)S(1)}, bf16[2,64,2048]{2,1,0:T(8,128)(2,1)S(1)}, u32[]{:S(2)}, u32[]{:S(2)}) collective-permute-start(bf16[2,64,2048]{2,1,0:T(8,128)(2,1)S(1)} %get-tuple-element.91), channel_id=1, source_target_pairs={{0,4},{1,5},{2,6},{3,7},{4,8},{5,9},{6,10},{7,11},{8,12},{9,13},{1... | collective-permute-start | bytes 1572872 | tf_op jit(solution)/shard_map/ppermute | solution.py:46
  82.1 10.2 %collective-permute-start.14 = (bf16[2,64,2048]{2,1,0:T(8,128)(2,1)S(1)}, bf16[2,64,2048]{2,1,0:T(8,128)(2,1)S(1)}, u32[]{:S(2)}, u32[]{:S(2)}) collective-permute-start(bf16[2,64,2048]{2,1,0:T(8,128)(2,1)S(1)} %get-tuple-element.95), channel_id=1, source_target_pairs={{0,12},{1,13},{2,14},{3,15},{4,0},{5,1},{6,2},{7,3},{8,4},{9,5},{1... | collective-permute-start | bytes 1572872 | tf_op jit(solution)/shard_map/ppermute | solution.py:46
  97.6 8.8 %collective-permute-start.16 = (bf16[2,256,512]{2,1,0:T(8,128)(2,1)S(1)}, bf16[2,256,512]{2,1,0:T(8,128)(2,1)S(1)}, u32[]{:S(2)}, u32[]{:S(2)}) collective-permute-start(bf16[2,256,512]{2,1,0:T(8,128)(2,1)S(1)} %get-tuple-element.115), channel_id=1, source_target_pairs={{0,12},{1,13},{2,14},{3,15},{4,0},{5,1},{6,2},{7,3},{8,4},{9,5},{1... | collective-permute-start | bytes 1572872 | tf_op jit(solution)/shard_map/ppermute | solution.py:46
  99.3 9.5 %collective-permute-start.15 = (bf16[2,256,512]{2,1,0:T(8,128)(2,1)S(1)}, bf16[2,256,512]{2,1,0:T(8,128)(2,1)S(1)}, u32[]{:S(2)}, u32[]{:S(2)}) collective-permute-start(bf16[2,256,512]{2,1,0:T(8,128)(2,1)S(1)} %get-tuple-element.102), channel_id=1, source_target_pairs={{0,4},{1,5},{2,6},{3,7},{4,8},{5,9},{6,10},{7,11},{8,12},{9,13},{1... | collective-permute-start | bytes 1572872 | tf_op jit(solution)/shard_map/ppermute | solution.py:46
  109.2 25.2 %collective-permute-start.18 = (bf16[8,256,512]{2,1,0:T(8,128)(2,1)S(1)}, bf16[8,256,512]{2,1,0:T(8,128)(2,1)S(1)}, u32[]{:S(2)}, u32[]{:S(2)}) collective-permute-start(bf16[8,256,512]{2,1,0:T(8,128)(2,1)S(1)} %get-tuple-element.123), channel_id=1, source_target_pairs={{0,12},{1,13},{2,14},{3,15},{4,0},{5,1},{6,2},{7,3},{8,4},{9,5},{1... | collective-permute-start | bytes 6291464 | tf_op jit(solution)/shard_map/ppermute | solution.py:46
  109.6 26.4 %collective-permute-start.17 = (bf16[8,256,512]{2,1,0:T(8,128)(2,1)S(1)}, bf16[8,256,512]{2,1,0:T(8,128)(2,1)S(1)}, u32[]{:S(2)}, u32[]{:S(2)}) collective-permute-start(bf16[8,256,512]{2,1,0:T(8,128)(2,1)S(1)} %get-tuple-element.116), channel_id=1, source_target_pairs={{0,4},{1,5},{2,6},{3,7},{4,8},{5,9},{6,10},{7,11},{8,12},{9,13},{1... | collective-permute-start | bytes 6291464 | tf_op jit(solution)/shard_map/ppermute | solution.py:46
  138.0 32.2 %collective-permute-start.22 = (bf16[8,256,512]{2,1,0:T(8,128)(2,1)}, bf16[8,256,512]{2,1,0:T(8,128)(2,1)S(1)}, u32[]{:S(2)}, u32[]{:S(2)}) collective-permute-start(bf16[8,256,512]{2,1,0:T(8,128)(2,1)} %shard_map.122), channel_id=1, source_target_pairs={{0,4},{1,5},{2,6},{3,7},{4,8},{5,9},{6,10},{7,11},{8,12},{9,13},{1... | collective-permute-start | bytes 6291464 | tf_op jit(solution)/shard_map/ppermute | solution.py:46
  139.6 31.6 %collective-permute-start.23 = (bf16[8,256,512]{2,1,0:T(8,128)(2,1)}, bf16[8,256,512]{2,1,0:T(8,128)(2,1)}, u32[]{:S(2)}, u32[]{:S(2)}) collective-permute-start(bf16[8,256,512]{2,1,0:T(8,128)(2,1)} %shard_map.125), channel_id=1, source_target_pairs={{0,12},{1,13},{2,14},{3,15},{4,0},{5,1},{6,2},{7,3},{8,4},{9,5},{1... | collective-permute-start | bytes 6291464 | tf_op jit(solution)/shard_map/ppermute | solution.py:46
  142.9 5.5 %collective-permute-start.19 = (bf16[1,256,512]{2,1,0:T(8,128)(2,1)S(1)}, bf16[1,256,512]{2,1,0:T(8,128)(2,1)S(1)}, u32[]{:S(2)}, u32[]{:S(2)}) collective-permute-start(bf16[1,256,512]{2,1,0:T(8,128)(2,1)S(1)} %get-tuple-element.125), channel_id=1, source_target_pairs={{0,3},{1,0},{2,1},{3,2},{4,7},{5,4},{6,5},{7,6},{8,11},{9,8},{10,9... | collective-permute-start | bytes 786440 | tf_op jit(solution)/shard_map/ppermute | solution.py:42
  143.3 9.6 %collective-permute-start.20 = (bf16[1,256,512]{2,1,0:T(8,128)(2,1)S(1)}, bf16[1,256,512]{2,1,0:T(8,128)(2,1)S(1)}, u32[]{:S(2)}, u32[]{:S(2)}) collective-permute-start(bf16[1,256,512]{2,1,0:T(8,128)(2,1)S(1)} %get-tuple-element.126), channel_id=1, source_target_pairs={{0,2},{1,3},{2,0},{3,1},{4,6},{5,7},{6,4},{7,5},{8,10},{9,11},{10,... | collective-permute-start | bytes 786440 | tf_op jit(solution)/shard_map/ppermute | solution.py:42
  144.5 11.9 %collective-permute-start.21 = (bf16[1,256,512]{2,1,0:T(8,128)(2,1)S(1)}, bf16[1,256,512]{2,1,0:T(8,128)(2,1)S(1)}, u32[]{:S(2)}, u32[]{:S(2)}) collective-permute-start(bf16[1,256,512]{2,1,0:T(8,128)(2,1)S(1)} %get-tuple-element.127), channel_id=1, source_target_pairs={{0,1},{1,2},{2,3},{3,0},{4,5},{5,6},{6,7},{7,4},{8,9},{9,10},{10,1... | collective-permute-start | bytes 786440 | tf_op jit(solution)/shard_map/ppermute | solution.py:42
  173.5 28.0 %collective-permute-start.24 = (bf16[2,256,512]{2,1,0:T(8,128)(2,1)S(1)}, bf16[2,256,512]{2,1,0:T(8,128)(2,1)S(1)}, u32[]{:S(2)}, u32[]{:S(2)}) collective-permute-start(bf16[2,256,512]{2,1,0:T(8,128)(2,1)S(1)} %get-tuple-element.138), channel_id=1, source_target_pairs={{0,3},{1,0},{2,1},{3,2},{4,7},{5,4},{6,5},{7,6},{8,11},{9,8},{10,9... | collective-permute-start | bytes 1572872 | tf_op jit(solution)/shard_map/ppermute | solution.py:42
  173.9 27.6 %collective-permute-start.25 = (bf16[2,256,512]{2,1,0:T(8,128)(2,1)S(1)}, bf16[2,256,512]{2,1,0:T(8,128)(2,1)S(1)}, u32[]{:S(2)}, u32[]{:S(2)}) collective-permute-start(bf16[2,256,512]{2,1,0:T(8,128)(2,1)S(1)} %get-tuple-element.139), channel_id=1, source_target_pairs={{0,2},{1,3},{2,0},{3,1},{4,6},{5,7},{6,4},{7,5},{8,10},{9,11},{10,... | collective-permute-start | bytes 1572872 | tf_op jit(solution)/shard_map/ppermute | solution.py:42
  175.1 26.5 %collective-permute-start.26 = (bf16[2,256,512]{2,1,0:T(8,128)(2,1)S(1)}, bf16[2,256,512]{2,1,0:T(8,128)(2,1)S(1)}, u32[]{:S(2)}, u32[]{:S(2)}) collective-permute-start(bf16[2,256,512]{2,1,0:T(8,128)(2,1)S(1)} %get-tuple-element.140), channel_id=1, source_target_pairs={{0,1},{1,2},{2,3},{3,0},{4,5},{5,6},{6,7},{7,4},{8,9},{9,10},{10,1... | collective-permute-start | bytes 1572872 | tf_op jit(solution)/shard_map/ppermute | solution.py:42

commit v6 on v5

--- a/solution.py
+++ b/solution.py
@@ -318,39 +318,40 @@
 
 
 def add_pieces_kernel(*refs):
-    r3_ref, r1_ref = refs[4:6]
-    for n in range(4):
+    r3_ref, r1_ref = refs[3:5]
+    for n in range(3):
         tiles = refs[n].shape[0]
         for m in range(tiles):
-            refs[6 + n][m] = plus(refs[n][m], r3_ref[n * tiles + m], r1_ref[n * tiles + m])
+            at = (n + 1) * tiles + m
+            refs[5 + n][m] = plus(refs[n][m], r3_ref[at], r1_ref[at])
 
 
 def add_pieces(pieces, r3, r1):
     return pl.pallas_call(
         add_pieces_kernel,
-        out_shape=[jax.ShapeDtypeStruct(pieces[0].shape, BF)] * 4,
-        in_specs=in_vmem(6),
-        out_specs=in_vmem(4),
+        out_shape=[jax.ShapeDtypeStruct(pieces[0].shape, BF)] * 3,
+        in_specs=in_vmem(5),
+        out_specs=in_vmem(3),
         compiler_params=params(8),
         cost_estimate=cost(8 * r3.size, 8 * r3.size),
-    )(*pieces, r3, r1)
+    )(*pieces[1:], r3, r1)
 
 
 def move_pieces(pieces):
-    return move_u(pieces[1], -1), move_u(pieces[2], 2), move_u(pieces[3], 1)
-
-
-def finish_kernel(*refs):
-    for n, ref in enumerate(refs[4:]):
-        ref[...] = plus(*[part[n] for part in refs[:4]])
+    return move_u(pieces[0], -1), move_u(pieces[1], 2), move_u(pieces[2], 1)
+
+
+def finish_kernel(count, *refs):
+    for n, ref in enumerate(refs[count:]):
+        ref[...] = plus(*[part[n] for part in refs[:count]])
 
 
 def finish(*parts):
     tiles = parts[0].shape[0]
     return pl.pallas_call(
-        finish_kernel,
+        functools.partial(finish_kernel, len(parts)),
         out_shape=[jax.ShapeDtypeStruct(parts[0].shape[1:], BF)] * tiles,
-        in_specs=in_vmem(4),
+        in_specs=in_vmem(len(parts)),
         out_specs=in_vmem(tiles),
         compiler_params=params(8),
         cost_estimate=cost(4 * parts[0].size, 10 * parts[0].size),
@@ -520,10 +521,10 @@
     g3 = add_half(both_side[0], after(from_up, *pieces), True)
     g1 = add_half(both_side[1], after(from_down, g3), False)
     r3, r1 = move_v(g3, 1), move_v(g1, -1)
-    (summed,) = finish(pieces[0], *move_pieces(pieces))
+    (summed,) = finish(rest[2], from_up, from_down, *move_pieces(pieces))
     both_near = both_terms(index[0], [2] * 4, g3, summed)
     both_pieces = add_pieces(both_near, after(r3, summed), r1)
-    output, d_hidden = finish(both_pieces[0], *move_pieces(both_pieces))
+    output, d_hidden = finish(both_near[0], r3, r1, *move_pieces(both_pieces))
 
     placing = lax.broadcasted_iota(jnp.int32, (ENC, used), 0) == slot_shard[None, :]
     spread = summed.reshape(-1, used, chunk, cols // local, local).transpose(0, 3, 1, 2, 4)

time: 204 us -> 205 us (level)
  no operation moved by 1% of the time
where the time goes in v6:
time: 205 us
  waiting for transfers between devices  86.5 us (42%)
  Pallas kernels  50.4 us (25%)
  starting transfers between devices  35.9 us (18%)
  blocking collectives  26.3 us (13%)
  local copies, waits for them, and re-layouts  3.68 us (2%)
    ppermute x14, waiting for transfers between devices, move_v(): return lax.ppermute(value, AXES, shift_table(True, shift))  47.3 us
    ppermute x13, waiting for transfers between devices, move_u(): return lax.ppermute(value, AXES, shift_table(False, shift))  28.8 us
    all_to_all x1, blocking collectives, on_device(): lax.all_to_all(after(spread, *both_pieces).reshape(SEQ * ENC, chunk, loca...  26.3 us
    pallas_call x3, Pallas kernels, gathered_dots(): pl.pallas_call(functools.partial(gathered_kernel, counts, start is not No...  13.5 us
    ppermute x14, starting transfers between devices, move_v(): return lax.ppermute(value, AXES, shift_table(True, shift))  13.2 us
    ppermute x13, starting transfers between devices, move_u(): return lax.ppermute(value, AXES, shift_table(False, shift))  12.7 us
    pallas_call x3, Pallas kernels, call(): pl.pallas_call(functools.partial(terms_kernel, count), out_shape=[jax.Sha...  12.4 us
    all_to_all x1, waiting for transfers between devices, on_device(): lax.all_to_all(neighbour_states.reshape(SEQ * ENC, chunk, local), AXES, s...  10.4 us
  transfers between devices with their start and end apart: 28, of which 19 were waited for; matrix products, arithmetic and copies ran while one was open for 1% of the time, Pallas kernels for 18%

profile of v6, /device:TPU:1, one launch (start us, length us, event | category | flops | bytes accessed | tf_op | source)
XLA Modules:
  0.0 204.8 jit_solution(15012498507446103649)
XLA Ops:
  0.6 1.0 shard_map.103.refs_0_
  1.7 4.7 %collective-permute-start.2 = (bf16[2,256,512]{2,1,0:T(8,128)(2,1)S(1)}, bf16[2,256,512]{2,1,0:T(8,128)(2,1)S(1)}, u32[]{:S(2)}, u32[]{:S(2)}) collective-permute-start(bf16[2,256,512]{2,1,0:T(8,128)(2,1)S(1)} %shard_map.103.refs_0_), channel_id=1, source_target_pairs={{0,3},{1,0},{2,1},{3,2},{4,7},{5,4},{6,5},{7,6},{8,11},{9,8},{10,9... | collective-permute-start | bytes 1572872 | tf_op jit(solution)/shard_map/ppermute | solution.py:42
  6.3 0.7 collective-permute-start
  7.0 10.0 %all-to-all-start = ((bf16[128,8,256]{2,1,0:T(8,128)(2,1)}), bf16[128,8,256]{2,1,0:T(8,128)(2,1)S(1)}, u32[]{:S(2)}, u32[]{:S(2)}) async-start(bf16[128,8,256]{2,1,0:T(8,128)(2,1)} %bitcast.35), calls=%async_computation | async-start | bytes 1048576 | tf_op jit(solution)/shard_map/all_to_all | solution.py:484
  17.0 1.0 collective-permute-done.2.refs_3_
  18.1 3.4 %collective-permute-done.refs_1_ = bf16[2,256,512]{2,1,0:T(8,128)(2,1)S(1)} collective-permute-done((bf16[2,256,512]{2,1,0:T(8,128)(2,1)S(1)}, bf16[2,256,512]{2,1,0:T(8,128)(2,1)S(1)}, u32[]{:S(2)}, u32[]{:S(2)}) %collective-permute-start) | collective-permute-done | bytes 524320 | tf_op jit(solution)/shard_map/ppermute | solution.py:42
  21.6 1.3 copy-done.2
  23.0 10.4 %all-to-all-done = bf16[128,8,256]{2,1,0:T(8,128)(2,1)S(1)} async-done(((bf16[128,8,256]{2,1,0:T(8,128)(2,1)}), bf16[128,8,256]{2,1,0:T(8,128)(2,1)S(1)}, u32[]{:S(2)}, u32[]{:S(2)}) %all-to-all-start) | async-done | bytes 524320 | tf_op jit(solution)/shard_map/all_to_all | solution.py:484
  33.4 1.5 collective-permute-start.3
  35.1 0.6 gather_fusion
  35.8 0.2 collective-permute-start.8
  36.0 1.3 collective-permute-start.7
  37.4 7.0 %collective-permute-done.8.three_ref = bf16[2,32,2048]{2,1,0:T(8,128)(2,1)S(1)} collective-permute-done((bf16[2,32,2048]{2,1,0:T(8,128)(2,1)S(1)}, bf16[2,32,2048]{2,1,0:T(8,128)(2,1)S(1)}, u32[]{:S(2)}, u32[]{:S(2)}) %collective-permute-start.8) | collective-permute-done | bytes 262176 | tf_op jit(solution)/shard_map/ppermute | solution.py:42
  44.4 1.3 collective-permute-done.7.one_ref
  45.9 2.6 %collective-permute-start.10 = (bf16[1,32,2048]{2,1,0:T(8,128)(2,1)S(1)}, bf16[1,32,2048]{2,1,0:T(8,128)(2,1)S(1)}, u32[]{:S(2)}, u32[]{:S(2)}) collective-permute-start(bf16[1,32,2048]{2,1,0:T(8,128)(2,1)S(1)} %get-tuple-element.84), channel_id=1, source_target_pairs={{0,3},{1,0},{2,1},{3,2},{4,7},{5,4},{6,5},{7,6},{8,11},{9,8},{10,9... | collective-permute-start | bytes 393224 | tf_op jit(solution)/shard_map/ppermute | solution.py:42
  48.5 4.2 %collective-permute-done.9.low_ref = bf16[1,32,2048]{2,1,0:T(8,128)(2,1)S(1)} collective-permute-done((bf16[1,32,2048]{2,1,0:T(8,128)(2,1)S(1)}, bf16[1,32,2048]{2,1,0:T(8,128)(2,1)S(1)}, u32[]{:S(2)}, u32[]{:S(2)}) %collective-permute-start.9) | collective-permute-done | bytes 131104 | tf_op jit(solution)/shard_map/ppermute | solution.py:42
  52.7 1.4 collective-permute-start.12
  54.4 3.5 %shard_map.106 = (f32[256,512]{1,0:T(8,128)S(1)}, f32[256,512]{1,0:T(8,128)S(1)}) custom-call(s32[4]{0:T(128)S(1)} %get-tuple-element.146.index_ref, bf16[8192,512]{1,0:T(8,128)(2,1)} %query_ref.11, bf16[512,8192]{1,0:T(8,128)(2,1)} %output_ref.11, bf16[4,2,256,512]{3,2,1,0:T(8,128)(2,1)S(1)} %copy-done.3), custom_call_target="tpu_custom_call" | custom-call | flops 1048576 | bytes 6144 | tf_op jit(solution)/shard_map/pallas_call | solution.py:235
  57.9 5.2 %collective-permute-done.4.three_ref.refs_1_ = bf16[4,2,256,512]{3,2,1,0:T(8,128)(2,1)S(1)} collective-permute-done((bf16[4,2,256,512]{3,2,1,0:T(8,128)(2,1)}, bf16[4,2,256,512]{3,2,1,0:T(8,128)(2,1)S(1)}, u32[]{:S(2)}, u32[]{:S(2)}) %collective-permute-start.4) | collective-permute-done | bytes 2097184 | tf_op jit(solution)/shard_map/ppermute | solution.py:46
  63.1 1.2 collective-permute-done.3.one_ref.refs_0_
  64.3 1.7 shard_map.105
  66.1 1.5 collective-permute-start.5
  67.6 1.3 shard_map.111
  68.9 5.3 %collective-permute-done.12.refs_1_.three_ref = bf16[4,64,2048]{2,1,0:T(8,128)(2,1)S(1)} collective-permute-done((bf16[4,64,2048]{2,1,0:T(8,128)(2,1)S(1)}, bf16[4,64,2048]{2,1,0:T(8,128)(2,1)S(1)}, u32[]{:S(2)}, u32[]{:S(2)}) %collective-permute-start.12) | collective-permute-done | bytes 1048608 | tf_op jit(solution)/shard_map/ppermute | solution.py:46
  74.2 1.2 collective-permute-done.11.refs_0_.one_ref
  75.5 6.3 %shard_map.107 = (f32[256,512]{1,0:T(8,128)S(1)}, f32[256,512]{1,0:T(8,128)S(1)}) custom-call(s32[8]{0:T(128)S(1)} %get-tuple-element.148.index_ref, bf16[8192,512]{1,0:T(8,128)(2,1)} %query_ref.11, bf16[512,8192]{1,0:T(8,128)(2,1)} %output_ref.11, bf16[4,2,256,512]{3,2,1,0:T(8,128)(2,1)} %collective-permute-done.3.one_ref.refs_0_, ...), custom_call_target="tpu_custom_call" | custom-call | flops 2097152 | bytes 12288 | tf_op jit(solution)/shard_map/pallas_call | solution.py:235
  81.7 0.3 collective-permute-start.13
  82.1 2.4 %collective-permute-start.14 = (bf16[2,64,2048]{2,1,0:T(8,128)(2,1)S(1)}, bf16[2,64,2048]{2,1,0:T(8,128)(2,1)S(1)}, u32[]{:S(2)}, u32[]{:S(2)}) collective-permute-start(bf16[2,64,2048]{2,1,0:T(8,128)(2,1)S(1)} %get-tuple-element.93), channel_id=1, source_target_pairs={{0,12},{1,13},{2,14},{3,15},{4,0},{5,1},{6,2},{7,3},{8,4},{9,5},{1... | collective-permute-start | bytes 1572872 | tf_op jit(solution)/shard_map/ppermute | solution.py:46
  84.5 2.3 %shard_map.112 = (bf16[512,512]{1,0:T(8,128)(2,1)S(1)}, bf16[512,512]{1,0:T(8,128)(2,1)S(1)}) custom-call(bf16[2048,512]{1,0:T(8,128)(2,1)S(1)} %copy-done, bf16[2048,512]{1,0:T(8,128)(2,1)S(1)} %copy-done.1, bf16[4,64,2048]{2,1,0:T(8,128)(2,1)S(1)} %collective-permute-done.11.refs_0_.one_ref, bf16[4,64,2048]{2,1,0:T(8,128)(2,1)S(1)} %collective-permute-done.12.refs_1_.three_ref), custom_call_target="tpu_custom_call" | custom-call | flops 2097152 | bytes 8192 | tf_op jit(solution)/shard_map/pallas_call | solution.py:371
  86.8 3.7 %shard_map.108 = (bf16[256,512]{1,0:T(8,128)(2,1)S(1)}, bf16[256,512]{1,0:T(8,128)(2,1)S(1)}) custom-call(s32[4]{0:T(128)S(1)} %get-tuple-element.145.index_ref, bf16[8192,512]{1,0:T(8,128)(2,1)} %query_ref.11, bf16[512,8192]{1,0:T(8,128)(2,1)} %output_ref.11, bf16[2,2,256,512]{3,2,1,0:T(8,128)(2,1)S(1)} %collective-permute-done.5.refs_0_, ...), custom_call_target="tpu_custom_call" | custom-call | flops 1048576 | bytes 6144 | tf_op jit(solution)/shard_map/pallas_call | solution.py:235
  90.6 1.7 collective-permute-done.13.refs_0_
  92.3 1.3 shard_map.114
  93.5 2.8 %shard_map.115 = (bf16[256,512]{1,0:T(8,128)(2,1)S(1)}, bf16[256,512]{1,0:T(8,128)(2,1)S(1)}, bf16[256,512]{1,0:T(8,128)(2,1)S(1)}, bf16[256,512]{1,0:T(8,128)(2...) custom-call(bf16[256,512]{1,0:T(8,128)(2,1)S(1)} %get-tuple-element., ...), custom_call_target="tpu_custom_call" | custom-call | flops 393216 | bytes 10240 | tf_op jit(solution)/shard_map/pallas_call | solution.py:455
  96.3 1.3 shard_map.116
  97.6 1.7 collective-permute-start.16
  99.3 3.6 %shard_map.117 = (bf16[4,256,512]{2,1,0:T(8,128)(2,1)S(1)}, bf16[4,256,512]{2,1,0:T(8,128)(2,1)S(1)}) custom-call(s32[4]{0:T(128)S(1)} %get-tuple-element.145.index_ref, bf16[8192,512]{1,0:T(8,128)(2,1)} %query_ref.11, bf16[512,8192]{1,0:T(8,128)(2,1)} %output_ref.11, bf16[256,512]{1,0:T(8,128)(2,1)S(1)} %get-tuple-element.126.c_ref, ...), custom_call_target="tpu_custom_call" | custom-call | flops 1048576 | bytes 8192 | tf_op jit(solution)/shard_map/pallas_call | solution.py:263
  102.9 3.5 %shard_map.118 = (bf16[4,256,512]{2,1,0:T(8,128)(2,1)S(1)}, bf16[4,256,512]{2,1,0:T(8,128)(2,1)S(1)}, bf16[1,256,512]{2,1,0:T(8,128)(2,1)S(1)}, bf16[1,256,512]{...) custom-call(bf16[2048,512]{1,0:T(8,128)(2,1)S(1)} %copy-done, ...), custom_call_target="tpu_custom_call" | custom-call | flops 3145728 | bytes 10240 | tf_op jit(solution)/shard_map/pallas_call | solution.py:400
  106.4 2.4 %collective-permute-done.15.low_ref = bf16[2,256,512]{2,1,0:T(8,128)(2,1)S(1)} collective-permute-done((bf16[2,256,512]{2,1,0:T(8,128)(2,1)S(1)}, bf16[2,256,512]{2,1,0:T(8,128)(2,1)S(1)}, u32[]{:S(2)}, u32[]{:S(2)}) %collective-permute-start.15) | collective-permute-done | bytes 524320 | tf_op jit(solution)/shard_map/ppermute | solution.py:46
  108.8 0.4 shard_map.119
  109.2 0.3 collective-permute-start.18
  109.6 1.2 collective-permute-start.17
  110.8 5.3 %shard_map.120 = (bf16[8,256,512]{2,1,0:T(8,128)(2,1)S(1)}, bf16[8,256,512]{2,1,0:T(8,128)(2,1)S(1)}) custom-call(s32[8]{0:T(128)S(1)} %get-tuple-element.147.index_ref, bf16[8192,512]{1,0:T(8,128)(2,1)} %query_ref.11, bf16[512,8192]{1,0:T(8,128)(2,1)} %output_ref.11, bf16[256,512]{1,0:T(8,128)(2,1)S(1)} %get-tuple-element.126.c_ref, ...), custom_call_target="tpu_custom_call" | custom-call | flops 2097152 | bytes 16384 | tf_op jit(solution)/shard_map/pallas_call | solution.py:263
  116.1 18.4 %collective-permute-done.18.refs_4_.refs_2_.part_ref = bf16[8,256,512]{2,1,0:T(8,128)(2,1)S(1)} collective-permute-done((bf16[8,256,512]{2,1,0:T(8,128)(2,1)S(1)}, bf16[8,256,512]{2,1,0:T(8,128)(2,1)S(1)}, u32[]{:S(2)}, u32[]{:S(2)}) %collective-permute-start.18) | collective-permute-done | bytes 2097184 | tf_op jit(solution)/shard_map/ppermute | solution.py:46
  134.5 1.5 collective-permute-done.17.refs_3_.part_ref.refs_1_
  136.0 0.3 shard_map.121
  136.3 1.6 shard_map.122
  137.9 1.6 shard_map.125
  139.5 2.7 %collective-permute-start.23 = (bf16[8,256,512]{2,1,0:T(8,128)(2,1)}, bf16[8,256,512]{2,1,0:T(8,128)(2,1)}, u32[]{:S(2)}, u32[]{:S(2)}) collective-permute-start(bf16[8,256,512]{2,1,0:T(8,128)(2,1)} %shard_map.125), channel_id=1, source_target_pairs={{0,12},{1,13},{2,14},{3,15},{4,0},{5,1},{6,2},{7,3},{8,4},{9,5},{1... | collective-permute-start | bytes 6291464 | tf_op jit(solution)/shard_map/ppermute | solution.py:46
  142.3 0.6 iota_reduce_fusion
  142.9 0.3 collective-permute-start.19
  143.2 1.2 collective-permute-start.20
  144.4 4.0 %collective-permute-done.19.refs_3_ = bf16[1,256,512]{2,1,0:T(8,128)(2,1)S(1)} collective-permute-done((bf16[1,256,512]{2,1,0:T(8,128)(2,1)S(1)}, bf16[1,256,512]{2,1,0:T(8,128)(2,1)S(1)}, u32[]{:S(2)}, u32[]{:S(2)}) %collective-permute-start.19) | collective-permute-done | bytes 262176 | tf_op jit(solution)/shard_map/ppermute | solution.py:42
  148.4 4.4 %collective-permute-done.20.refs_4_ = bf16[1,256,512]{2,1,0:T(8,128)(2,1)S(1)} collective-permute-done((bf16[1,256,512]{2,1,0:T(8,128)(2,1)S(1)}, bf16[1,256,512]{2,1,0:T(8,128)(2,1)S(1)}, u32[]{:S(2)}, u32[]{:S(2)}) %collective-permute-start.20) | collective-permute-done | bytes 262176 | tf_op jit(solution)/shard_map/ppermute | solution.py:42
  152.8 3.5 %collective-permute-done.21.refs_5_ = bf16[1,256,512]{2,1,0:T(8,128)(2,1)S(1)} collective-permute-done((bf16[1,256,512]{2,1,0:T(8,128)(2,1)S(1)}, bf16[1,256,512]{2,1,0:T(8,128)(2,1)S(1)}, u32[]{:S(2)}, u32[]{:S(2)}) %collective-permute-start.21) | collective-permute-done | bytes 262176 | tf_op jit(solution)/shard_map/ppermute | solution.py:42
  156.6 0.6 gather_fusion.1
  157.2 3.6 %shard_map.124 = (bf16[2,256,512]{2,1,0:T(8,128)(2,1)S(1)}, bf16[2,256,512]{2,1,0:T(8,128)(2,1)S(1)}, bf16[2,256,512]{2,1,0:T(8,128)(2,1)S(1)}, bf16[2,256,512]{2,1,0:T(8,128)(2,1)S(1)}) custom-call(s32[4]{0:T(128)S(1)} %get-tuple-element.146.index_ref, bf16[8192,512]{1,0:T(8,128)(2,1)} %query_ref.11, bf16[512,8192]{1,0:T(8,128)(2,1)} %output_ref.11, ...), custom_call_target="tpu_custom_call" | custom-call | flops 1048576 | bytes 8192 | tf_op jit(solution)/shard_map/pallas_call | solution.py:263
  160.8 9.4 %collective-permute-done.22.refs_3_.refs_1_ = bf16[8,256,512]{2,1,0:T(8,128)(2,1)S(1)} collective-permute-done((bf16[8,256,512]{2,1,0:T(8,128)(2,1)}, bf16[8,256,512]{2,1,0:T(8,128)(2,1)S(1)}, u32[]{:S(2)}, u32[]{:S(2)}) %collective-permute-start.22) | collective-permute-done | bytes 2097184 | tf_op jit(solution)/shard_map/ppermute | solution.py:46
  170.1 1.0 collective-permute-done.23.refs_4_.refs_2_
  171.1 2.2 %shard_map.126 = (bf16[2,256,512]{2,1,0:T(8,128)(2,1)S(1)}, bf16[2,256,512]{2,1,0:T(8,128)(2,1)S(1)}, bf16[2,256,512]{2,1,0:T(8,128)(2,1)S(1)}) custom-call(bf16[2,256,512]{2,1,0:T(8,128)(2,1)S(1)} %get-tuple-element.130.refs_0_, bf16[2,256,512]{2,1,0:T(8,128)(2,1)S(1)} %get-tuple-element.131.refs_1_, bf16[2,256,512]{2,1,0:T(8,128)(2,1)S(1)} %get-tuple-element.132.refs_2_, ...), custom_call_target="tpu_custom_call" | custom-call | flops 8192 | bytes 8192 | tf_op jit(solution)/shard_map/pallas_call | solution.py:330
  173.3 0.4 collective-permute-start.24
  173.7 1.2 collective-permute-start.25
  175.1 26.3 %all_to_all.10 = bf16[128,8,256]{2,1,0:T(8,128)(2,1)S(1)} all-to-all(bf16[128,8,256]{2,1,0:T(8,128)(2,1)S(1)} %bitcast.33), channel_id=1, replica_groups=mesh['seq'=8,'enc'=16] {'seq','enc'}, dimensions={0} | all-to-all | bytes 1048576 | tf_op jit(solution)/shard_map/all_to_all | solution.py:535
  201.3 2.7 %shard_map.127 = (bf16[256,512]{1,0:T(8,128)(2,1)}, bf16[256,512]{1,0:T(8,128)(2,1)}) custom-call(bf16[2,256,512]{2,1,0:T(8,128)(2,1)S(1)} %get-tuple-element.127.refs_0_, bf16[8,256,512]{2,1,0:T(8,128)(2,1)S(1)} %collective-permute-done.22.refs_3_.refs_1_, bf16[8,256,512]{2,1,0:T(8,128)(2,1)} %collective-permute-done.23.refs_4_.refs_2_, ...), custom_call_target="tpu_custom_call" | custom-call | flops 1024 | bytes 2560 | tf_op jit(solution)/shard_map/pallas_call | solution.py:351
  204.0 0.8 copy.25
  (52 shorter events, 1.8 us)
Async XLA Ops:
  1.7 16.4 %collective-permute-start.2 = (bf16[2,256,512]{2,1,0:T(8,128)(2,1)S(1)}, bf16[2,256,512]{2,1,0:T(8,128)(2,1)S(1)}, u32[]{:S(2)}, u32[]{:S(2)}) collective-permute-start(bf16[2,256,512]{2,1,0:T(8,128)(2,1)S(1)} %shard_map.103.refs_0_), channel_id=1, source_target_pairs={{0,3},{1,0},{2,1},{3,2},{4,7},{5,4},{6,5},{7,6},{8,11},{9,8},{10,9... | collective-permute-start | bytes 1572872 | tf_op jit(solution)/shard_map/ppermute | solution.py:42
  6.3 11.7 %collective-permute-start.1 = (bf16[2,256,512]{2,1,0:T(8,128)(2,1)S(1)}, bf16[2,256,512]{2,1,0:T(8,128)(2,1)S(1)}, u32[]{:S(2)}, u32[]{:S(2)}) collective-permute-start(bf16[2,256,512]{2,1,0:T(8,128)(2,1)S(1)} %shard_map.103.refs_0_), channel_id=1, source_target_pairs={{0,2},{1,3},{2,0},{3,1},{4,6},{5,7},{6,4},{7,5},{8,10},{9,11},{10,... | collective-permute-start | bytes 1572872 | tf_op jit(solution)/shard_map/ppermute | solution.py:42
  6.3 15.2 %collective-permute-start = (bf16[2,256,512]{2,1,0:T(8,128)(2,1)S(1)}, bf16[2,256,512]{2,1,0:T(8,128)(2,1)S(1)}, u32[]{:S(2)}, u32[]{:S(2)}) collective-permute-start(bf16[2,256,512]{2,1,0:T(8,128)(2,1)S(1)} %shard_map.103.refs_0_), channel_id=1, source_target_pairs={{0,1},{1,2},{2,3},{3,0},{4,5},{5,6},{6,7},{7,4},{8,9},{9,10},{10,1... | collective-permute-start | bytes 1572872 | tf_op jit(solution)/shard_map/ppermute | solution.py:42
  7.0 26.3 %all-to-all-start = ((bf16[128,8,256]{2,1,0:T(8,128)(2,1)}), bf16[128,8,256]{2,1,0:T(8,128)(2,1)S(1)}, u32[]{:S(2)}, u32[]{:S(2)}) async-start(bf16[128,8,256]{2,1,0:T(8,128)(2,1)} %bitcast.35), calls=%async_computation | async-start | bytes 1048576 | tf_op jit(solution)/shard_map/all_to_all | solution.py:484
  17.0 17.8 %copy-start.4 = (s32[4,2]{0,1:T(2,128)S(1)}, s32[4,2]{0,1:T(2,128)}, u32[]{:S(2)}) copy-start(s32[4,2]{0,1:T(2,128)} %param.14) | copy-start | bytes 100
  21.6 1.4 copy-start.2
  33.4 29.7 %collective-permute-start.4 = (bf16[4,2,256,512]{3,2,1,0:T(8,128)(2,1)}, bf16[4,2,256,512]{3,2,1,0:T(8,128)(2,1)S(1)}, u32[]{:S(2)}, u32[]{:S(2)}) collective-permute-start(bf16[4,2,256,512]{3,2,1,0:T(8,128)(2,1)} %copy-done.2), channel_id=1, source_target_pairs={{0,12},{1,13},{2,14},{3,15},{4,0},{5,1},{6,2},{7,3},{8,4},{9,5},{1... | collective-permute-start | bytes 6291464 | tf_op jit(solution)/shard_map/ppermute | solution.py:46
  33.4 30.9 %collective-permute-start.3 = (bf16[4,2,256,512]{3,2,1,0:T(8,128)(2,1)}, bf16[4,2,256,512]{3,2,1,0:T(8,128)(2,1)}, u32[]{:S(2)}, u32[]{:S(2)}) collective-permute-start(bf16[4,2,256,512]{3,2,1,0:T(8,128)(2,1)} %copy-done.2), channel_id=1, source_target_pairs={{0,4},{1,5},{2,6},{3,7},{4,8},{5,9},{6,10},{7,11},{8,12},{9,13},{1... | collective-permute-start | bytes 6291464 | tf_op jit(solution)/shard_map/ppermute | solution.py:46
  35.8 8.6 %collective-permute-start.8 = (bf16[2,32,2048]{2,1,0:T(8,128)(2,1)S(1)}, bf16[2,32,2048]{2,1,0:T(8,128)(2,1)S(1)}, u32[]{:S(2)}, u32[]{:S(2)}) collective-permute-start(bf16[2,32,2048]{2,1,0:T(8,128)(2,1)S(1)} %bitcast.27), channel_id=1, source_target_pairs={{0,3},{1,0},{2,1},{3,2},{4,7},{5,4},{6,5},{7,6},{8,11},{9,8},{10,9... | collective-permute-start | bytes 786440 | tf_op jit(solution)/shard_map/ppermute | solution.py:42
  36.0 9.6 %collective-permute-start.7 = (bf16[2,32,2048]{2,1,0:T(8,128)(2,1)S(1)}, bf16[2,32,2048]{2,1,0:T(8,128)(2,1)S(1)}, u32[]{:S(2)}, u32[]{:S(2)}) collective-permute-start(bf16[2,32,2048]{2,1,0:T(8,128)(2,1)S(1)} %bitcast.28), channel_id=1, source_target_pairs={{0,1},{1,2},{2,3},{3,0},{4,5},{5,6},{6,7},{7,4},{8,9},{9,10},{10,1... | collective-permute-start | bytes 786440 | tf_op jit(solution)/shard_map/ppermute | solution.py:42
  45.7 7.0 %collective-permute-start.9 = (bf16[1,32,2048]{2,1,0:T(8,128)(2,1)S(1)}, bf16[1,32,2048]{2,1,0:T(8,128)(2,1)S(1)}, u32[]{:S(2)}, u32[]{:S(2)}) collective-permute-start(bf16[1,32,2048]{2,1,0:T(8,128)(2,1)S(1)} %get-tuple-element.83), channel_id=1, source_target_pairs={{0,1},{1,2},{2,3},{3,0},{4,5},{5,6},{6,7},{7,4},{8,9},{9,10},{10,1... | collective-permute-start | bytes 393224 | tf_op jit(solution)/shard_map/ppermute | solution.py:42
  45.9 6.8 %collective-permute-start.10 = (bf16[1,32,2048]{2,1,0:T(8,128)(2,1)S(1)}, bf16[1,32,2048]{2,1,0:T(8,128)(2,1)S(1)}, u32[]{:S(2)}, u32[]{:S(2)}) collective-permute-start(bf16[1,32,2048]{2,1,0:T(8,128)(2,1)S(1)} %get-tuple-element.84), channel_id=1, source_target_pairs={{0,3},{1,0},{2,1},{3,2},{4,7},{5,4},{6,5},{7,6},{8,11},{9,8},{10,9... | collective-permute-start | bytes 393224 | tf_op jit(solution)/shard_map/ppermute | solution.py:42
  48.5 5.9 %copy-start.3 = (bf16[4,2,256,512]{3,2,1,0:T(8,128)(2,1)S(1)}, bf16[4,2,256,512]{3,2,1,0:T(8,128)(2,1)}, u32[]{:S(2)}) copy-start(bf16[4,2,256,512]{3,2,1,0:T(8,128)(2,1)} %copy-done.2) | copy-start | bytes 6291460
  52.7 21.4 %collective-permute-start.12 = (bf16[4,64,2048]{2,1,0:T(8,128)(2,1)S(1)}, bf16[4,64,2048]{2,1,0:T(8,128)(2,1)S(1)}, u32[]{:S(2)}, u32[]{:S(2)}) collective-permute-start(bf16[4,64,2048]{2,1,0:T(8,128)(2,1)S(1)} %bitcast.24), channel_id=1, source_target_pairs={{0,12},{1,13},{2,14},{3,15},{4,0},{5,1},{6,2},{7,3},{8,4},{9,5},{1... | collective-permute-start | bytes 3145736 | tf_op jit(solution)/shard_map/ppermute | solution.py:46
  54.2 21.3 %collective-permute-start.11 = (bf16[4,64,2048]{2,1,0:T(8,128)(2,1)S(1)}, bf16[4,64,2048]{2,1,0:T(8,128)(2,1)S(1)}, u32[]{:S(2)}, u32[]{:S(2)}) collective-permute-start(bf16[4,64,2048]{2,1,0:T(8,128)(2,1)S(1)} %bitcast.25), channel_id=1, source_target_pairs={{0,4},{1,5},{2,6},{3,7},{4,8},{5,9},{6,10},{7,11},{8,12},{9,13},{1... | collective-permute-start | bytes 3145736 | tf_op jit(solution)/shard_map/ppermute | solution.py:46
  57.9 9.8 %copy-start = (bf16[2048,512]{1,0:T(8,128)(2,1)S(1)}, bf16[2048,512]{1,0:T(8,128)(2,1)}, u32[]{:S(2)}) copy-start(bf16[2048,512]{1,0:T(8,128)(2,1)} %key_ref.9) | copy-start | bytes 6291460
  57.9 9.7 %copy-start.1 = (bf16[2048,512]{1,0:T(8,128)(2,1)S(1)}, bf16[2048,512]{1,0:T(8,128)(2,1)}, u32[]{:S(2)}) copy-start(bf16[2048,512]{1,0:T(8,128)(2,1)} %value_ref.9) | copy-start | bytes 6291460
  66.0 20.8 %collective-permute-start.6 = (bf16[2,2,256,512]{3,2,1,0:T(8,128)(2,1)S(1)}, bf16[2,2,256,512]{3,2,1,0:T(8,128)(2,1)S(1)}, u32[]{:S(2)}, u32[]{:S(2)}) collective-permute-start(bf16[2,2,256,512]{3,2,1,0:T(8,128)(2,1)S(1)} %get-tuple-element.78), channel_id=1, source_target_pairs={{0,12},{1,13},{2,14},{3,15},{4,0},{5,1},{6,2},{7,3},{8,4},{9,5},{1... | collective-permute-start | bytes 3145736 | tf_op jit(solution)/shard_map/ppermute | solution.py:46
  66.1 20.7 %collective-permute-start.5 = (bf16[2,2,256,512]{3,2,1,0:T(8,128)(2,1)S(1)}, bf16[2,2,256,512]{3,2,1,0:T(8,128)(2,1)S(1)}, u32[]{:S(2)}, u32[]{:S(2)}) collective-permute-start(bf16[2,2,256,512]{3,2,1,0:T(8,128)(2,1)S(1)} %get-tuple-element.76), channel_id=1, source_target_pairs={{0,4},{1,5},{2,6},{3,7},{4,8},{5,9},{6,10},{7,11},{8,12},{9,13},{1... | collective-permute-start | bytes 3145736 | tf_op jit(solution)/shard_map/ppermute | solution.py:46
  81.7 10.5 %collective-permute-start.13 = (bf16[2,64,2048]{2,1,0:T(8,128)(2,1)S(1)}, bf16[2,64,2048]{2,1,0:T(8,128)(2,1)S(1)}, u32[]{:S(2)}, u32[]{:S(2)}) collective-permute-start(bf16[2,64,2048]{2,1,0:T(8,128)(2,1)S(1)} %get-tuple-element.89), channel_id=1, source_target_pairs={{0,4},{1,5},{2,6},{3,7},{4,8},{5,9},{6,10},{7,11},{8,12},{9,13},{1... | collective-permute-start | bytes 1572872 | tf_op jit(solution)/shard_map/ppermute | solution.py:46
  82.1 10.2 %collective-permute-start.14 = (bf16[2,64,2048]{2,1,0:T(8,128)(2,1)S(1)}, bf16[2,64,2048]{2,1,0:T(8,128)(2,1)S(1)}, u32[]{:S(2)}, u32[]{:S(2)}) collective-permute-start(bf16[2,64,2048]{2,1,0:T(8,128)(2,1)S(1)} %get-tuple-element.93), channel_id=1, source_target_pairs={{0,12},{1,13},{2,14},{3,15},{4,0},{5,1},{6,2},{7,3},{8,4},{9,5},{1... | collective-permute-start | bytes 1572872 | tf_op jit(solution)/shard_map/ppermute | solution.py:46
  97.6 8.8 %collective-permute-start.16 = (bf16[2,256,512]{2,1,0:T(8,128)(2,1)S(1)}, bf16[2,256,512]{2,1,0:T(8,128)(2,1)S(1)}, u32[]{:S(2)}, u32[]{:S(2)}) collective-permute-start(bf16[2,256,512]{2,1,0:T(8,128)(2,1)S(1)} %get-tuple-element.113), channel_id=1, source_target_pairs={{0,12},{1,13},{2,14},{3,15},{4,0},{5,1},{6,2},{7,3},{8,4},{9,5},{1... | collective-permute-start | bytes 1572872 | tf_op jit(solution)/shard_map/ppermute | solution.py:46
  99.3 9.5 %collective-permute-start.15 = (bf16[2,256,512]{2,1,0:T(8,128)(2,1)S(1)}, bf16[2,256,512]{2,1,0:T(8,128)(2,1)S(1)}, u32[]{:S(2)}, u32[]{:S(2)}) collective-permute-start(bf16[2,256,512]{2,1,0:T(8,128)(2,1)S(1)} %get-tuple-element.100), channel_id=1, source_target_pairs={{0,4},{1,5},{2,6},{3,7},{4,8},{5,9},{6,10},{7,11},{8,12},{9,13},{1... | collective-permute-start | bytes 1572872 | tf_op jit(solution)/shard_map/ppermute | solution.py:46
  109.2 25.2 %collective-permute-start.18 = (bf16[8,256,512]{2,1,0:T(8,128)(2,1)S(1)}, bf16[8,256,512]{2,1,0:T(8,128)(2,1)S(1)}, u32[]{:S(2)}, u32[]{:S(2)}) collective-permute-start(bf16[8,256,512]{2,1,0:T(8,128)(2,1)S(1)} %get-tuple-element.120), channel_id=1, source_target_pairs={{0,12},{1,13},{2,14},{3,15},{4,0},{5,1},{6,2},{7,3},{8,4},{9,5},{1... | collective-permute-start | bytes 6291464 | tf_op jit(solution)/shard_map/ppermute | solution.py:46
  109.6 26.4 %collective-permute-start.17 = (bf16[8,256,512]{2,1,0:T(8,128)(2,1)S(1)}, bf16[8,256,512]{2,1,0:T(8,128)(2,1)S(1)}, u32[]{:S(2)}, u32[]{:S(2)}) collective-permute-start(bf16[8,256,512]{2,1,0:T(8,128)(2,1)S(1)} %get-tuple-element.114), channel_id=1, source_target_pairs={{0,4},{1,5},{2,6},{3,7},{4,8},{5,9},{6,10},{7,11},{8,12},{9,13},{1... | collective-permute-start | bytes 6291464 | tf_op jit(solution)/shard_map/ppermute | solution.py:46
  137.9 32.2 %collective-permute-start.22 = (bf16[8,256,512]{2,1,0:T(8,128)(2,1)}, bf16[8,256,512]{2,1,0:T(8,128)(2,1)S(1)}, u32[]{:S(2)}, u32[]{:S(2)}) collective-permute-start(bf16[8,256,512]{2,1,0:T(8,128)(2,1)} %shard_map.122), channel_id=1, source_target_pairs={{0,4},{1,5},{2,6},{3,7},{4,8},{5,9},{6,10},{7,11},{8,12},{9,13},{1... | collective-permute-start | bytes 6291464 | tf_op jit(solution)/shard_map/ppermute | solution.py:46
  139.5 31.6 %collective-permute-start.23 = (bf16[8,256,512]{2,1,0:T(8,128)(2,1)}, bf16[8,256,512]{2,1,0:T(8,128)(2,1)}, u32[]{:S(2)}, u32[]{:S(2)}) collective-permute-start(bf16[8,256,512]{2,1,0:T(8,128)(2,1)} %shard_map.125), channel_id=1, source_target_pairs={{0,12},{1,13},{2,14},{3,15},{4,0},{5,1},{6,2},{7,3},{8,4},{9,5},{1... | collective-permute-start | bytes 6291464 | tf_op jit(solution)/shard_map/ppermute | solution.py:46
  142.9 5.5 %collective-permute-start.19 = (bf16[1,256,512]{2,1,0:T(8,128)(2,1)S(1)}, bf16[1,256,512]{2,1,0:T(8,128)(2,1)S(1)}, u32[]{:S(2)}, u32[]{:S(2)}) collective-permute-start(bf16[1,256,512]{2,1,0:T(8,128)(2,1)S(1)} %get-tuple-element.121), channel_id=1, source_target_pairs={{0,3},{1,0},{2,1},{3,2},{4,7},{5,4},{6,5},{7,6},{8,11},{9,8},{10,9... | collective-permute-start | bytes 786440 | tf_op jit(solution)/shard_map/ppermute | solution.py:42
  143.2 9.6 %collective-permute-start.20 = (bf16[1,256,512]{2,1,0:T(8,128)(2,1)S(1)}, bf16[1,256,512]{2,1,0:T(8,128)(2,1)S(1)}, u32[]{:S(2)}, u32[]{:S(2)}) collective-permute-start(bf16[1,256,512]{2,1,0:T(8,128)(2,1)S(1)} %get-tuple-element.122), channel_id=1, source_target_pairs={{0,2},{1,3},{2,0},{3,1},{4,6},{5,7},{6,4},{7,5},{8,10},{9,11},{10,... | collective-permute-start | bytes 786440 | tf_op jit(solution)/shard_map/ppermute | solution.py:42
  144.4 11.9 %collective-permute-start.21 = (bf16[1,256,512]{2,1,0:T(8,128)(2,1)S(1)}, bf16[1,256,512]{2,1,0:T(8,128)(2,1)S(1)}, u32[]{:S(2)}, u32[]{:S(2)}) collective-permute-start(bf16[1,256,512]{2,1,0:T(8,128)(2,1)S(1)} %get-tuple-element.123), channel_id=1, source_target_pairs={{0,1},{1,2},{2,3},{3,0},{4,5},{5,6},{6,7},{7,4},{8,9},{9,10},{10,1... | collective-permute-start | bytes 786440 | tf_op jit(solution)/shard_map/ppermute | solution.py:42
  173.3 28.0 %collective-permute-start.24 = (bf16[2,256,512]{2,1,0:T(8,128)(2,1)S(1)}, bf16[2,256,512]{2,1,0:T(8,128)(2,1)S(1)}, u32[]{:S(2)}, u32[]{:S(2)}) collective-permute-start(bf16[2,256,512]{2,1,0:T(8,128)(2,1)S(1)} %get-tuple-element.134), channel_id=1, source_target_pairs={{0,3},{1,0},{2,1},{3,2},{4,7},{5,4},{6,5},{7,6},{8,11},{9,8},{10,9... | collective-permute-start | bytes 1572872 | tf_op jit(solution)/shard_map/ppermute | solution.py:42
  173.7 27.6 %collective-permute-start.25 = (bf16[2,256,512]{2,1,0:T(8,128)(2,1)S(1)}, bf16[2,256,512]{2,1,0:T(8,128)(2,1)S(1)}, u32[]{:S(2)}, u32[]{:S(2)}) collective-permute-start(bf16[2,256,512]{2,1,0:T(8,128)(2,1)S(1)} %get-tuple-element.135), channel_id=1, source_target_pairs={{0,2},{1,3},{2,0},{3,1},{4,6},{5,7},{6,4},{7,5},{8,10},{9,11},{10,... | collective-permute-start | bytes 1572872 | tf_op jit(solution)/shard_map/ppermute | solution.py:42
  174.9 26.5 %collective-permute-start.26 = (bf16[2,256,512]{2,1,0:T(8,128)(2,1)S(1)}, bf16[2,256,512]{2,1,0:T(8,128)(2,1)S(1)}, u32[]{:S(2)}, u32[]{:S(2)}) collective-permute-start(bf16[2,256,512]{2,1,0:T(8,128)(2,1)S(1)} %get-tuple-element.136), channel_id=1, source_target_pairs={{0,1},{1,2},{2,3},{3,0},{4,5},{5,6},{6,7},{7,4},{8,9},{9,10},{10,1... | collective-permute-start | bytes 1572872 | tf_op jit(solution)/shard_map/ppermute | solution.py:42
